TPU v7x, 128 devices: a whole 4x4x4 slice. The times are simulated.
128 devices in a mesh: wide: 16 (over x_lo, y, core), narrow: 8 (over x_hi, z).
Axes of the slice: x: 4 (x_hi: 2, x_lo: 2; x = x_hi * 2 + x_lo), y: 4, z: 4, core: 2. Of those that a mesh axis runs over, the one named last changes fastest.
Arguments:
- tokens: bfloat16 [65536, 768], P(('wide', 'narrow')), may hold values from -6 to 6
- seq_lengths: int32 [128, 4], P(('wide', 'narrow')), may hold values from 0 to 512, as said below
- ln1_gain: bfloat16 [768], P(('wide', 'narrow')), may hold values from 0.25 to 1.75
- ln1_bias: bfloat16 [768], P(('wide', 'narrow')), may hold values from -3 to 3
- qkv_weight: bfloat16 [768, 2304], P(('wide', 'narrow')), may hold values from -0.21875 to 0.21875
- out_weight: bfloat16 [768, 768], P(('wide', 'narrow')), may hold values from -0.4375 to 0.4375
- ln2_gain: bfloat16 [768], P(('wide', 'narrow')), may hold values from 0.25 to 1.75
- ln2_bias: bfloat16 [768], P(('wide', 'narrow')), may hold values from -3 to 3
- up_weight: bfloat16 [768, 3072], P(None, ('wide', 'narrow')), may hold values from -0.21875 to 0.21875
- down_weight: bfloat16 [3072, 768], P(('wide', 'narrow')), may hold values from -0.109375 to 0.109375
- cotangent: bfloat16 [65536, 768], P(('wide', 'narrow')), may hold values from -6 to 6
Outputs:
- output: bfloat16 [65536, 768], P(('wide', 'narrow'))
- tokens_grad: bfloat16 [65536, 768], P(('wide', 'narrow'))
- ln1_gain_grad: float32 [768], P(('wide', 'narrow'))
- ln1_bias_grad: float32 [768], P(('wide', 'narrow'))
- qkv_grad: float32 [768, 2304], P(('wide', 'narrow'))
- out_grad: float32 [768, 768], P(('wide', 'narrow'))
- ln2_gain_grad: float32 [768], P(('wide', 'narrow'))
- ln2_bias_grad: float32 [768], P(('wide', 'narrow'))
- up_grad: float32 [768, 3072], P(None, ('wide', 'narrow'))
- down_grad: float32 [3072, 768], P(('wide', 'narrow'))
Inputs may be any that keep to these rules, and one draw needn't show every extreme that they name: `seq_lengths`: each device's row is either 512, 0, 0, 0 or two to four entries 128 followed by zeros; both kinds occur in every draw.
All inputs are finite; a program needn't handle non-finite values.
Results may differ from a plain program's by a relative error of at most 0.018.
Values may be sent and summed in bfloat16 or wider, within the bound.
No kernel may reach another device: no remote copies, remote signals or barrier semaphores. Data moves between devices by JAX's collectives and lax.ppermute only.
A program may use at most 128 MiB of HBM per device.

v0:
```python
import jax
import jax.numpy as jnp
from jax import lax
from jax.sharding import PartitionSpec as P

HEAD_DIM = 64


EPS = 1e-05
SHARP = 4.0
NEG = -1e30
HIGH = lax.Precision.HIGHEST


def layout_masks(row_lengths, row_count):
    positions = jnp.arange(row_count, dtype=jnp.int32)
    group_ends = jnp.cumsum(row_lengths)
    segment = jnp.sum((positions[:, None] >= group_ends[None, :]).astype(jnp.int32), axis=1)
    first_row = jnp.concatenate([jnp.ones((1,), dtype=bool), segment[1:] != segment[:-1]])
    same_group = segment[:, None] == segment[None, :]
    allowed = same_group & (positions[None, :] <= positions[:, None])
    chosen = (
        same_group & (positions[None, :] < positions[:, None]) & jnp.logical_not(first_row)[None, :]
    )
    live_rows = (positions < group_ends[-1]).astype(jnp.float32)
    strict_lower = (positions[:, None] > positions[None, :]).astype(jnp.float32)
    return (allowed, chosen, live_rows, strict_lower)


def norm_forward(values, gain_row, bias_row):
    row_mean = jnp.mean(values, axis=-1, keepdims=True)
    centered = values - row_mean
    inverse = lax.rsqrt(jnp.mean(centered * centered, axis=-1, keepdims=True) + EPS)
    normed = centered * inverse
    return (normed * gain_row + bias_row, normed, inverse)


def norm_backward(gradient, normed, inverse, gain_row):
    gain_grad = jnp.sum(gradient * normed, axis=0)
    bias_grad = jnp.sum(gradient, axis=0)
    scaled = gradient * gain_row
    backward = inverse * (
        scaled
        - jnp.mean(scaled, axis=-1, keepdims=True)
        - normed * jnp.mean(scaled * normed, axis=-1, keepdims=True)
    )
    return (backward, gain_grad, bias_grad)


def matmul_tn(left_side, right_side):
    return lax.dot_general(
        left_side, right_side, (((0,), (0,)), ((), ())), preferred_element_type=jnp.float32
    )


def matmul_nt(left_side, right_side):
    return lax.dot_general(
        left_side, right_side, (((1,), (1,)), ((), ())), preferred_element_type=jnp.float32
    )


def gelu_tanh(values):
    return jax.nn.gelu(values, approximate=True)


def on_device(
    tokens,
    seq_lengths,
    ln1_gain,
    ln1_bias,
    qkv_weight,
    out_weight,
    ln2_gain,
    ln2_bias,
    up_weight,
    down_weight,
    cotangent,
):
    row_count = tokens.shape[0]
    model_width = tokens.shape[1]
    head_count = model_width // HEAD_DIM
    score_scale = HEAD_DIM ** (-0.5)
    allowed, chosen, live_rows, strict_lower = layout_masks(seq_lengths[0], row_count)
    gain_one, bias_one, qkv_full, out_full = (
        lax.all_gather(ln1_gain, ("wide", "narrow"), axis=0, tiled=True),
        lax.all_gather(ln1_bias, ("wide", "narrow"), axis=0, tiled=True),
        lax.all_gather(qkv_weight, ("wide", "narrow"), axis=0, tiled=True),
        lax.all_gather(out_weight, ("wide", "narrow"), axis=0, tiled=True),
    )
    gain_two, bias_two, up_full, down_full = (
        lax.all_gather(ln2_gain, ("wide", "narrow"), axis=0, tiled=True),
        lax.all_gather(ln2_bias, ("wide", "narrow"), axis=0, tiled=True),
        lax.all_gather(up_weight, ("wide", "narrow"), axis=1, tiled=True),
        lax.all_gather(down_weight, ("wide", "narrow"), axis=0, tiled=True),
    )
    inputs = tokens.astype(jnp.float32)
    normed_one, unit_one, inverse_one = norm_forward(
        inputs, gain_one.astype(jnp.float32), bias_one.astype(jnp.float32)
    )
    h_one = normed_one.astype(jnp.bfloat16)
    qkv = jnp.dot(h_one, qkv_full, preferred_element_type=jnp.float32).astype(jnp.bfloat16)
    split_heads = qkv.reshape(row_count, 3, head_count, HEAD_DIM).transpose(1, 2, 0, 3)
    queries = split_heads[0]
    keys_all = split_heads[1]
    values = split_heads[2]
    first_logits = matmul_nt(queries[0], keys_all[0]) * score_scale
    selected = jnp.where(chosen, jax.nn.softplus(SHARP * first_logits) / SHARP, 0.0)
    penalty = jnp.dot(strict_lower, selected, precision=HIGH)

    def head_scores(query_head, key_head):
        logits = matmul_nt(query_head, key_head) * score_scale
        return (logits, jnp.where(allowed, logits - penalty, NEG))

    def head_forward(head_parts):
        query_head, key_head, value_head = head_parts
        _, shifted = head_scores(query_head, key_head)
        row_top = jnp.max(shifted, axis=-1, keepdims=True)
        exponent = jnp.exp(shifted - row_top)
        row_total = jnp.sum(exponent, axis=-1, keepdims=True)
        weights_low = (exponent / row_total).astype(jnp.bfloat16)
        mixed_head = jnp.dot(weights_low, value_head, preferred_element_type=jnp.float32).astype(
            jnp.bfloat16
        )
        return (mixed_head, (row_top + jnp.log(row_total))[:, 0])

    mixed_heads, log_totals = lax.map(head_forward, (queries, keys_all, values))
    mixed = mixed_heads.transpose(1, 0, 2).reshape(row_count, model_width)
    branch = jnp.dot(mixed, out_full, preferred_element_type=jnp.float32)
    middle = inputs + branch
    normed_two, unit_two, inverse_two = norm_forward(
        middle, gain_two.astype(jnp.float32), bias_two.astype(jnp.float32)
    )
    h_two = normed_two.astype(jnp.bfloat16)
    up_value = jnp.dot(h_two, up_full, preferred_element_type=jnp.float32)
    activated, gelu_pull = jax.vjp(gelu_tanh, up_value)
    act_low = activated.astype(jnp.bfloat16)
    result = middle + jnp.dot(act_low, down_full, preferred_element_type=jnp.float32)
    output = result.astype(jnp.bfloat16)
    gain_two_back, bias_two_unused, up_back, down_back = (
        lax.all_gather(ln2_gain, ("wide", "narrow"), axis=0, tiled=True),
        lax.all_gather(ln2_bias, ("wide", "narrow"), axis=0, tiled=True),
        lax.all_gather(up_weight, ("wide", "narrow"), axis=1, tiled=True),
        lax.all_gather(down_weight, ("wide", "narrow"), axis=0, tiled=True),
    )
    grad_out = cotangent.astype(jnp.float32) * live_rows[:, None]
    grad_low = grad_out.astype(jnp.bfloat16)
    down_weight_grad = matmul_tn(act_low, grad_low)
    act_grad = matmul_nt(grad_low, down_back)
    up_grad_low = gelu_pull(act_grad)[0].astype(jnp.bfloat16)
    up_weight_grad = matmul_tn(h_two, up_grad_low)
    h_two_grad = matmul_nt(up_grad_low, up_back)
    norm_two_back, gain_two_grad, bias_two_grad = norm_backward(
        h_two_grad, unit_two, inverse_two, gain_two_back.astype(jnp.float32)
    )
    middle_grad = grad_out + norm_two_back
    gain_one_back, bias_one_unused, qkv_back, out_back = (
        lax.all_gather(ln1_gain, ("wide", "narrow"), axis=0, tiled=True),
        lax.all_gather(ln1_bias, ("wide", "narrow"), axis=0, tiled=True),
        lax.all_gather(qkv_weight, ("wide", "narrow"), axis=0, tiled=True),
        lax.all_gather(out_weight, ("wide", "narrow"), axis=0, tiled=True),
    )
    out_grad_low = middle_grad.astype(jnp.bfloat16)
    out_weight_grad = matmul_tn(mixed, out_grad_low)
    mixed_grad = matmul_nt(out_grad_low, out_back).astype(jnp.bfloat16)
    mixed_grad_heads = mixed_grad.reshape(row_count, head_count, HEAD_DIM).transpose(1, 0, 2)

    def head_grads(query_head, key_head, value_head, upstream, log_total):
        _, shifted = head_scores(query_head, key_head)
        soft_weights = jnp.exp(shifted - log_total[:, None])
        soft_low = soft_weights.astype(jnp.bfloat16)
        value_grad = matmul_tn(soft_low, upstream)
        weight_grad = matmul_nt(upstream, value_head)
        score_grad = soft_weights * (
            weight_grad - jnp.sum(weight_grad * soft_weights, axis=-1, keepdims=True)
        )
        return (score_grad, value_grad)

    def query_key_grads(score_low, query_head, key_head):
        query_grad = jnp.dot(score_low, key_head, preferred_element_type=jnp.float32) * score_scale
        key_grad = matmul_tn(score_low, query_head) * score_scale
        return (query_grad, key_grad)

    def other_head(carried, head_parts):
        query_head, key_head, value_head, upstream, log_total = head_parts
        score_grad, value_grad = head_grads(query_head, key_head, value_head, upstream, log_total)
        query_grad, key_grad = query_key_grads(
            score_grad.astype(jnp.bfloat16), query_head, key_head
        )
        return (carried - score_grad, (query_grad, key_grad, value_grad))

    penalty_grad, rest_grads = lax.scan(
        other_head,
        jnp.zeros((row_count, row_count), jnp.float32),
        (queries[1:], keys_all[1:], values[1:], mixed_grad_heads[1:], log_totals[1:]),
    )
    first_score_grad, first_value_grad = head_grads(
        queries[0], keys_all[0], values[0], mixed_grad_heads[0], log_totals[0]
    )
    penalty_grad = penalty_grad - first_score_grad
    selected_grad = lax.dot_general(
        strict_lower, penalty_grad, (((0,), (0,)), ((), ())), precision=HIGH
    )
    first_total = first_score_grad + jnp.where(
        chosen, jax.nn.sigmoid(SHARP * first_logits) * selected_grad, 0.0
    )
    first_query_grad, first_key_grad = query_key_grads(
        first_total.astype(jnp.bfloat16), queries[0], keys_all[0]
    )
    query_grads = jnp.concatenate([first_query_grad[None], rest_grads[0]], axis=0)
    key_grads = jnp.concatenate([first_key_grad[None], rest_grads[1]], axis=0)
    value_grads = jnp.concatenate([first_value_grad[None], rest_grads[2]], axis=0)
    qkv_grad_low = (
        jnp.stack([query_grads, key_grads, value_grads])
        .transpose(2, 0, 1, 3)
        .reshape(row_count, 3 * model_width)
        .astype(jnp.bfloat16)
    )
    qkv_weight_grad = matmul_tn(h_one, qkv_grad_low)
    h_one_grad = matmul_nt(qkv_grad_low, qkv_back)
    norm_one_back, gain_one_grad, bias_one_grad = norm_backward(
        h_one_grad, unit_one, inverse_one, gain_one_back.astype(jnp.float32)
    )
    input_grad = (middle_grad + norm_one_back).astype(jnp.bfloat16)
    gain_one_own, bias_one_own, qkv_own, out_own, gain_two_own, bias_two_own, up_own, down_own = (
        lax.psum_scatter(gain_one_grad, ("wide", "narrow"), scatter_dimension=0, tiled=True),
        lax.psum_scatter(bias_one_grad, ("wide", "narrow"), scatter_dimension=0, tiled=True),
        lax.psum_scatter(qkv_weight_grad, ("wide", "narrow"), scatter_dimension=0, tiled=True),
        lax.psum_scatter(out_weight_grad, ("wide", "narrow"), scatter_dimension=0, tiled=True),
        lax.psum_scatter(gain_two_grad, ("wide", "narrow"), scatter_dimension=0, tiled=True),
        lax.psum_scatter(bias_two_grad, ("wide", "narrow"), scatter_dimension=0, tiled=True),
        lax.psum_scatter(up_weight_grad, ("wide", "narrow"), scatter_dimension=1, tiled=True),
        lax.psum_scatter(down_weight_grad, ("wide", "narrow"), scatter_dimension=0, tiled=True),
    )
    return (
        output,
        input_grad,
        gain_one_own,
        bias_one_own,
        qkv_own,
        out_own,
        gain_two_own,
        bias_two_own,
        up_own,
        down_own,
    )


def solution(mesh):
    return jax.shard_map(
        on_device,
        mesh=mesh,
        in_specs=(
            P(("wide", "narrow"), None),
            P(("wide", "narrow"), None),
            P(("wide", "narrow")),
            P(("wide", "narrow")),
            P(("wide", "narrow"), None),
            P(("wide", "narrow"), None),
            P(("wide", "narrow")),
            P(("wide", "narrow")),
            P(None, ("wide", "narrow")),
            P(("wide", "narrow"), None),
            P(("wide", "narrow"), None),
        ),
        out_specs=(
            P(("wide", "narrow"), None),
            P(("wide", "narrow"), None),
            P(("wide", "narrow")),
            P(("wide", "narrow")),
            P(("wide", "narrow"), None),
            P(("wide", "narrow"), None),
            P(("wide", "narrow")),
            P(("wide", "narrow")),
            P(None, ("wide", "narrow")),
            P(("wide", "narrow"), None),
        ),
        check_vma=False,
    )
```

profile of v0, /device:TPU:0, one launch (start us, length us, event | category | flops | bytes accessed | tf_op | source)
XLA Modules:
  0.0 2601.9 jit_solution(13123046285561315284)
XLA Ops:
  13.4 68.4 %all-reduce.13 = (bf16[768]{0:T(1024)(128)(2,1)S(1)}, bf16[768]{0:T(1024)(128)(2,1)S(1)}, bf16[768]{0:T(1024)(128)(2,1)S(1)}, bf16[768]{0:T(1024)(128)(2,1)S(1)}) all-reduce(bf16[768]{0:T(1024)(128)(2,1)S(1)} %dynamic-update-slice.1, bf16[768]{0:T(1024)(128)(2,1)S(1)} %dynamic-update-slice, ...), channel_id=1, replica_groups=mesh['wide'=16,'narrow'=8] {'wide','narrow'}, use_global_device_ids=true, to_apply=%add.1 | all-reduce | flops 3072 | bytes 12288
  86.9 222.2 %all-gather.13.cloned.1.call-done = bf16[128,6,768]{2,1,0:T(8,128)(2,1)} async-done(((bf16[1,6,768]{2,1,0:T(8,128)(2,1)}), bf16[128,6,768]{2,1,0:T(8,128)(2,1)}) %all-gather.13.cloned.1.call-update) | async-done | bytes 1179664 | tf_op jit(solution)/shard_map/all_gather | solution.py:88
  309.1 3.2 reshape.157
  312.3 307.0 %all-gather.11.cloned.1.call-done = bf16[128,6,2304]{2,1,0:T(8,128)(2,1)} async-done(((bf16[1,6,2304]{2,1,0:T(8,128)(2,1)}), bf16[128,6,2304]{2,1,0:T(8,128)(2,1)}) %all-gather.11.cloned.1.call-update) | async-done | bytes 3538960 | tf_op jit(solution)/shard_map/all_gather | solution.py:87
  619.3 6.6 reshape.155
  625.9 5.5 convolution_convert_fusion.1
  631.4 2.8 copy.44
  637.7 39.9 %while.30 = (s32[]{:T(128)}, bf16[12,512,64]{1,2,0:T(8,128)(2,1)}, f32[12,512]{1,0:T(8,128)S(1)}, bf16[12,512,64]{1,2,0:T(8,128)(2,1)}, bf16[12,512,64]{1,2,0:T(...) while((s32[]{:T(128)}, bf16[12,512,64]{1,2,0:T(8,128)(2,1)}, ...), condition=%wide.region_7.8_spmd.clone, body=%wide.region_4.7_spmd.clone.sunk | while | flops 70286848 | bytes 4483185 | solution.py:126
  681.8 248.0 %all-gather.7.cloned.1.call-done = bf16[768,3072]{0,1:T(8,128)(2,1)} async-done(((bf16[768,24]{0,1:T(8,128)(2,1)}), bf16[768,3072]{0,1:T(8,128)(2,1)}) %all-gather.7.cloned.1.call-update) | async-done | bytes 4718608 | tf_op jit(solution)/shard_map/all_gather | solution.py:93
  929.8 8.1 fusion.126
  937.9 302.7 %all-gather.9.cloned.1.call-done = bf16[3072,768]{1,0:T(8,128)(2,1)} async-done(((bf16[24,768]{1,0:T(8,128)(2,1)}), bf16[3072,768]{1,0:T(8,128)(2,1)}) %all-gather.9.cloned.1.call-update) | async-done | bytes 4718608 | tf_op jit(solution)/shard_map/all_gather | solution.py:94
  1240.6 8.9 fusion.58
  1251.2 5.4 fusion.125
  1259.0 6.9 multiply_reduce_fusion.1
  1272.6 9.7 fusion.110
  1282.3 113.7 %while.31 = (s32[]{:T(128)}, f32[512,512]{0,1:T(8,128)}, bf16[11,512,64]{1,2,0:T(8,128)(2,1)}, bf16[11,512,64]{1,2,0:T(8,128)(2,1)}, bf16[11,512,64]{1,2,0:T(8,1...) while((s32[]{:T(128)}, f32[512,512]{0,1:T(8,128)}, ...), condition=%wide.region_15.16_spmd.clone, body=%wide.region_13.15_spmd.clone.sunk | while | flops 171769344 | bytes 11881627 | solution.py:191
  1356.9 2.7 fusion.178
  1377.7 2.7 fusion.178
  1399.1 2.7 fusion.77
  1408.1 5.2 fusion.122
  1413.4 392.9 %fusion.127 = (f32[8,2304]{1,0:T(8,128)S(1)}, f32[8,768]{1,0:T(8,128)S(1)}) fusion(f32[768,2304]{1,0:T(8,128)} %fusion.122, f32[768,768]{1,0:T(8,128)} %fusion.107), kind=kCustom, calls=%all-reduce-scatter.2 | all-reduce-scatter fusion | flops 3145729 | bytes 9535488
  1818.1 15.7 collective-permute-start.54
  1833.8 5.4 collective-permute-start.53
  1839.2 3.4 collective-permute-start.52
  1850.9 7.4 collective-permute-start.46
  1862.3 3.6 collective-permute-start.43
  1867.4 3.8 collective-permute-start.41
  1874.3 6.9 collective-permute-start.38
  1885.8 3.8 collective-permute-start.36
  1892.1 3.6 collective-permute-start.34
  1895.8 5.5 collective-permute-start.33
  1903.2 3.0 collective-permute-start.29
  1912.1 9.3 add_convert_fusion
  1925.1 7.1 collective-permute-start.22
  1934.8 3.1 fusion.72
  1945.7 6.0 collective-permute-start.14
  1957.7 2.8 collective-permute-start.10
  1960.5 4.3 collective-permute-start.9
  1966.8 3.2 collective-permute-start.7
  1970.0 6.1 collective-permute-start.6
  1979.8 64.2 %all-reduce.12 = (f32[768]{0:T(1024)S(1)}, f32[768]{0:T(1024)S(1)}, f32[768]{0:T(1024)S(1)}, f32[768]{0:T(1024)S(1)}) all-reduce(f32[768]{0:T(1024)} %get-tuple-element.247, f32[768]{0:T(1024)} %get-tuple-element.252, f32[768]{0:T(1024)S(1)} %get-tuple-element.245, ...), channel_id=2, replica_groups=mesh['wide'=16,'narrow'=8] {'wide','narrow'}, use_global_device_ids=true, to_apply=%region_19.20.clone | all-reduce | flops 3072 | bytes 24576
  2046.3 25.7 concatenate.24
  2074.1 3.0 collective-permute-start.3
  2077.1 4.5 collective-permute-start.2
  2081.6 3.8 collective-permute-start.1
  2085.4 3.0 collective-permute-start
  2090.4 20.2 concatenate.23
  2111.3 483.6 %reduce-scatter.9.cloned.1.call-done = f32[24,768]{1,0:T(8,128)} async-done(((f32[3072,768]{1,0:T(8,128)}), f32[24,768]{1,0:T(8,128)}) %reduce-scatter.9.cloned.1.call-update) | async-done | bytes 73744 | tf_op jit(solution)/shard_map/reduce_scatter | solution.py:232
  (446 shorter events, 261.2 us)
Async XLA Ops:
  7.2 301.9 %all-gather.13.cloned.1.call-start = ((), (), s32[]{:S(2)}) async-start(), calls=%async_computation.7 | async-start | bytes 1585152 | tf_op jit(solution)/shard_map/all_gather | solution.py:88
  7.9 611.4 %all-gather.11.cloned.1.call-start = ((), (), s32[]{:S(2)}) async-start(), calls=%async_computation.6 | async-start | bytes 4755456 | tf_op jit(solution)/shard_map/all_gather | solution.py:87
  8.7 921.1 %all-gather.7.cloned.1.call-start = ((), (), s32[]{:S(2)}) async-start(), calls=%async_computation.2 | async-start | bytes 4755456 | tf_op jit(solution)/shard_map/all_gather | solution.py:93
  9.4 1231.2 %all-gather.9.cloned.1.call-start = ((), (), s32[]{:S(2)}) async-start(), calls=%async_computation.3 | async-start | bytes 4755456 | tf_op jit(solution)/shard_map/all_gather | solution.py:94
  10.0 2101.3 %reduce-scatter.7.cloned.1.call-start = ((), (), s32[]{:S(2)}) async-start(), calls=%async_computation.4 | async-start | bytes 9510912 | tf_op jit(solution)/shard_map/reduce_scatter | solution.py:231
  1256.7 1338.2 %reduce-scatter.9.cloned.1.call-start = ((), (), s32[]{:S(2)}) async-start(), calls=%async_computation.5 | async-start | bytes 9510912 | tf_op jit(solution)/shard_map/reduce_scatter | solution.py:232
  1812.8 21.0 collective-permute-start.58
  1814.1 25.1 collective-permute-start.57
  1815.4 27.2 %collective-permute-start.56 = (f32[8,768]{1,0:T(8,128)S(1)}, f32[8,768]{1,0:T(8,128)S(1)}, u32[]{:S(2)}, u32[]{:S(2)}) collective-permute-start(f32[8,768]{1,0:T(8,128)S(1)} %get-tuple-element.304), channel_id=1, source_target_pairs={{0,25},{1,26},{2,27},{3,28},{4,29},{5,30},{6,31},{7,32},{8,33},{9,... | collective-permute-start | bytes 73736
  1816.8 27.2 %collective-permute-start.55 = (f32[8,768]{1,0:T(8,128)S(1)}, f32[8,768]{1,0:T(8,128)S(1)}, u32[]{:S(2)}, u32[]{:S(2)}) collective-permute-start(f32[8,768]{1,0:T(8,128)S(1)} %get-tuple-element.304), channel_id=1, source_target_pairs={{0,24},{1,25},{2,26},{3,27},{4,28},{5,29},{6,30},{7,31},{8,32},{9,... | collective-permute-start | bytes 73736
  1818.1 27.2 %collective-permute-start.54 = (f32[8,768]{1,0:T(8,128)S(1)}, f32[8,768]{1,0:T(8,128)S(1)}, u32[]{:S(2)}, u32[]{:S(2)}) collective-permute-start(f32[8,768]{1,0:T(8,128)S(1)} %get-tuple-element.304), channel_id=1, source_target_pairs={{0,23},{1,24},{2,25},{3,26},{4,27},{5,28},{6,29},{7,30},{8,31},{9,... | collective-permute-start | bytes 73736
  1833.8 13.6 collective-permute-start.53
  1844.0 14.4 collective-permute-start.50
  1845.3 14.4 collective-permute-start.49
  1847.5 14.8 collective-permute-start.48
  1849.6 16.3 collective-permute-start.47
  1850.9 16.5 collective-permute-start.46
  1859.7 12.8 collective-permute-start.44
  1865.9 15.3 collective-permute-start.42
  1867.4 15.7 collective-permute-start.41
  1871.2 13.2 collective-permute-start.40
  1872.6 13.2 collective-permute-start.39
  1874.3 15.3 collective-permute-start.38
  1881.8 28.8 %collective-permute-start.30 = (f32[8,2304]{1,0:T(8,128)S(1)}, f32[8,2304]{1,0:T(8,128)S(1)}, u32[]{:S(2)}, u32[]{:S(2)}) collective-permute-start(f32[8,2304]{1,0:T(8,128)S(1)} %get-tuple-element.303), channel_id=1, source_target_pairs={{0,31},{1,32},{2,33},{3,34},{4,35},{5,36},{6,37},{7,38},{8,39},{9,... | collective-permute-start | bytes 221192
  1883.1 26.2 %collective-permute-start.31 = (f32[6,2304]{1,0:T(8,128)S(1)}, f32[6,2304]{1,0:T(8,128)S(1)}, u32[]{:S(2)}, u32[]{:S(2)}) collective-permute-start(f32[6,2304]{1,0:T(8,128)S(1)} %slice.101), channel_id=1, source_target_pairs={{0,32},{1,33},{2,34},{3,35},{4,36},{5,37},{6,38},{7,39},{8,40},{9,... | collective-permute-start | bytes 165896
  1903.2 18.1 collective-permute-start.29
  1906.3 17.5 collective-permute-start.28
  1907.6 17.5 collective-permute-start.27
  1909.3 22.9 collective-permute-start.26
  1910.6 22.9 collective-permute-start.25
  1921.4 16.5 collective-permute-start.24
  1923.8 15.4 collective-permute-start.23
  1925.1 15.4 collective-permute-start.22
  1940.5 13.1 collective-permute-start.17
  1941.8 13.8 collective-permute-start.16
  1943.9 13.8 collective-permute-start.15
  1945.7 14.8 collective-permute-start.14
  1951.8 13.1 collective-permute-start.13
  1953.7 13.1 collective-permute-start.12
  1955.6 14.4 collective-permute-start.11
  1957.7 18.4 collective-permute-start.10
  1960.5 111.5 %collective-permute-start.9 = (f32[8,2304]{1,0:T(8,128)S(1)}, f32[8,2304]{1,0:T(8,128)}, u32[]{:S(2)}, u32[]{:S(2)}) collective-permute-start(f32[8,2304]{1,0:T(8,128)S(1)} %get-tuple-element.303), channel_id=1, source_target_pairs={{0,10},{1,11},{2,12},{3,13},{4,14},{5,15},{6,16},{7,17},{8,18},{9,... | collective-permute-start | bytes 221192
  1964.9 109.2 %collective-permute-start.8 = (f32[8,2304]{1,0:T(8,128)S(1)}, f32[8,2304]{1,0:T(8,128)}, u32[]{:S(2)}, u32[]{:S(2)}) collective-permute-start(f32[8,2304]{1,0:T(8,128)S(1)} %get-tuple-element.303), channel_id=1, source_target_pairs={{0,9},{1,10},{2,11},{3,12},{4,13},{5,14},{6,15},{7,16},{8,17},{9,1... | collective-permute-start | bytes 221192
  1966.8 110.3 %collective-permute-start.7 = (f32[8,2304]{1,0:T(8,128)S(1)}, f32[8,2304]{1,0:T(8,128)}, u32[]{:S(2)}, u32[]{:S(2)}) collective-permute-start(f32[8,2304]{1,0:T(8,128)S(1)} %get-tuple-element.303), channel_id=1, source_target_pairs={{0,8},{1,9},{2,10},{3,11},{4,12},{5,13},{6,14},{7,15},{8,16},{9,17... | collective-permute-start | bytes 221192
  1970.0 111.7 %collective-permute-start.6 = (f32[8,2304]{1,0:T(8,128)S(1)}, f32[8,2304]{1,0:T(8,128)}, u32[]{:S(2)}, u32[]{:S(2)}) collective-permute-start(f32[8,2304]{1,0:T(8,128)S(1)} %get-tuple-element.303), channel_id=1, source_target_pairs={{0,7},{1,8},{2,9},{3,10},{4,11},{5,12},{6,13},{7,14},{8,15},{9,16}... | collective-permute-start | bytes 221192
  1976.0 109.4 %collective-permute-start.5 = (f32[8,2304]{1,0:T(8,128)S(1)}, f32[8,2304]{1,0:T(8,128)}, u32[]{:S(2)}, u32[]{:S(2)}) collective-permute-start(f32[8,2304]{1,0:T(8,128)S(1)} %get-tuple-element.303), channel_id=1, source_target_pairs={{0,6},{1,7},{2,8},{3,9},{4,10},{5,11},{6,12},{7,13},{8,14},{9,15},... | collective-permute-start | bytes 221192
  2072.1 17.0 collective-permute-start.4
  2074.1 14.9 collective-permute-start.3
  (86 other events, 2256.3 us)
Sparse Core Ops, SparseCore 0:
  9.7 299.3 all-gather.12
  310.8 308.4 all-gather.10
  621.0 308.7 all-gather.6
  931.3 309.2 all-gather.8
  1256.8 683.4 reduce-scatter.6
  1943.1 651.7 reduce-scatter.8
where the time goes:
time: 2620 us; the launch traced here: 2600 us
  waiting for transfers between devices  1570 us (60%)
  blocking collectives  525 us (20%)
  matrix products  199 us (8%)
  starting transfers between devices  174 us (7%)
  local copies, waits for them, and re-layouts  80.4 us (3%)
  other arithmetic  39.3 us (1%)
    unnamed x3, blocking collectives  525 us
    reduce_scatter x1, waiting for transfers between devices, on_device(): lax.psum_scatter(down_weight_grad, ('wide', 'narrow'), scatter_dimension=...  484 us
    all_gather x1, waiting for transfers between devices, on_device(): lax.all_gather(qkv_weight, ('wide', 'narrow'), axis=0, tiled=True)  307 us
    all_gather x1, waiting for transfers between devices, on_device(): lax.all_gather(down_weight, ('wide', 'narrow'), axis=0, tiled=True)  303 us
    all_gather x1, waiting for transfers between devices, on_device(): lax.all_gather(up_weight, ('wide', 'narrow'), axis=1, tiled=True)  248 us
    all_gather x1, waiting for transfers between devices, on_device(): lax.all_gather(out_weight, ('wide', 'narrow'), axis=0, tiled=True)  222 us
    unnamed x64, starting transfers between devices  174 us
    unnamed x148, local copies, waits for them, and re-layouts  70.9 us
  transfers between devices with their start and end apart: 70, of which 6 were waited for; matrix products, arithmetic and copies ran while one was open for 26% of the time, Pallas kernels for 0%

commit v1 on v0

v1 whole, which is shorter than its diff:
```python
import itertools

import jax
import jax.numpy as jnp
from jax import lax
from jax.experimental import pallas as pl
from jax.experimental.pallas import tpu as pltpu
from jax.sharding import PartitionSpec as P

BF = jnp.bfloat16
F32 = jnp.float32
I32 = jnp.int32
AXES = ("wide", "narrow")
D = 768
ROWS = 512
FF = 3072
OWN = 6
SLOT = 8
PEERS = 64
HALF = PEERS * SLOT
EPS = 1e-05
FAR = 1e30
TANH_SCALE = 0.7978845608028654
TANH_CUBE = 0.044715
MIB = 1 << 20


def device_number(x, y, z, core):
    return ((x & 1) * 8 + y * 2 + core) * 8 + (x >> 1) * 4 + z


def peer_groups(dims):
    sizes = dict(x=4, y=4, z=4, c=2)
    rest = [name for name in "xyzc" if name not in dims]
    groups = []
    for fixed in itertools.product(*[range(sizes[name]) for name in rest]):
        members = []
        for moving in itertools.product(*[range(sizes[name]) for name in dims]):
            at = dict(zip(rest, fixed))
            at.update(zip(dims, moving))
            members.append(device_number(at["x"], at["y"], at["z"], at["c"]))
        groups.append(members)
    return groups


def core_pairs():
    return [
        (device_number(x, y, z, c), device_number(x, y, z, 1 - c))
        for x, y, z, c in itertools.product(range(4), range(4), range(4), range(2))
    ]


def dot_nn(left, right):
    return lax.dot_general(left, right, (((1,), (0,)), ((), ())), preferred_element_type=F32)


def dot_nt(left, right):
    return lax.dot_general(left, right, (((1,), (1,)), ((), ())), preferred_element_type=F32)


def dot_tn(left, right):
    return lax.dot_general(left, right, (((0,), (0,)), ((), ())), preferred_element_type=F32)


def iota(shape, dim):
    return lax.broadcasted_iota(I32, shape, dim)


def one_hot(mask):
    return jnp.where(mask, 1.0, 0.0).astype(BF)


def split_low(values):
    high = values.astype(BF)
    return high, (values - high.astype(F32)).astype(BF)


def owner(group, core):
    z = group >> 4
    y = (group >> 2) & 3
    x = group & 3
    return ((x & 1) << 6) + (y << 4) + (core << 3) + ((x >> 1) << 2) + z


def sixth(number):
    return (number * 43691) >> 18


def place_matrix(core):
    slot = iota((1, HALF), 1)
    inner = slot & 7
    feature = jnp.where(inner < OWN, owner(slot >> 3, core) * OWN + inner, -1)
    return one_hot(iota((D, HALF), 0) == feature)


def vector_lanes(which):
    feature = iota((1, D), 1)
    lane = which * OWN + feature - OWN * sixth(feature)
    return iota((128, D), 0) == lane


def owned_features(core):
    return owner(iota((PEERS, 1), 0), core) == sixth(iota((1, D), 1))


def unpack_vectors(weights, core, count):
    pick = one_hot(iota((PEERS, HALF), 1) == iota((PEERS, HALF), 0) * SLOT + OWN)
    packed = dot_nn(pick, weights).astype(BF)
    mine = owned_features(core)
    return [
        jnp.sum(
            jnp.where(mine, dot_nn(packed, one_hot(vector_lanes(which))), 0.0),
            axis=0,
            keepdims=True,
        )
        for which in range(count)
    ]


def pack_vectors(vectors, core):
    mine = owned_features(core)
    total = jnp.zeros((PEERS, 128), F32)
    for which, vector in enumerate(vectors):
        spread = jnp.where(mine, vector, 0.0).astype(BF)
        total = total + dot_nt(spread, one_hot(vector_lanes(which)))
    put = one_hot(iota((HALF, PEERS), 0) == iota((HALF, PEERS), 1) * SLOT + OWN)
    return dot_nn(put, total.astype(BF))


def norm_stats(values):
    center = values - jnp.mean(values, axis=-1, keepdims=True)
    inverse = lax.rsqrt(jnp.mean(center * center, axis=-1, keepdims=True) + EPS)
    return center * inverse, inverse


def norm_pull(gradient, unit, inverse, gain):
    scaled = gradient * gain
    return inverse * (
        scaled
        - jnp.mean(scaled, axis=-1, keepdims=True)
        - unit * jnp.mean(scaled * unit, axis=-1, keepdims=True)
    )


def group_ends(lens_ref):
    ends = []
    total = 0
    for slot in range(4):
        total = total + lens_ref[0, slot]
        ends.append(total)
    return ends


def segments(positions, ends):
    return sum((positions >= end).astype(I32) for end in ends)


VM = pl.BlockSpec(memory_space=pltpu.VMEM)
SM = pl.BlockSpec(memory_space=pltpu.SMEM)
ANY = pl.BlockSpec(memory_space=pl.ANY)


def params(limit=56):
    return pltpu.CompilerParams(vmem_limit_bytes=limit * MIB)


def pack_kernel(
    g1_ref, b1_ref, qkv_ref, out_ref, g2_ref, b2_ref, up_ref, down_ref, early_ref, late_ref, es, ls
):
    es[...] = jnp.zeros_like(es)
    ls[...] = jnp.zeros_like(ls)
    qkv = qkv_ref[...].astype(F32)
    for part in range(3):
        es[SLOT * part : SLOT * part + OWN, :] = qkv[:, part * D : part * D + D]
    es[OWN : OWN + 1, 0:OWN] = g1_ref[...].astype(F32)
    es[OWN : OWN + 1, OWN : 2 * OWN] = b1_ref[...].astype(F32)
    up = up_ref[...].astype(F32).T
    down = down_ref[...].astype(F32)
    ls[0:16, :] = up[0:16]
    ls[16:32, :] = down[0:16]
    ls[32:40, :] = up[16:24]
    ls[40:48, :] = down[16:24]
    ls[48 : 48 + OWN, :] = out_ref[...].astype(F32)
    ls[48 + OWN : 49 + OWN, 0:OWN] = g2_ref[...].astype(F32)
    ls[48 + OWN : 49 + OWN, OWN : 2 * OWN] = b2_ref[...].astype(F32)
    early_ref[...] = es[...].astype(BF)
    late_ref[...] = ls[...].astype(BF)


def pack(g1, b1, qkv, out, g2, b2, up, down):
    return pl.pallas_call(
        pack_kernel,
        out_shape=(
            jax.ShapeDtypeStruct((24, D), BF),
            jax.ShapeDtypeStruct((64, D), BF),
        ),
        in_specs=[VM] * 8,
        out_specs=(VM, VM),
        scratch_shapes=[pltpu.VMEM((24, D), F32), pltpu.VMEM((64, D), F32)],
        compiler_params=params(),
        name="pack",
    )(g1[None], b1[None], qkv, out, g2[None], b2[None], up, down)


def project_kernel(core_ref, x_ref, own_ref, oth_ref, h_ref, qkv_ref, w_ref, ln_ref, hs):
    core = core_ref[0, 0]
    gain = jnp.zeros((1, D), F32)
    bias = jnp.zeros((1, D), F32)
    for half, source in enumerate((own_ref, oth_ref)):

        @pl.loop(0, 4)
        def _(block):
            slab = source[pl.ds(block * 16, 16)].astype(F32)
            for part in range(3):
                rows = slab[:, SLOT * part : SLOT * part + SLOT, :].reshape(128, D)
                w_ref[half, part, pl.ds(pl.multiple_of(block * 128, 128), 128), :] = rows.astype(BF)

        side = core if half == 0 else 1 - core
        found = unpack_vectors(w_ref[half, 0, :, 0:128], side, 2)
        gain = gain + found[0]
        bias = bias + found[1]
    ln_ref[...] = jnp.zeros_like(ln_ref)
    ln_ref[0:1, :] = gain

    @pl.loop(0, 4)
    def _(block):
        rows = pl.ds(pl.multiple_of(block * 128, 128), 128)
        unit, _ = norm_stats(x_ref[rows, :].astype(F32))
        hs[rows, :] = (unit * gain + bias).astype(BF)

    for half in range(2):
        side = core if half == 0 else 1 - core
        h_ref[half] = dot_nn(hs[...], place_matrix(side)).astype(BF)
    for part in range(3):
        total = dot_nn(h_ref[0], w_ref[0, part]) + dot_nn(h_ref[1], w_ref[1, part])
        qkv_ref[:, part * D : part * D + D] = total.astype(BF)


def project(core, x, own, oth):
    return pl.pallas_call(
        project_kernel,
        out_shape=(
            jax.ShapeDtypeStruct((2, ROWS, HALF), BF),
            jax.ShapeDtypeStruct((ROWS, 3 * D), BF),
            jax.ShapeDtypeStruct((2, 3, HALF, D), BF),
            jax.ShapeDtypeStruct((8, D), F32),
        ),
        in_specs=[SM, VM, VM, VM],
        out_specs=(VM, VM, VM, VM),
        scratch_shapes=[pltpu.VMEM((ROWS, D), BF)],
        compiler_params=params(),
        name="project",
    )(core, x, own, oth)


def softplus4(logits):
    sharp = 4.0 * logits
    return 0.25 * (jnp.maximum(sharp, 0.0) + jnp.log(1.0 + jnp.exp(-jnp.abs(sharp))))


def block_masks(block, ends):
    count = (block + 1) * 128
    row = iota((128, 1), 0) + block * 128
    column = iota((1, count), 1)
    same = segments(row, ends) == segments(column, ends)
    first = column == 0
    for end in ends:
        first = first | (column == end)
    allowed = same & (column <= row)
    chosen = same & (column < row) & jnp.logical_not(first)
    return allowed, chosen


def attend_kernel(lens_ref, qkv_ref, attn_ref, pen_ref, lse_ref, carry):
    ends = group_ends(lens_ref)
    left = iota((1, 128), 1) < 64
    zero = jnp.zeros((), BF)
    q0 = jnp.where(left, qkv_ref[:, 0:128], zero) * jnp.asarray(0.125, BF)
    k0 = qkv_ref[:, D : D + 128]
    lower = one_hot(iota((128, 128), 0) > iota((128, 128), 1))
    carry[...] = jnp.zeros_like(carry)
    for block in range(4):
        count = (block + 1) * 128
        rows = slice(block * 128, count)
        allowed, chosen = block_masks(block, ends)
        chosen_values = jnp.where(chosen, softplus4(dot_nt(q0[rows], k0[:count])), 0.0)
        high, low = split_low(chosen_values)
        penalty = dot_nn(lower, high) + dot_nn(lower, low) + carry[0:1, :count]
        carry[0:1, :count] = carry[0:1, :count] + jnp.sum(chosen_values, axis=0, keepdims=True)
        pen_ref[rows, :count] = jnp.where(allowed, penalty, FAR)

    @pl.loop(0, 6)
    def _(pair):
        lanes = pl.ds(pl.multiple_of(pair * 128, 128), 128)
        q = qkv_ref[:, lanes] * jnp.asarray(0.125, BF)
        k = qkv_ref[:, pl.ds(pl.multiple_of(pair * 128 + D, 128), 128)]
        v = qkv_ref[:, pl.ds(pl.multiple_of(pair * 128 + 2 * D, 128), 128)]
        sides = (jnp.where(left, q, zero), jnp.where(left, zero, q))
        for block in range(4):
            count = (block + 1) * 128
            rows = slice(block * 128, count)
            mixed = []
            totals = []
            for side in sides:
                shifted = dot_nt(side[rows], k[:count]) - pen_ref[rows, :count]
                top = jnp.max(shifted, axis=-1, keepdims=True)
                exponent = jnp.exp(shifted - top)
                total = jnp.sum(exponent, axis=-1, keepdims=True)
                mixed.append(dot_nn((exponent * (1.0 / total)).astype(BF), v[:count]))
                totals.append(top + jnp.log(total))
            attn_ref[rows, lanes] = jnp.where(left, mixed[0], mixed[1]).astype(BF)
            lse_ref[pair, rows, :] = jnp.where(left, totals[0], totals[1])


def attend(lens, qkv):
    return pl.pallas_call(
        attend_kernel,
        out_shape=(
            jax.ShapeDtypeStruct((ROWS, D), BF),
            jax.ShapeDtypeStruct((ROWS, ROWS), F32),
            jax.ShapeDtypeStruct((6, ROWS, 128), F32),
        ),
        in_specs=[SM, VM],
        out_specs=(VM, VM, VM),
        scratch_shapes=[pltpu.VMEM((8, ROWS), F32)],
        compiler_params=params(),
        name="attend",
    )(lens, qkv)


def attend_back_kernel(
    lens_ref, qkv_ref, up_ref, pen_ref, lse_ref, dqkv_ref, total, kept, dk_acc, dv_acc, carry
):
    ends = group_ends(lens_ref)
    left = iota((1, 128), 1) < 64
    zero = jnp.zeros((), BF)
    scale = jnp.asarray(0.125, BF)
    total[...] = jnp.zeros_like(total)

    def pair_parts(pair):
        lanes = pl.ds(pl.multiple_of(pair * 128, 128), 128)
        q = qkv_ref[:, lanes] * scale
        k = qkv_ref[:, pl.ds(pl.multiple_of(pair * 128 + D, 128), 128)]
        v = qkv_ref[:, pl.ds(pl.multiple_of(pair * 128 + 2 * D, 128), 128)]
        return q, k, v, up_ref[:, lanes]

    def one_side(values, side):
        return jnp.where(left, values, zero) if side == 0 else jnp.where(left, zero, values)

    def score_gradient(qs, k, us, v, block, log_total):
        count = (block + 1) * 128
        rows = slice(block * 128, count)
        shifted = dot_nt(qs[rows], k[:count]) - pen_ref[rows, :count]
        soft = jnp.exp(shifted - log_total)
        gradient = dot_nt(us[rows], v[:count])
        inner = jnp.sum(gradient * soft, axis=-1, keepdims=True)
        return soft.astype(BF), soft * (gradient - inner)

    def run_pair(pair, skip_first):
        q, k, v, u = pair_parts(pair)
        dk_acc[...] = jnp.zeros_like(dk_acc)
        dv_acc[...] = jnp.zeros_like(dv_acc)
        lanes = pl.ds(pl.multiple_of(pair * 128, 128), 128)
        for block in range(4):
            count = (block + 1) * 128
            rows = slice(block * 128, count)
            log_totals = lse_ref[pair, rows, :]
            dq = []
            for side in range(2):
                qs, us = one_side(q, side), one_side(u, side)
                soft, dz = score_gradient(
                    qs, k, us, v, block, log_totals[:, side * 64 : side * 64 + 1]
                )
                total[rows, :count] = total[rows, :count] + dz
                dv_acc[:count, :] = dv_acc[:count, :] + dot_tn(soft, us[rows])
                if side == 0 and skip_first:
                    kept[rows, :count] = dz
                    dq.append(jnp.zeros((128, 128), F32))
                else:
                    low = dz.astype(BF)
                    dq.append(dot_nn(low, k[:count]))
                    dk_acc[:count, :] = dk_acc[:count, :] + dot_tn(low, qs[rows])
            dqkv_ref[rows, lanes] = (jnp.where(left, dq[0], dq[1]) * 0.125).astype(BF)
        dqkv_ref[:, pl.ds(pl.multiple_of(pair * 128 + D, 128), 128)] = dk_acc[...].astype(BF)
        dqkv_ref[:, pl.ds(pl.multiple_of(pair * 128 + 2 * D, 128), 128)] = dv_acc[...].astype(BF)

    @pl.loop(1, 6)
    def _(pair):
        run_pair(pair, False)

    run_pair(0, True)
    q, k, _, _ = pair_parts(0)
    qs = one_side(q, 0)
    upper = one_hot(iota((128, 128), 1) > iota((128, 128), 0))
    carry[...] = jnp.zeros_like(carry)
    for block in (3, 2, 1, 0):
        count = (block + 1) * 128
        rows = slice(block * 128, count)
        _, chosen = block_masks(block, ends)
        dz = total[rows, :count]
        high, low = split_low(dz)
        selected = -(dot_nn(upper, high) + dot_nn(upper, low) + carry[0:1, :count])
        carry[0:1, :count] = carry[0:1, :count] + jnp.sum(dz, axis=0, keepdims=True)
        sharp = 4.0 * dot_nt(qs[rows], k[:count])
        slope = 1.0 / (1.0 + jnp.exp(-sharp))
        low = (kept[rows, :count] + jnp.where(chosen, slope * selected, 0.0)).astype(BF)
        dq = dot_nn(low, k[:count]) * 0.125
        dqkv_ref[rows, 0:128] = jnp.where(left, dq, dqkv_ref[rows, 0:128].astype(F32)).astype(BF)
        dk_acc[:count, :] = dk_acc[:count, :] + dot_tn(low, qs[rows])
    dqkv_ref[:, D : D + 128] = dk_acc[...].astype(BF)


def attend_back(lens, qkv, upstream, pen, lse):
    return pl.pallas_call(
        attend_back_kernel,
        out_shape=jax.ShapeDtypeStruct((ROWS, 3 * D), BF),
        in_specs=[SM, VM, VM, VM, VM],
        out_specs=VM,
        scratch_shapes=[
            pltpu.VMEM((ROWS, ROWS), F32),
            pltpu.VMEM((ROWS, ROWS), F32),
            pltpu.VMEM((ROWS, 128), F32),
            pltpu.VMEM((ROWS, 128), F32),
            pltpu.VMEM((8, ROWS), F32),
        ],
        compiler_params=params(),
        name="attend_back",
    )(lens, qkv, upstream, pen, lse)


def feed_kernel(
    core_ref, lens_ref, x_ref, attn_ref, cot_ref, own_ref, oth_ref,
    y_ref, dx_ref, dattn_ref, lng_ref, ga_own, gb_own, go_own, ga_oth, gb_oth, go_oth,
    up_s, down_s, mid_s, out_s, gup_s, gdown_s, gmid_s, mid_f, wo_s, ap_s, h_s, dy_s, unit_s, acc_s, dh_s,
    sems, out_sems,
):
    core = core_ref[0, 0]
    sources = (own_ref, oth_ref)
    loads = {}

    def load(key, source, target, slot):
        loads[key] = pltpu.make_async_copy(source, target, sems.at[slot])
        loads[key].start()

    for half in range(2):
        load(("out", half), sources[half].at[:, 48:64, :], out_s.at[half], half)
    for half in range(2):
        for part in range(2):
            chunk = half * 3 + part
            devices = pl.ds(part * 32, 32)
            load(("up", chunk), sources[half].at[devices, 0:16, :], up_s.at[chunk], 2 + chunk)
            load(("down", chunk), sources[half].at[devices, 16:32, :], down_s.at[chunk], 8 + chunk)
        load(("mid", half), sources[half].at[:, 32:48, :], mid_s.at[half], 14 + half)

    gain = jnp.zeros((1, D), F32)
    bias = jnp.zeros((1, D), F32)
    for half in range(2):
        side = core if half == 0 else 1 - core
        loads["out", half].wait()
        rows = out_s[half].astype(F32)[:, 0:SLOT, :].reshape(HALF, D)
        wo_s[half] = rows.astype(BF)
        found = unpack_vectors(wo_s[half, :, 0:128], side, 2)
        gain = gain + found[0]
        bias = bias + found[1]
        ap_s[half] = dot_nn(attn_ref[...], place_matrix(side)).astype(BF)
    acc_s[...] = dot_nn(ap_s[0], wo_s[0]) + dot_nn(ap_s[1], wo_s[1])
    ends = group_ends(lens_ref)

    @pl.loop(0, 4)
    def _(block):
        rows = pl.ds(pl.multiple_of(block * 128, 128), 128)
        middle = x_ref[rows, :].astype(F32) + acc_s[rows, :]
        acc_s[rows, :] = middle
        unit, _ = norm_stats(middle)
        unit_s[rows, :] = unit
        h_s[rows, :] = (unit * gain + bias).astype(BF)
        live = (iota((128, 1), 0) + block * 128) < ends[3]
        dy_s[rows, :] = jnp.where(live, cot_ref[rows, :].astype(F32), 0.0).astype(BF)

    dh_s[...] = jnp.zeros_like(dh_s)
    for half in range(2):
        for part in range(2):
            loads["up", half * 3 + part].wait()
            loads["down", half * 3 + part].wait()
        loads["mid", half].wait()
        mid = mid_s[half].astype(F32)
        up_s[half * 3 + 2] = mid[:, 0:8, :].reshape(32, 16, D).astype(BF)
        down_s[half * 3 + 2] = mid[:, 8:16, :].reshape(32, 16, D).astype(BF)

    @pl.loop(0, 6)
    def _(chunk):
        up = up_s[chunk].reshape(ROWS, D)
        down = down_s[chunk].reshape(ROWS, D)
        value = dot_nt(h_s[...], up)
        square = value * value
        bend = jnp.tanh(TANH_SCALE * (value + TANH_CUBE * (value * square)))
        act = (0.5 * value * (1.0 + bend)).astype(BF)
        slope = 0.5 * (1.0 + bend) + (0.5 * TANH_SCALE) * value * (1.0 - bend * bend) * (
            1.0 + 3.0 * TANH_CUBE * square
        )
        pulled = (dot_nt(dy_s[...], down) * slope).astype(BF)
        acc_s[...] = acc_s[...] + dot_nn(act, down)
        dh_s[...] = dh_s[...] + dot_nn(pulled, up)
        gdown_s[chunk] = dot_tn(act, dy_s[...]).astype(BF).reshape(32, 16, D)
        gup_s[chunk] = dot_tn(pulled, h_s[...]).astype(BF).reshape(32, 16, D)

    stores = []

    def store(source, target, slot):
        copy = pltpu.make_async_copy(source, target, out_sems.at[slot])
        copy.start()
        stores.append(copy)

    for half, (big, small) in enumerate(((ga_own, gb_own), (ga_oth, gb_oth))):
        for part in range(2):
            chunk = half * 3 + part
            devices = pl.ds(part * 32, 32)
            store(gup_s.at[chunk], big.at[devices, 0:16, :], half * 5 + part * 2)
            store(gdown_s.at[chunk], big.at[devices, 16:32, :], half * 5 + part * 2 + 1)
        mid_f[:, 0:8, :] = gup_s[half * 3 + 2].astype(F32).reshape(PEERS, 8, D)
        mid_f[:, 8:16, :] = gdown_s[half * 3 + 2].astype(F32).reshape(PEERS, 8, D)
        gmid_s[half] = mid_f[...].astype(BF)
        store(gmid_s.at[half], small, half * 5 + 4)

    lng_ref[...] = jnp.zeros_like(lng_ref)

    @pl.loop(0, 4)
    def _(block):
        rows = pl.ds(pl.multiple_of(block * 128, 128), 128)
        y_ref[rows, :] = acc_s[rows, :].astype(BF)
        unit = unit_s[rows, :]
        gradient = dh_s[rows, :]
        lng_ref[0:1, :] = lng_ref[0:1, :] + jnp.sum(gradient * unit, axis=0, keepdims=True)
        lng_ref[1:2, :] = lng_ref[1:2, :] + jnp.sum(gradient, axis=0, keepdims=True)

    middle_rows = dot_nn(ap_s[0], wo_s[0]) + dot_nn(ap_s[1], wo_s[1])
    acc_s[...] = middle_rows

    @pl.loop(0, 4)
    def _(block):
        rows = pl.ds(pl.multiple_of(block * 128, 128), 128)
        _, inverse = norm_stats(x_ref[rows, :].astype(F32) + acc_s[rows, :])
        moved = dy_s[rows, :].astype(F32) + norm_pull(dh_s[rows, :], unit_s[rows, :], inverse, gain)
        dx_ref[rows, :] = moved
        h_s[rows, :] = moved.astype(BF)

    total = jnp.zeros((ROWS, D), F32)
    for half, target in enumerate((go_own, go_oth)):
        side = core if half == 0 else 1 - core
        target[...] = dot_tn(ap_s[half], h_s[...]).reshape(PEERS, SLOT, D).astype(BF)
        total = total + dot_nt(dot_nt(h_s[...], wo_s[half]).astype(BF), place_matrix(side))
    dattn_ref[...] = total.astype(BF)
    for copy in stores:
        copy.wait()


def feed(core, lens, x, attn, cot, own, oth):
    big = jax.ShapeDtypeStruct((PEERS, 32, D), BF)
    small = jax.ShapeDtypeStruct((PEERS, 16, D), BF)
    outer = jax.ShapeDtypeStruct((PEERS, SLOT, D), BF)
    return pl.pallas_call(
        feed_kernel,
        out_shape=(
            jax.ShapeDtypeStruct((ROWS, D), BF),
            jax.ShapeDtypeStruct((ROWS, D), F32),
            jax.ShapeDtypeStruct((ROWS, D), BF),
            jax.ShapeDtypeStruct((8, D), F32),
            big, small, outer, big, small, outer,
        ),
        in_specs=[SM, SM, VM, VM, VM, ANY, ANY],
        out_specs=(VM, VM, VM, VM, ANY, ANY, VM, ANY, ANY, VM),
        scratch_shapes=[
            pltpu.VMEM((6, 32, 16, D), BF),
            pltpu.VMEM((6, 32, 16, D), BF),
            pltpu.VMEM((2, PEERS, 16, D), BF),
            pltpu.VMEM((2, PEERS, 16, D), BF),
            pltpu.VMEM((6, 32, 16, D), BF),
            pltpu.VMEM((6, 32, 16, D), BF),
            pltpu.VMEM((2, PEERS, 16, D), BF),
            pltpu.VMEM((PEERS, 16, D), F32),
            pltpu.VMEM((2, HALF, D), BF),
            pltpu.VMEM((2, ROWS, HALF), BF),
            pltpu.VMEM((ROWS, D), BF),
            pltpu.VMEM((ROWS, D), BF),
            pltpu.VMEM((ROWS, D), F32),
            pltpu.VMEM((ROWS, D), F32),
            pltpu.VMEM((ROWS, D), F32),
            pltpu.SemaphoreType.DMA((16,)),
            pltpu.SemaphoreType.DMA((10,)),
        ],
        compiler_params=params(),
        name="feed",
    )(core, lens, x, attn, cot, own, oth)


def project_back_kernel(
    core_ref, x_ref, dx_ref, h_ref, w_ref, dqkv_ref, ln_ref, lng_ref, dtok_ref, own_ref, oth_ref, dh_s, vec_s
):
    core = core_ref[0, 0]
    total = jnp.zeros((ROWS, D), F32)
    for half in range(2):
        side = core if half == 0 else 1 - core
        parts = dot_nt(dqkv_ref[:, 0:D], w_ref[half, 0])
        parts = parts + dot_nt(dqkv_ref[:, D : 2 * D], w_ref[half, 1])
        parts = parts + dot_nt(dqkv_ref[:, 2 * D : 3 * D], w_ref[half, 2])
        high, low = split_low(parts)
        place = place_matrix(side)
        total = total + dot_nt(high, place) + dot_nt(low, place)
    dh_s[...] = total
    vec_s[...] = jnp.zeros_like(vec_s)
    gain = ln_ref[0:1, :]

    @pl.loop(0, 4)
    def _(block):
        rows = pl.ds(pl.multiple_of(block * 128, 128), 128)
        unit, inverse = norm_stats(x_ref[rows, :].astype(F32))
        gradient = dh_s[rows, :]
        vec_s[0:1, :] = vec_s[0:1, :] + jnp.sum(gradient * unit, axis=0, keepdims=True)
        vec_s[1:2, :] = vec_s[1:2, :] + jnp.sum(gradient, axis=0, keepdims=True)
        moved = dx_ref[rows, :] + norm_pull(gradient, unit, inverse, gain)
        dtok_ref[rows, :] = moved.astype(BF)

    vectors = [vec_s[0:1, :], vec_s[1:2, :], lng_ref[0:1, :], lng_ref[1:2, :]]
    for half, target in enumerate((own_ref, oth_ref)):
        side = core if half == 0 else 1 - core
        pads = pack_vectors(vectors, side)
        pieces = []
        for part in range(3):
            piece = dot_tn(h_ref[half], dqkv_ref[:, part * D : part * D + D])
            if part == 0:
                piece = jnp.concatenate([piece[:, 0:128] + pads, piece[:, 128:]], axis=1)
            pieces.append(piece.reshape(PEERS, SLOT, D))
        target[...] = jnp.concatenate(pieces, axis=1).astype(BF)


def project_back(core, x, dx, h, w, dqkv, ln, lng):
    slab = jax.ShapeDtypeStruct((PEERS, 24, D), BF)
    return pl.pallas_call(
        project_back_kernel,
        out_shape=(jax.ShapeDtypeStruct((ROWS, D), BF), slab, slab),
        in_specs=[SM] + [VM] * 7,
        out_specs=(VM, VM, VM),
        scratch_shapes=[pltpu.VMEM((ROWS, D), F32), pltpu.VMEM((8, D), F32)],
        compiler_params=params(),
        name="project_back",
    )(core, x, dx, h, w, dqkv, ln, lng)


def join_kernel(a0, b0, c0, a1, b1, c1, out_ref):
    pieces = [
        left[...].astype(F32) + right[...].astype(F32)
        for left, right in ((a0, a1), (b0, b1), (c0, c1))
    ]
    out_ref[...] = jnp.concatenate(pieces, axis=1).astype(BF)


def join(own, received):
    sizes = (32, 16, SLOT)
    specs = [pl.BlockSpec((8, size, D), lambda i: (i, 0, 0)) for size in sizes]
    return pl.pallas_call(
        join_kernel,
        grid=(8,),
        out_shape=jax.ShapeDtypeStruct((PEERS, 56, D), BF),
        in_specs=specs + specs,
        out_specs=pl.BlockSpec((8, 56, D), lambda i: (i, 0, 0)),
        compiler_params=params(),
        name="join",
    )(*own, *received)


def finish_kernel(early_ref, qkv_ref, g1_ref, b1_ref, g2_ref, b2_ref):
    total = jnp.sum(early_ref[...].astype(F32), axis=0)
    for part in range(3):
        qkv_ref[:, part * D : part * D + D] = total[SLOT * part : SLOT * part + OWN, :]
    for which, target in enumerate((g1_ref, b1_ref, g2_ref, b2_ref)):
        target[...] = total[OWN : OWN + 1, which * OWN : which * OWN + OWN]


def finish(early):
    vector = jax.ShapeDtypeStruct((1, OWN), F32)
    return pl.pallas_call(
        finish_kernel,
        out_shape=(jax.ShapeDtypeStruct((OWN, 3 * D), F32), vector, vector, vector, vector),
        in_specs=[VM],
        out_specs=(VM,) * 5,
        compiler_params=params(),
        name="finish",
    )(early)


def unpack_kernel(late_ref, up_ref, down_ref, out_ref, down_s):
    late = late_ref[...].astype(F32)
    up_ref[...] = jnp.concatenate([late[0:16], late[32:40]], axis=0).T
    down_ref[...] = jnp.concatenate([late[16:32], late[40:48]], axis=0)
    out_ref[...] = late[48 : 48 + OWN]


def unpack(late):
    return pl.pallas_call(
        unpack_kernel,
        out_shape=(
            jax.ShapeDtypeStruct((D, 24), F32),
            jax.ShapeDtypeStruct((24, D), F32),
            jax.ShapeDtypeStruct((OWN, D), F32),
        ),
        in_specs=[VM],
        out_specs=(VM,) * 3,
        scratch_shapes=[pltpu.VMEM((8, D), F32)],
        compiler_params=params(),
        name="unpack",
    )(late)


def on_device(
    tokens,
    seq_lengths,
    ln1_gain,
    ln1_bias,
    qkv_weight,
    out_weight,
    ln2_gain,
    ln2_bias,
    up_weight,
    down_weight,
    cotangent,
):
    core = (lax.axis_index("wide") & 1).astype(I32).reshape(1, 1)
    everyone = peer_groups("zyx")
    pairs = core_pairs()
    early, late = pack(
        ln1_gain, ln1_bias, qkv_weight, out_weight, ln2_gain, ln2_bias, up_weight, down_weight
    )
    late_own = lax.all_gather(late, AXES, axis_index_groups=everyone)
    early_own = lax.all_to_all(
        jnp.broadcast_to(early, (PEERS, 24, D)), AXES, 0, 0, axis_index_groups=everyone, tiled=True
    )
    early_oth = lax.ppermute(early_own, AXES, pairs)
    h_slots, qkv, weights, ln_rows = project(core, tokens, early_own, early_oth)
    attn, penalty, log_totals = attend(seq_lengths, qkv)
    late_oth = lax.ppermute(late_own, AXES, pairs)
    output, dx, dattn, ln_grads, *slabs = feed(
        core, seq_lengths, tokens, attn, cotangent, late_own, late_oth
    )
    received = [lax.ppermute(slab, AXES, pairs) for slab in slabs[3:]]
    joined = join(slabs[:3], received).reshape(PEERS * 56, D)
    for dim in "zyx":
        joined = lax.psum_scatter(
            joined, AXES, scatter_dimension=0, axis_index_groups=peer_groups(dim), tiled=True
        )
    dqkv = attend_back(seq_lengths, qkv, dattn, penalty, log_totals)
    dtokens, tail_own, tail_oth = project_back(
        core, tokens, dx, h_slots, weights, dqkv, ln_rows, ln_grads
    )
    tail_received = lax.ppermute(tail_oth, AXES, pairs)
    tail = (tail_own.astype(F32) + tail_received.astype(F32)).astype(BF)
    tail = lax.all_to_all(tail, AXES, 0, 0, axis_index_groups=everyone, tiled=True)
    qkv_grad, g1_grad, b1_grad, g2_grad, b2_grad = finish(tail)
    up_grad, down_grad, out_grad = unpack(joined)
    return (
        output,
        dtokens,
        g1_grad.reshape(OWN),
        b1_grad.reshape(OWN),
        qkv_grad,
        out_grad,
        g2_grad.reshape(OWN),
        b2_grad.reshape(OWN),
        up_grad,
        down_grad,
    )


def solution(mesh):
    rows = P(AXES, None)
    flat = P(AXES)
    columns = P(None, AXES)
    return jax.shard_map(
        on_device,
        mesh=mesh,
        in_specs=(rows, rows, flat, flat, rows, rows, flat, flat, columns, rows, rows),
        out_specs=(rows, rows, flat, flat, rows, rows, flat, flat, columns, rows),
        check_vma=False,
    )
```

time: 2620 us -> 358 us (0.14)
  waiting for transfers between devices: 1570 us -> 161 us
  blocking collectives: 525 us -> 42.1 us
  matrix products: 199 us -> 0 us
  starting transfers between devices: 174 us -> 9.63 us
  Pallas kernels: 0 us -> 119 us
  local copies, waits for them, and re-layouts: 80.4 us -> 8.18 us
  other arithmetic: 39.3 us -> 3.69 us
    all_gather x4 -> x1, waiting for transfers between devices: 1080 us -> 75.1 us  [on_device(): late_own = lax.all_gather(late, AXES, axis_index_groups=everyone)]
    unnamed x3 -> x0, blocking collectives: 525 us -> none
    reduce_scatter x2 -> x3, waiting for transfers between devices: 484 us -> 73 us  [on_device(): lax.psum_scatter(joined, AXES, scatter_dimension=0, axis_index_groups=pee...]
    dot_general x98 -> x0, matrix products: 199 us -> none  [the longest x40 65.9 us: matmul_nt(): lax.dot_general(left_side, right_side, (((1,), (1,)), ((), ())), preferre...]
    unnamed x64 -> x0, starting transfers between devices: 174 us -> none
    pallas_call x0 -> x9, Pallas kernels: none -> 119 us  [the longest x1 32.8 us: feed(): pl.pallas_call(feed_kernel, out_shape=(jax.ShapeDtypeStruct((ROWS, D), BF...]
    unnamed x148 -> x12, local copies, waits for them, and re-layouts: 70.9 us -> 7.26 us
    all_to_all x0 -> x1, blocking collectives: none -> 42.1 us  [on_device(): lax.all_to_all(jnp.broadcast_to(early, (PEERS, 24, D)), AXES, 0, 0, axis_...]
  transfers between devices with their start and end apart: 70 -> 11, of which waited for: 6 -> 6; matrix products, arithmetic and copies ran while one was open for 26% -> 1% of each run, Pallas kernels for 0% -> 21%
where the time goes in v1:
time: 358 us; the launch traced here: 357 us
  waiting for transfers between devices  161 us (45%)
  Pallas kernels  119 us (33%)
  blocking collectives  42.1 us (12%)
  between operations  13.8 us (4%)
  starting transfers between devices  9.63 us (3%)
  local copies, waits for them, and re-layouts  8.18 us (2%)
  other arithmetic  3.69 us (1%)
    all_gather x1, waiting for transfers between devices, on_device(): late_own = lax.all_gather(late, AXES, axis_index_groups=everyone)  75.1 us
    reduce_scatter x3, waiting for transfers between devices, on_device(): lax.psum_scatter(joined, AXES, scatter_dimension=0, axis_index_groups=pee...  73 us
    all_to_all x1, blocking collectives, on_device(): lax.all_to_all(jnp.broadcast_to(early, (PEERS, 24, D)), AXES, 0, 0, axis_...  42.1 us
    pallas_call x1, Pallas kernels, feed(): pl.pallas_call(feed_kernel, out_shape=(jax.ShapeDtypeStruct((ROWS, D), BF...  32.8 us
    pallas_call x1, Pallas kernels, attend_back(): pl.pallas_call(attend_back_kernel, out_shape=jax.ShapeDtypeStruct((ROWS,...  21.6 us
    pallas_call x1, Pallas kernels, attend(): pl.pallas_call(attend_kernel, out_shape=(jax.ShapeDtypeStruct((ROWS, D),...  20.9 us
    pallas_call x1, Pallas kernels, project_back(): pl.pallas_call(project_back_kernel, out_shape=(jax.ShapeDtypeStruct((ROWS...  16.8 us
    pallas_call x1, Pallas kernels, project(): pl.pallas_call(project_kernel, out_shape=(jax.ShapeDtypeStruct((2, ROWS,...  11.2 us
  transfers between devices with their start and end apart: 11, of which 6 were waited for; matrix products, arithmetic and copies ran while one was open for 1% of the time, Pallas kernels for 21%

profile of v1, /device:TPU:0, one launch (start us, length us, event | category | flops | bytes accessed | tf_op | source)
XLA Modules:
  0.0 357.4 jit_solution(9988464739291560261)
XLA Ops:
  7.2 0.0 all-gather.3.cloned.1.call-start
  7.2 1.6 copy.21.up_ref
  8.8 1.8 pack.1
  10.6 0.0 all-gather.3.cloned.1.call-update
  10.7 0.0 reduce-scatter.4.cloned.1.call-start
  10.7 75.1 %all-gather.3.cloned.1.call-done = bf16[4096,768]{1,0:T(8,128)(2,1)} async-done(((bf16[64,768]{1,0:T(8,128)(2,1)}), bf16[4096,768]{1,0:T(8,128)(2,1)}) %all-gather.3.cloned.1.call-update) | async-done | bytes 6291472 | tf_op jit(solution)/shard_map/all_gather | solution.py:733
  85.8 0.0 collective-permute-start.1
  85.8 0.9 broadcast_in_dim.19
  86.7 42.1 %all_to_all.10.own_ref = bf16[64,24,768]{2,1,0:T(8,128)(2,1)S(1)} all-to-all(bf16[64,24,768]{2,1,0:T(8,128)(2,1)S(1)} %broadcast_in_dim.19), channel_id=1, replica_groups={{0,64,4,68,16,80,20,84,32,96,36,100,48,112,52,116,1,65,5,69,17,81,21,85..., dimensions={0} | all-to-all | bytes 4718592 | tf_op jit(solution)/shard_map/all_to_all | solution.py:734
  128.8 0.0 copy-start.1
  128.8 0.0 collective-permute-start
  128.8 4.7 %collective-permute-done.oth_ref = bf16[64,24,768]{2,1,0:T(8,128)(2,1)} collective-permute-done((bf16[64,24,768]{2,1,0:T(8,128)(2,1)S(1)}, bf16[64,24,768]{2,1,0:T(8,128)(2,1)}, u32[]{:S(2)}, u32[]{:S(2)}) %collective-permute-start) | collective-permute-done | bytes 2359328 | tf_op jit(solution)/shard_map/ppermute | solution.py:737
  133.4 0.0 copy-done.1
  133.4 11.2 %project.1 = (bf16[2,512,512]{2,1,0:T(8,128)(2,1)}, bf16[512,2304]{1,0:T(8,128)(2,1)}, bf16[2,3,512,768]{3,2,1,0:T(8,128)(2,1)}, f32[8,768]{1,0:T(8,128)}) custom-call(s32[1,1]{1,0:T(1,128)} %bitcast.core_ref, bf16[512,768]{1,0:T(8,128)(2,1)} %x_ref.5, bf16[64,24,768]{2,1,0:T(8,128)(2,1)} %copy-done.1, bf16[64,24,768]{2,1,0:T(8,128)(2,1)} %collective-permute-done.oth_ref), custom_call_target="tpu_custom_call" | custom-call | tf_op jit(solution)/shard_map/project/pallas_call | solution.py:240
  144.7 20.9 %attend.1 = (bf16[512,768]{1,0:T(8,128)(2,1)}, f32[512,512]{1,0:T(8,128)}, f32[6,512,128]{2,1,0:T(8,128)}) custom-call(s32[1,4]{1,0:T(1,128)} %lens_ref.5, bf16[512,2304]{1,0:T(8,128)(2,1)} %get-tuple-element.41.qkv_ref), custom_call_target="tpu_custom_call" | custom-call | tf_op jit(solution)/shard_map/attend/pallas_call | solution.py:316
  165.6 0.0 collective-permute-done.1.oth_ref
  165.6 32.8 %feed.1 = (bf16[512,768]{1,0:T(8,128)(2,1)}, f32[512,768]{1,0:T(8,128)}, bf16[512,768]{1,0:T(8,128)(2,1)}, f32[8,768]{1,0:T(8,128)}, bf16[64,32,768]{2,1,0:T(8,1...) custom-call(s32[1,1]{1,0:T(1,128)} %bitcast.core_ref, ...), custom_call_target="tpu_custom_call" | custom-call | tf_op jit(solution)/shard_map/feed/pallas_call | solution.py:561
  198.4 0.2 collective-permute-start.3
  198.6 0.4 collective-permute-start.4
  199.0 0.1 collective-permute-start.5
  199.2 8.6 %collective-permute-done.5.c1 = bf16[64,8,768]{2,1,0:T(8,128)(2,1)S(1)} collective-permute-done((bf16[64,8,768]{2,1,0:T(8,128)(2,1)}, bf16[64,8,768]{2,1,0:T(8,128)(2,1)S(1)}, u32[]{:S(2)}, u32[]{:S(2)}) %collective-permute-start.5) | collective-permute-done | bytes 786464 | tf_op jit(solution)/shard_map/ppermute | solution.py:744
  207.8 0.0 collective-permute-done.4.b1
  207.8 0.0 collective-permute-done.3.a1
  207.8 0.0 copy-start.2
  207.8 0.9 copy-done.4
  208.6 0.5 copy-done.3
  209.2 1.1 copy-done.2
  210.2 8.8 %join.1 = bf16[64,56,768]{2,1,0:T(8,128)(2,1)} custom-call(bf16[64,32,768]{2,1,0:T(8,128)(2,1)} %get-tuple-element.59.a0, bf16[64,16,768]{2,1,0:T(8,128)(2,1)} %get-tuple-element.60.b0, bf16[64,8,768]{2,1,0:T(8,128)(2,1)} %get-tuple-element.61.c0, bf16[64,32,768]{2,1,0:T(8,128)(2,1)} %copy-done.2, bf16[64,16,768]{2,1,0:T(8,128)(2,1)} %copy-done.3, ...), custom_call_target="tpu_custom_call" | custom-call | tf_op jit(solution)/shard_map/join/pallas_call | solution.py:660
  219.0 0.0 reduce-scatter.4.cloned.1.call-update
  219.1 0.0 reduce-scatter.6.cloned.1.call-start
  219.1 21.6 %attend_back.1.dqkv_ref = bf16[512,2304]{1,0:T(8,128)(2,1)} custom-call(s32[1,4]{1,0:T(1,128)} %lens_ref.5, bf16[512,2304]{1,0:T(8,128)(2,1)} %get-tuple-element.41.qkv_ref, bf16[512,768]{1,0:T(8,128)(2,1)} %get-tuple-element.48.up_ref, f32[512,512]{1,0:T(8,128)} %get-tuple-element.49.pen_ref, f32[6,512,128]{2,1,0:T(8,128)} %get-tuple-element.50.lse_ref), custom_call_target="tpu_custom_call" | custom-call | tf_op jit(solution)/shard_map/attend_back/pallas_call | solution.py:414
  240.7 16.8 %project_back.1 = (bf16[512,768]{1,0:T(8,128)(2,1)}, bf16[64,24,768]{2,1,0:T(8,128)(2,1)}, bf16[64,24,768]{2,1,0:T(8,128)(2,1)}) custom-call(s32[1,1]{1,0:T(1,128)} %bitcast.core_ref, bf16[512,768]{1,0:T(8,128)(2,1)} %x_ref.5, f32[512,768]{1,0:T(8,128)} %get-tuple-element.45.dx_ref, bf16[2,512,512]{2,1,0:T(8,128)(2,1)} %get-tuple-element.46.h_ref, ...), custom_call_target="tpu_custom_call" | custom-call | tf_op jit(solution)/shard_map/project_back/pallas_call | solution.py:638
  257.5 0.2 collective-permute-start.2
  257.7 15.5 %reduce-scatter.4.cloned.1.call-done = bf16[896,768]{1,0:T(8,128)(2,1)} async-done(((bf16[3584,768]{1,0:T(8,128)(2,1)}), bf16[896,768]{1,0:T(8,128)(2,1)}) %reduce-scatter.4.cloned.1.call-update) | async-done | bytes 1376272 | tf_op jit(solution)/shard_map/reduce_scatter | solution.py:747
  273.2 0.0 reduce-scatter.6.cloned.1.call-update
  273.2 0.0 collective-permute-done.2
  273.2 3.7 %add_convert_fusion = bf16[64,24,768]{2,1,0:T(8,128)(2,1)} fusion(bf16[64,24,768]{2,1,0:T(8,128)(2,1)S(1)} %collective-permute-done.2, bf16[64,24,768]{2,1,0:T(8,128)(2,1)} %get-tuple-element.54), kind=kLoop, calls=%fused_computation | loop fusion | flops 4718592 | bytes 7077888 | tf_op jit(solution)/shard_map/convert_element_type | solution.py:755
  276.9 8.6 %all-to-all-start.1 = ((bf16[64,24,768]{2,1,0:T(8,128)(2,1)}), bf16[64,24,768]{2,1,0:T(8,128)(2,1)S(1)}, u32[]{:S(2)}, u32[]{:S(2)}) async-start(bf16[64,24,768]{2,1,0:T(8,128)(2,1)} %add_convert_fusion), calls=%async_computation.1 | async-start | bytes 4718592 | tf_op jit(solution)/shard_map/all_to_all | solution.py:756
  285.5 0.0 reduce-scatter.8.cloned.1.call-start
  285.5 38.7 %reduce-scatter.6.cloned.1.call-done = bf16[224,768]{1,0:T(8,128)(2,1)} async-done(((bf16[896,768]{1,0:T(8,128)(2,1)}), bf16[224,768]{1,0:T(8,128)(2,1)}) %reduce-scatter.6.cloned.1.call-update) | async-done | bytes 344080 | tf_op jit(solution)/shard_map/reduce_scatter | solution.py:747
  324.3 0.0 reduce-scatter.8.cloned.1.call-update
  324.3 0.0 all-to-all-done.1.early_ref
  324.3 0.0 copy-start
  324.3 1.4 copy-done
  325.8 2.8 finish.1
  328.6 18.7 %reduce-scatter.8.cloned.1.call-done.late_ref = bf16[56,768]{1,0:T(8,128)(2,1)} async-done(((bf16[224,768]{1,0:T(8,128)(2,1)}), bf16[56,768]{1,0:T(8,128)(2,1)}) %reduce-scatter.8.cloned.1.call-update) | async-done | bytes 86032 | tf_op jit(solution)/shard_map/reduce_scatter | solution.py:747
  347.3 1.8 unpack.1
  349.1 1.8 copy.22
  (2 shorter events, 0.0 us)
Async XLA Ops:
  7.2 78.6 %all-gather.3.cloned.1.call-start = ((), (), s32[]{:S(2)}) async-start(), calls=%async_computation.8 | async-start | bytes 6389760 | tf_op jit(solution)/shard_map/all_gather | solution.py:733
  10.7 262.5 %reduce-scatter.4.cloned.1.call-start = ((), (), s32[]{:S(2)}) async-start(), calls=%async_computation.5 | async-start | bytes 6881280 | tf_op jit(solution)/shard_map/reduce_scatter | solution.py:747
  85.8 79.8 %collective-permute-start.1 = (bf16[64,64,768]{2,1,0:T(8,128)(2,1)}, bf16[64,64,768]{2,1,0:T(8,128)(2,1)}, u32[]{:S(2)}, u32[]{:S(2)}) collective-permute-start(bf16[64,64,768]{2,1,0:T(8,128)(2,1)} %bitcast.12), channel_id=1, source_target_pairs={{0,8},{8,0},{1,9},{9,1},{2,10},{10,2},{3,11},{11,3},{16,24},{24,16... | collective-permute-start | bytes 18874376 | tf_op jit(solution)/shard_map/ppermute | solution.py:740
  128.8 4.7 %copy-start.1 = (bf16[64,24,768]{2,1,0:T(8,128)(2,1)}, bf16[64,24,768]{2,1,0:T(8,128)(2,1)S(1)}, u32[]{:S(2)}) copy-start(bf16[64,24,768]{2,1,0:T(8,128)(2,1)S(1)} %all_to_all.10.own_ref) | copy-start | bytes 7077892
  128.8 4.7 %collective-permute-start = (bf16[64,24,768]{2,1,0:T(8,128)(2,1)S(1)}, bf16[64,24,768]{2,1,0:T(8,128)(2,1)}, u32[]{:S(2)}, u32[]{:S(2)}) collective-permute-start(bf16[64,24,768]{2,1,0:T(8,128)(2,1)S(1)} %all_to_all.10.own_ref), channel_id=1, source_target_pairs={{0,8},{8,0},{1,9},{9,1},{2,10},{10,2},{3,11},{11,3},{16,24},{24,16... | collective-permute-start | bytes 7077896 | tf_op jit(solution)/shard_map/ppermute | solution.py:737
  198.4 9.3 %collective-permute-start.3 = (bf16[64,32,768]{2,1,0:T(8,128)(2,1)}, bf16[64,32,768]{2,1,0:T(8,128)(2,1)S(1)}, u32[]{:S(2)}, u32[]{:S(2)}) collective-permute-start(bf16[64,32,768]{2,1,0:T(8,128)(2,1)} %get-tuple-element.62), channel_id=1, source_target_pairs={{0,8},{8,0},{1,9},{9,1},{2,10},{10,2},{3,11},{11,3},{16,24},{24,16... | collective-permute-start | bytes 9437192 | tf_op jit(solution)/shard_map/ppermute | solution.py:744
  198.6 9.1 %collective-permute-start.4 = (bf16[64,16,768]{2,1,0:T(8,128)(2,1)}, bf16[64,16,768]{2,1,0:T(8,128)(2,1)S(1)}, u32[]{:S(2)}, u32[]{:S(2)}) collective-permute-start(bf16[64,16,768]{2,1,0:T(8,128)(2,1)} %get-tuple-element.63), channel_id=1, source_target_pairs={{0,8},{8,0},{1,9},{9,1},{2,10},{10,2},{3,11},{11,3},{16,24},{24,16... | collective-permute-start | bytes 4718600 | tf_op jit(solution)/shard_map/ppermute | solution.py:744
  199.0 8.7 %collective-permute-start.5 = (bf16[64,8,768]{2,1,0:T(8,128)(2,1)}, bf16[64,8,768]{2,1,0:T(8,128)(2,1)S(1)}, u32[]{:S(2)}, u32[]{:S(2)}) collective-permute-start(bf16[64,8,768]{2,1,0:T(8,128)(2,1)} %get-tuple-element.64), channel_id=1, source_target_pairs={{0,8},{8,0},{1,9},{9,1},{2,10},{10,2},{3,11},{11,3},{16,24},{24,16... | collective-permute-start | bytes 2359304 | tf_op jit(solution)/shard_map/ppermute | solution.py:744
  207.8 0.9 copy-start.4
  207.8 1.4 copy-start.3
  207.8 2.5 copy-start.2
  219.1 105.2 %reduce-scatter.6.cloned.1.call-start = ((), (), s32[]{:S(2)}) async-start(), calls=%async_computation.6 | async-start | bytes 1720320 | tf_op jit(solution)/shard_map/reduce_scatter | solution.py:747
  257.5 15.7 %collective-permute-start.2 = (bf16[64,24,768]{2,1,0:T(8,128)(2,1)}, bf16[64,24,768]{2,1,0:T(8,128)(2,1)S(1)}, u32[]{:S(2)}, u32[]{:S(2)}) collective-permute-start(bf16[64,24,768]{2,1,0:T(8,128)(2,1)} %get-tuple-element.55), channel_id=1, source_target_pairs={{0,8},{8,0},{1,9},{9,1},{2,10},{10,2},{3,11},{11,3},{16,24},{24,16... | collective-permute-start | bytes 7077896 | tf_op jit(solution)/shard_map/ppermute | solution.py:754
  276.9 47.4 %all-to-all-start.1 = ((bf16[64,24,768]{2,1,0:T(8,128)(2,1)}), bf16[64,24,768]{2,1,0:T(8,128)(2,1)S(1)}, u32[]{:S(2)}, u32[]{:S(2)}) async-start(bf16[64,24,768]{2,1,0:T(8,128)(2,1)} %add_convert_fusion), calls=%async_computation.1 | async-start | bytes 4718592 | tf_op jit(solution)/shard_map/all_to_all | solution.py:756
  285.5 61.8 %reduce-scatter.8.cloned.1.call-start = ((), (), s32[]{:S(2)}) async-start(), calls=%async_computation.7 | async-start | bytes 430080 | tf_op jit(solution)/shard_map/reduce_scatter | solution.py:747
  324.3 1.4 copy-start
Sparse Core Ops, SparseCore 0:
  11.3 74.3 all-gather.2
  219.2 53.9 reduce-scatter.3
  275.6 48.6 reduce-scatter.5
  326.6 20.6 reduce-scatter.7

commit v2 on v1

v2 whole, which is shorter than its diff:
```python
import itertools

import jax
import jax.numpy as jnp
from jax import lax
from jax.experimental import pallas as pl
from jax.experimental.pallas import tpu as pltpu
from jax.sharding import PartitionSpec as P

BF = jnp.bfloat16
F32 = jnp.float32
I32 = jnp.int32
AXES = ("wide", "narrow")
D = 768
ROWS = 512
FF = 3072
OWN = 6
PEERS = 64
HALF = PEERS * OWN
BLOCKS = 6
OUTER = 3 * OWN * BLOCKS
GATHERED = OUTER + OWN * BLOCKS
EARLY = 152
LATE = 48
WHOLE = 336
TAIL = 112
STEP = TAIL + 1
WIDE = 128 * 8
EPS = 1e-05
FAR = 1e30
TANH_SCALE = 0.7978845608028654
TANH_CUBE = 0.044715
MIB = 1 << 20


def device_number(x, y, z, core):
    return ((x & 1) * 8 + y * 2 + core) * 8 + (x >> 1) * 4 + z


def peer_groups(dims):
    sizes = dict(x=4, y=4, z=4, c=2)
    rest = [name for name in "xyzc" if name not in dims]
    groups = []
    for fixed in itertools.product(*[range(sizes[name]) for name in rest]):
        members = []
        for moving in itertools.product(*[range(sizes[name]) for name in dims]):
            at = dict(zip(rest, fixed))
            at.update(zip(dims, moving))
            members.append(device_number(at["x"], at["y"], at["z"], at["c"]))
        groups.append(members)
    return groups


def core_pairs():
    return [
        (device_number(x, y, z, c), device_number(x, y, z, 1 - c))
        for x, y, z, c in itertools.product(range(4), range(4), range(4), range(2))
    ]


def dot_nn(left, right):
    return lax.dot_general(left, right, (((1,), (0,)), ((), ())), preferred_element_type=F32)


def dot_nt(left, right):
    return lax.dot_general(left, right, (((1,), (1,)), ((), ())), preferred_element_type=F32)


def dot_tn(left, right):
    return lax.dot_general(left, right, (((0,), (0,)), ((), ())), preferred_element_type=F32)


def iota(shape, dim):
    return lax.broadcasted_iota(I32, shape, dim)


def one_hot(mask):
    return jnp.where(mask, 1.0, 0.0).astype(BF)


def split_low(values):
    high = values.astype(BF)
    return high, (values - high.astype(F32)).astype(BF)


def owner(group, core, spot):
    y = group >> 4
    x = (group >> 2) & 3
    z = (spot[1] - (group & 3)) & 3
    return ((x & 1) << 6) + (y << 4) + (core << 3) + ((x >> 1) << 2) + z


def sixth(number):
    return (number * 43691) >> 18


def place_matrix(spot):
    slot = iota((1, D), 1)
    other = (slot >= HALF).astype(I32)
    inner = slot - HALF * other
    side = spot[0] + other - 2 * spot[0] * other
    feature = owner(inner & (PEERS - 1), side, spot) * OWN + (inner >> 6)
    return one_hot(iota((D, D), 0) == feature)


def place_transposed(spot):
    slot = iota((D, 1), 0)
    other = (slot >= HALF).astype(I32)
    inner = slot - HALF * other
    side = spot[0] + other - 2 * spot[0] * other
    feature = owner(inner & (PEERS - 1), side, spot) * OWN + (inner >> 6)
    return one_hot(iota((D, D), 1) == feature)


def late_owner(group):
    z = group >> 5
    c = (group >> 4) & 1
    y = (group >> 2) & 3
    x = group & 3
    return ((x & 1) << 6) + (y << 4) + (c << 3) + ((x >> 1) << 2) + z


def place_late():
    slot = iota((1, WIDE), 1)
    inner = slot & 7
    feature = jnp.where(inner < OWN, late_owner(slot >> 3) * OWN + inner, -1)
    return one_hot(iota((D, WIDE), 0) == feature)


def vector_lanes(which):
    feature = iota((1, D), 1)
    lane = which * OWN + feature - OWN * sixth(feature)
    return one_hot(iota((128, D), 0) == lane)


def owned_features(core, spot):
    return owner(iota((PEERS, 1), 0), core, spot) == sixth(iota((1, D), 1))


def unpack_vector(packed, mine, which):
    spread = dot_nn(packed.astype(BF), vector_lanes(which))
    return jnp.sum(jnp.where(mine, spread, 0.0), axis=0, keepdims=True)


def pack_vectors(vectors, core, spot):
    mine = owned_features(core, spot)
    total = jnp.zeros((PEERS, 128), F32)
    for which, vector in enumerate(vectors):
        spread = jnp.where(mine, vector, 0.0).astype(BF)
        total = total + dot_nt(spread, vector_lanes(which))
    return total


def norm_stats(values):
    center = values - jnp.mean(values, axis=-1, keepdims=True)
    inverse = lax.rsqrt(jnp.mean(center * center, axis=-1, keepdims=True) + EPS)
    return center * inverse, inverse


def norm_pull(gradient, unit, inverse, gain):
    scaled = gradient * gain
    return inverse * (
        scaled
        - jnp.mean(scaled, axis=-1, keepdims=True)
        - unit * jnp.mean(scaled * unit, axis=-1, keepdims=True)
    )


def group_ends(lens_ref):
    ends = []
    total = 0
    for slot in range(4):
        total = total + lens_ref[0, slot]
        ends.append(total)
    return ends


def segments(positions, ends):
    return sum((positions >= end).astype(I32) for end in ends)


VM = pl.BlockSpec(memory_space=pltpu.VMEM)
SM = pl.BlockSpec(memory_space=pltpu.SMEM)
ANY = pl.BlockSpec(memory_space=pl.ANY)
OUT_WEIGHT = pl.BlockSpec((D, D), lambda i: (0, 3), memory_space=pltpu.VMEM)


def params(limit=60):
    return pltpu.CompilerParams(vmem_limit_bytes=limit * MIB)


def pack_kernel(
    g1_ref, b1_ref, qkv_ref, out_ref, g2_ref, b2_ref, up_ref, down_ref, early_ref, late_ref, es
):
    es[...] = jnp.zeros_like(es)
    qkv = qkv_ref[...].astype(F32)
    out = out_ref[...].astype(F32)
    for pair in range(BLOCKS):
        for part in range(3):
            start = (pair * 3 + part) * OWN
            es[start : start + OWN, :] = qkv[:, part * D + pair * 128 : part * D + pair * 128 + 128]
        start = OUTER + pair * OWN
        es[start : start + OWN, :] = out[:, pair * 128 : pair * 128 + 128]
    for which, ref in enumerate((g1_ref, b1_ref, g2_ref, b2_ref)):
        es[GATHERED : GATHERED + 1, which * OWN : which * OWN + OWN] = ref[...].astype(F32)
    early_ref[...] = es[...].astype(BF)
    up = up_ref[...].astype(F32)
    down = down_ref[...].astype(F32)
    late_ref[...] = jnp.concatenate([up[0:16], down[0:16], up[16:24], down[16:24]], axis=0).astype(BF)


def pack(g1, b1, qkv, out, g2, b2, up, down):
    return pl.pallas_call(
        pack_kernel,
        out_shape=(
            jax.ShapeDtypeStruct((EARLY, 128), BF),
            jax.ShapeDtypeStruct((LATE, D), BF),
        ),
        in_specs=[VM] * 8,
        out_specs=(VM, VM),
        scratch_shapes=[pltpu.VMEM((EARLY, 128), F32)],
        compiler_params=params(),
        name="pack",
    )(g1[None], b1[None], qkv, out, g2[None], b2[None], up, down)


def project_kernel(spot_ref, x_ref, own_ref, oth_ref, ht_ref, qkv_ref, w_ref, ln_ref, hs, rows_s):
    spot = (spot_ref[0, 0], spot_ref[0, 1])
    core = spot[0]
    vectors = [jnp.zeros((1, D), F32) for _ in range(4)]
    for half, source in enumerate((own_ref, oth_ref)):
        side = core if half == 0 else 1 - core

        @pl.loop(0, 8)
        def _(block):
            start = pl.multiple_of(block * (8 * EARLY), 8 * EARLY)
            values = source[pl.ds(block * 8, 8)].astype(F32)
            rows_s[pl.ds(start, 8 * EARLY), :] = values.reshape(8 * EARLY, 128)

        for block in range(4 * BLOCKS):
            for row in range(OWN):
                to = half * HALF + row * PEERS
                w_ref[to : to + PEERS, block * 128 : block * 128 + 128] = rows_s[
                    pl.ds(block * OWN + row, PEERS, stride=EARLY), :
                ].astype(BF)
        packed = rows_s[pl.ds(GATHERED, PEERS, stride=EARLY), :]
        mine = owned_features(side, spot)
        vectors = [
            vector + unpack_vector(packed, mine, which) for which, vector in enumerate(vectors)
        ]
    for which, vector in enumerate(vectors):
        ln_ref[which : which + 1, :] = vector
    ln_ref[4:8, :] = jnp.zeros((4, D), F32)

    @pl.loop(0, 4)
    def _(block):
        rows = pl.ds(pl.multiple_of(block * 128, 128), 128)
        unit, _ = norm_stats(x_ref[rows, :].astype(F32))
        hs[rows, :] = (unit * ln_ref[0:1, :] + ln_ref[1:2, :]).astype(BF)

    placed = dot_nn(hs[...], place_matrix(spot)).astype(BF)
    for part in range(3):
        columns = slice(part * D, part * D + D)
        qkv_ref[:, columns] = dot_nn(placed, w_ref[:, columns]).astype(BF)
    ht_ref[...] = dot_nt(place_transposed(spot), hs[...]).astype(BF)


def project(spot, x, own, oth):
    return pl.pallas_call(
        project_kernel,
        out_shape=(
            jax.ShapeDtypeStruct((D, ROWS), BF),
            jax.ShapeDtypeStruct((ROWS, 3 * D), BF),
            jax.ShapeDtypeStruct((D, 4 * D), BF),
            jax.ShapeDtypeStruct((8, D), F32),
        ),
        in_specs=[SM, VM, VM, VM],
        out_specs=(VM, VM, VM, VM),
        scratch_shapes=[pltpu.VMEM((ROWS, D), BF), pltpu.VMEM((PEERS * EARLY, 128), F32)],
        compiler_params=params(),
        name="project",
    )(spot, x, own, oth)


def softplus4(logits):
    sharp = 4.0 * logits
    return 0.25 * (jnp.maximum(sharp, 0.0) + jnp.log(1.0 + jnp.exp(-jnp.abs(sharp))))


def block_masks(block, ends):
    count = (block + 1) * 128
    query = iota((1, 128), 1) + block * 128
    key = iota((count, 1), 0)
    same = segments(key, ends) == segments(query, ends)
    first = key == 0
    for end in ends:
        first = first | (key == end)
    allowed = same & (key <= query)
    chosen = same & (key < query) & jnp.logical_not(first)
    return allowed, chosen


def twice(values):
    return jnp.concatenate([values, values], axis=1)


def side_by_side(values):
    left = iota((1, 128), 1) < 64
    zero = jnp.zeros((), BF)
    return jnp.concatenate([jnp.where(left, values, zero), jnp.where(left, zero, values)], axis=0)


def own_halves(values):
    return jnp.concatenate([values[0:64, 0:128], values[64:128, 128:256]], axis=0)


def lanes_of(pair, part):
    return pl.ds(pl.multiple_of(pair * 384 + part * 128, 128), 128)


def attend_kernel(
    spot_ref, lens_ref, x_ref, qkv_ref, wo_ref, ln_ref, mixed_ref, middle_ref, h_ref, pen_ref, lse_ref, attn_s, carry
):
    ends = group_ends(lens_ref)
    scale = jnp.asarray(0.125, BF)
    row, column = iota((128, 256), 0), iota((128, 256), 1)
    before = one_hot((row < column) | (column >= 128))
    carry[...] = jnp.zeros_like(carry)
    k0 = qkv_ref[:, 128:256]
    for block in range(4):
        count = (block + 1) * 128
        rows = slice(block * 128, count)
        q0 = side_by_side(qkv_ref[rows, 0:128] * scale)[0:128]
        allowed, chosen = block_masks(block, ends)
        picked = jnp.where(chosen, softplus4(dot_nt(k0[:count], q0)), 0.0)
        high, low = split_low(picked)
        sums = dot_nn(high, before) + dot_nn(low, before)
        pen_ref[:count, rows] = jnp.where(allowed, sums[:, 0:128] + carry[:count, :], FAR)
        carry[:count, :] = carry[:count, :] + sums[:, 128:256]

    @pl.loop(0, 6)
    def _(pair):
        lanes = pl.ds(pl.multiple_of(pair * 128, 128), 128)
        k = qkv_ref[:, lanes_of(pair, 1)]
        v = qkv_ref[:, lanes_of(pair, 2)]
        for block in range(4):
            count = (block + 1) * 128
            rows = slice(block * 128, count)
            q = side_by_side(qkv_ref[rows, lanes_of(pair, 0)] * scale)
            shifted = dot_nt(k[:count], q) - twice(pen_ref[:count, rows])
            top = jnp.max(shifted, axis=0, keepdims=True)
            exponent = jnp.exp(shifted - top)
            total = jnp.sum(exponent, axis=0, keepdims=True)
            mixed = dot_tn(v[:count], exponent.astype(BF)) * (1.0 / total)
            attn_s[lanes, rows] = own_halves(mixed).astype(BF)
            log_total = top + jnp.log(total)
            lse_ref[pair, 0:1, rows] = log_total[:, 0:128]
            lse_ref[pair, 1:2, rows] = log_total[:, 128:256]

    mixed_ref[...] = dot_tn(attn_s[...], place_late()).astype(BF)
    mixed = dot_tn(attn_s[...], place_matrix((spot_ref[0, 0], spot_ref[0, 1]))).astype(BF)
    middle_ref[...] = dot_nn(mixed, wo_ref[...])

    @pl.loop(0, 4)
    def _(block):
        rows = pl.ds(pl.multiple_of(block * 128, 128), 128)
        middle = x_ref[rows, :].astype(F32) + middle_ref[rows, :]
        middle_ref[rows, :] = middle
        unit, _ = norm_stats(middle)
        h_ref[rows, :] = (unit * ln_ref[2:3, :] + ln_ref[3:4, :]).astype(BF)


def attend(spot, lens, x, qkv, weights, ln):
    return pl.pallas_call(
        attend_kernel,
        grid=(1,),
        out_shape=(
            jax.ShapeDtypeStruct((ROWS, WIDE), BF),
            jax.ShapeDtypeStruct((ROWS, D), F32),
            jax.ShapeDtypeStruct((ROWS, D), BF),
            jax.ShapeDtypeStruct((ROWS, ROWS), F32),
            jax.ShapeDtypeStruct((6, 8, ROWS), F32),
        ),
        in_specs=[SM, SM, VM, VM, OUT_WEIGHT, VM],
        out_specs=(VM,) * 5,
        scratch_shapes=[pltpu.VMEM((D, ROWS), BF), pltpu.VMEM((ROWS, 128), F32)],
        compiler_params=params(),
        name="attend",
    )(spot, lens, x, qkv, weights, ln)


def back_pair(pair, qkv, up, pen, lse, total, grads, kept, dk_acc, dv_acc):
    scale = jnp.asarray(0.125, BF)
    k = qkv[:, lanes_of(pair, 1)]
    v = qkv[:, lanes_of(pair, 2)]
    dv_acc[...] = jnp.zeros_like(dv_acc)
    dk_acc[...] = jnp.zeros_like(dk_acc)
    for block in range(4):
        count = (block + 1) * 128
        rows = slice(block * 128, count)
        q = side_by_side(qkv[rows, lanes_of(pair, 0)] * scale)
        u = side_by_side(up[rows, pl.ds(pl.multiple_of(pair * 128, 128), 128)])
        log_total = jnp.concatenate([lse[pair, 0:1, rows], lse[pair, 1:2, rows]], axis=1)
        soft = jnp.exp(dot_nt(k[:count], q) - twice(pen[:count, rows]) - log_total)
        pulled = dot_nt(v[:count], u)
        inner = jnp.sum(pulled * soft, axis=0, keepdims=True)
        dz = soft * (pulled - inner)
        total[:count, rows] = total[:count, rows] + (dz[:, 0:128] + dz[:, 128:256])
        dv_acc[:count, :] = dv_acc[:count, :] + dot_nn(soft.astype(BF), u)
        if kept is not None:
            kept[block, :count, :] = dz
        else:
            low = dz.astype(BF)
            dk_acc[:count, :] = dk_acc[:count, :] + dot_nn(low, q)
            dq = (own_halves(dot_tn(k[:count], low)) * 0.125).T
            grads[rows, lanes_of(pair, 0)] = dq.astype(BF)
    grads[:, lanes_of(pair, 2)] = dv_acc[...].astype(BF)
    if kept is None:
        grads[:, lanes_of(pair, 1)] = dk_acc[...].astype(BF)


def back_first(ends, qkv, total, grads, kept, dk_acc, carry):
    scale = jnp.asarray(0.125, BF)
    k = qkv[:, 128:256]
    row, column = iota((128, 256), 0), iota((128, 256), 1)
    after = one_hot((row > column) | (column >= 128))
    carry[...] = jnp.zeros_like(carry)
    for block in (3, 2, 1, 0):
        count = (block + 1) * 128
        rows = slice(block * 128, count)
        q = side_by_side(qkv[rows, 0:128] * scale)
        _, chosen = block_masks(block, ends)
        high, low = split_low(total[:count, rows])
        sums = dot_nn(high, after) + dot_nn(low, after)
        picked = sums[:, 0:128] + carry[:count, :]
        carry[:count, :] = carry[:count, :] + sums[:, 128:256]
        slope = 1.0 / (1.0 + jnp.exp(-4.0 * dot_nt(k[:count], q[0:128])))
        first = kept[block, :count, 0:128] - jnp.where(chosen, slope * picked, 0.0)
        low = jnp.concatenate([first, kept[block, :count, 128:256]], axis=1).astype(BF)
        dk_acc[:count, :] = dk_acc[:count, :] + dot_nn(low, q)
        grads[rows, 0:128] = (own_halves(dot_tn(k[:count], low)) * 0.125).T.astype(BF)
    grads[:, 128:256] = dk_acc[...].astype(BF)


def put_rows(rows_s, piece, start):
    for row in range(OWN):
        rows_s[pl.ds(start + row, PEERS, stride=STEP), :] = piece[
            row * PEERS : row * PEERS + PEERS
        ]


def back_kernel(
    spot_ref, lens_ref, x_ref, up, vec_ref,
    qkv_hbm, pen_hbm, lse_hbm, w_hbm, ht_hbm,
    oth_ref, own_ref, dh_one_ref,
    qkv, pen, lse, w, ht,
    total, kept, grads, dk_acc, dv_acc, carry, dh_s, vec_s, rows_s, slab_s, sems, out_sems,
):
    spot = (spot_ref[0, 0], spot_ref[0, 1])
    core = spot[0]
    ends = group_ends(lens_ref)
    loads = [
        pltpu.make_async_copy(source, target, sems.at[number])
        for number, (source, target) in enumerate(
            ((qkv_hbm, qkv), (pen_hbm, pen), (lse_hbm, lse), (w_hbm.at[:, 0 : 3 * D], w), (ht_hbm, ht))
        )
    ]
    for load in loads:
        load.start()
    total[...] = jnp.zeros_like(total)
    vec_s[...] = vec_ref[...]
    for load in loads[0:3]:
        load.wait()

    @pl.loop(1, 6)
    def _(pair):
        back_pair(pair, qkv, up, pen, lse, total, grads, None, dk_acc, dv_acc)

    back_pair(0, qkv, up, pen, lse, total, grads, kept, dk_acc, dv_acc)
    back_first(ends, qkv, total, grads, kept, dk_acc, carry)
    for load in loads[3:]:
        load.wait()
    high, low = split_low(dot_nt(grads[...], w[...]))
    place = place_matrix(spot)
    dh_s[...] = dot_nt(high, place) + dot_nt(low, place)

    @pl.loop(0, 4)
    def _(block):
        rows = pl.ds(pl.multiple_of(block * 128, 128), 128)
        unit, _ = norm_stats(x_ref[rows, :].astype(F32))
        gradient = dh_s[rows, :]
        vec_s[0:1, :] = vec_s[0:1, :] + jnp.sum(gradient * unit, axis=0, keepdims=True)
        vec_s[1:2, :] = vec_s[1:2, :] + jnp.sum(gradient, axis=0, keepdims=True)

    store_dh = pltpu.make_async_copy(dh_s, dh_one_ref, out_sems.at[2])
    store_dh.start()
    vectors = [vec_s[which : which + 1, :] for which in range(4)]
    stores = [store_dh]
    for half, target in ((1, oth_ref), (0, own_ref)):
        side = core if half == 0 else 1 - core
        slots = slice(half * HALF, half * HALF + HALF)
        for part in range(3):
            piece = dot_nn(ht[slots, :], grads[:, part * D : part * D + D])
            for block in range(BLOCKS):
                start = (part * BLOCKS + block) * OWN
                put_rows(rows_s, piece[:, block * 128 : block * 128 + 128], start)
        rows_s[pl.ds(OUTER, PEERS, stride=STEP), :] = pack_vectors(vectors, side, spot)

        @pl.loop(0, 8)
        def _(block):
            for peer in range(8):
                start = (block * 8 + peer) * STEP
                slab_s[half, block * 8 + peer] = rows_s[pl.ds(start, TAIL), :].astype(BF)

        store = pltpu.make_async_copy(slab_s.at[half], target, out_sems.at[half])
        store.start()
        stores.append(store)
    for store in stores:
        store.wait()


def back(spot, lens, x, up, vec, qkv, pen, lse, weights, ht):
    slab = jax.ShapeDtypeStruct((PEERS, TAIL, 128), BF)
    return pl.pallas_call(
        back_kernel,
        out_shape=(slab, slab, jax.ShapeDtypeStruct((ROWS, D), F32)),
        in_specs=[SM, SM] + [VM] * 3 + [ANY] * 5,
        out_specs=(ANY,) * 3,
        scratch_shapes=[
            pltpu.VMEM((ROWS, 3 * D), BF),
            pltpu.VMEM((ROWS, ROWS), F32),
            pltpu.VMEM((6, 8, ROWS), F32),
            pltpu.VMEM((D, 3 * D), BF),
            pltpu.VMEM((D, ROWS), BF),
            pltpu.VMEM((ROWS, ROWS), F32),
            pltpu.VMEM((4, ROWS, 256), F32),
            pltpu.VMEM((ROWS, 3 * D), BF),
            pltpu.VMEM((ROWS, 128), F32),
            pltpu.VMEM((ROWS, 128), F32),
            pltpu.VMEM((ROWS, 128), F32),
            pltpu.VMEM((ROWS, D), F32),
            pltpu.VMEM((8, D), F32),
            pltpu.VMEM((PEERS * STEP, 128), F32),
            pltpu.VMEM((2, PEERS, TAIL, 128), BF),
            pltpu.SemaphoreType.DMA((5,)),
            pltpu.SemaphoreType.DMA((3,)),
        ],
        compiler_params=params(),
        name="back",
    )(spot, lens, x, up, vec, qkv, pen, lse, weights, ht)


def feed_kernel(
    spot_ref, lens_ref, middle_ref, h_ref, mixed_ref, wo_ref, ln_ref, cot_ref, late_ref,
    y_ref, grad_ref, dx_ref, up_ref, vec_ref,
    up_s, down_s, mid_s, gup_s, gdown_s, gout_s, dy_s, h_s, acc_s, dh_ref, sems, out_sems,
):
    def load_up(chunk):
        devices = pl.ds(chunk * 32, 32)
        return pltpu.make_async_copy(late_ref.at[devices, 0:16, :], up_s.at[chunk], sems.at[chunk])

    def load_down(chunk):
        devices = pl.ds(chunk * 32, 32)
        return pltpu.make_async_copy(
            late_ref.at[devices, 16:32, :], down_s.at[chunk], sems.at[4 + chunk]
        )

    def load_mid(half):
        devices = pl.ds(half * 64, 64)
        return pltpu.make_async_copy(
            late_ref.at[devices, 32:48, :], mid_s.at[half], sems.at[8 + half]
        )

    def store_big(chunk, block):
        devices = pl.ds(chunk * 32, 32)
        lanes = slice(block * 128, block * 128 + 128)
        return [
            pltpu.make_async_copy(
                grads.at[chunk, :, :, lanes],
                grad_ref.at[devices, block * 48 + offset : block * 48 + offset + 16, :],
                out_sems.at[chunk],
            )
            for grads, offset in ((gup_s, 0), (gdown_s, 16))
        ]

    def store_mid(half, block):
        devices = pl.ds(half * 64, 64)
        lanes = slice(block * 128, block * 128 + 128)
        return pltpu.make_async_copy(
            mid_s.at[half, :, :, lanes],
            grad_ref.at[devices, block * 48 + 32 : block * 48 + 48, :],
            out_sems.at[4 + half],
        )

    for chunk in range(4):
        load_up(chunk).start()
        load_down(chunk).start()
    for half in range(2):
        load_mid(half).start()
    ends = group_ends(lens_ref)
    gain = ln_ref[2:3, :]
    vec_ref[...] = jnp.zeros_like(vec_ref)

    @pl.loop(0, 4)
    def _(block):
        rows = pl.ds(pl.multiple_of(block * 128, 128), 128)
        acc_s[rows, :] = middle_ref[rows, :]
        live = (iota((128, 1), 0) + block * 128) < ends[3]
        dy_s[rows, :] = jnp.where(live, cot_ref[rows, :].astype(F32), 0.0).astype(BF)
        dh_ref[rows, :] = jnp.zeros((128, D), F32)

    def both_ways(up, down):
        value = dot_nt(h_ref[...], up)
        square = value * value
        bend = jnp.tanh(TANH_SCALE * (value + TANH_CUBE * (value * square)))
        act = (0.5 * value * (1.0 + bend)).astype(BF)
        slope = 0.5 * (1.0 + bend) + (0.5 * TANH_SCALE) * value * (1.0 - bend * bend) * (
            1.0 + 3.0 * TANH_CUBE * square
        )
        pulled = (dot_nt(dy_s[...], down) * slope).astype(BF)
        acc_s[...] = acc_s[...] + dot_nn(act, down)
        dh_ref[...] = dh_ref[...] + dot_nn(pulled, up)
        return dot_tn(pulled, h_ref[...]), dot_tn(act, dy_s[...])

    @pl.loop(0, 4)
    def _(chunk):
        load_up(chunk).wait()
        load_down(chunk).wait()
        up_grad, down_grad = both_ways(
            up_s[chunk].reshape(ROWS, D), down_s[chunk].reshape(ROWS, D)
        )
        gup_s[chunk] = up_grad.astype(BF).reshape(32, 16, D)
        gdown_s[chunk] = down_grad.astype(BF).reshape(32, 16, D)
        for block in range(BLOCKS):
            for copy in store_big(chunk, block):
                copy.start()

    @pl.loop(0, 2)
    def _(half):
        load_mid(half).wait()
        mid = mid_s[half].astype(F32)
        up_grad, down_grad = both_ways(
            mid[:, 0:8, :].reshape(ROWS, D).astype(BF), mid[:, 8:16, :].reshape(ROWS, D).astype(BF)
        )
        joined = jnp.concatenate(
            [up_grad.reshape(PEERS, 8, D), down_grad.reshape(PEERS, 8, D)], axis=1
        )
        mid_s[half] = joined.astype(BF)
        for block in range(BLOCKS):
            store_mid(half, block).start()

    @pl.loop(0, 4)
    def _(block):
        rows = pl.ds(pl.multiple_of(block * 128, 128), 128)
        y_ref[rows, :] = acc_s[rows, :].astype(BF)
        unit, inverse = norm_stats(middle_ref[rows, :])
        gradient = dh_ref[rows, :]
        vec_ref[2:3, :] = vec_ref[2:3, :] + jnp.sum(gradient * unit, axis=0, keepdims=True)
        vec_ref[3:4, :] = vec_ref[3:4, :] + jnp.sum(gradient, axis=0, keepdims=True)
        live = (iota((128, 1), 0) + block * 128) < ends[3]
        dy = jnp.where(live, cot_ref[rows, :].astype(F32), 0.0)
        moved = dy + norm_pull(gradient, unit, inverse, gain)
        dx_ref[rows, :] = moved
        h_s[rows, :] = moved.astype(BF)

    outer = dot_tn(mixed_ref[...], h_s[...])
    stores = []
    for block in range(0, BLOCKS, 2):
        pieces = [
            outer[:, at * 128 : at * 128 + 128].reshape(128, 8, 128) for at in (block, block + 1)
        ]
        gout_s[block // 2] = jnp.concatenate(pieces, axis=1).astype(BF)
        start = 288 + block * 8
        store = pltpu.make_async_copy(
            gout_s.at[block // 2], grad_ref.at[:, start : start + 16, :], out_sems.at[6 + block // 2]
        )
        store.start()
        stores.append(store)
    placed = dot_nt(h_s[...], wo_ref[...]).astype(BF)
    up_ref[...] = dot_nt(placed, place_matrix((spot_ref[0, 0], spot_ref[0, 1]))).astype(BF)
    for block in range(BLOCKS):
        for chunk in range(4):
            for copy in store_big(chunk, block):
                copy.wait()
        for half in range(2):
            store_mid(half, block).wait()
    for store in stores:
        store.wait()


def feed(spot, lens, middle, h, mixed, weights, ln, cot, late):
    return pl.pallas_call(
        feed_kernel,
        grid=(1,),
        out_shape=(
            jax.ShapeDtypeStruct((ROWS, D), BF),
            jax.ShapeDtypeStruct((128, WHOLE, 128), BF),
            jax.ShapeDtypeStruct((ROWS, D), F32),
            jax.ShapeDtypeStruct((ROWS, D), BF),
            jax.ShapeDtypeStruct((8, D), F32),
        ),
        in_specs=[SM, SM, VM, VM, VM, OUT_WEIGHT, VM, VM, ANY],
        out_specs=(VM, ANY, VM, VM, VM),
        scratch_shapes=[
            pltpu.VMEM((4, 32, 16, D), BF),
            pltpu.VMEM((4, 32, 16, D), BF),
            pltpu.VMEM((2, PEERS, 16, D), BF),
            pltpu.VMEM((4, 32, 16, D), BF),
            pltpu.VMEM((4, 32, 16, D), BF),
            pltpu.VMEM((3, 128, 16, 128), BF),
            pltpu.VMEM((ROWS, D), BF),
            pltpu.VMEM((ROWS, D), BF),
            pltpu.VMEM((ROWS, D), F32),
            pltpu.VMEM((ROWS, D), F32),
            pltpu.SemaphoreType.DMA((10,)),
            pltpu.SemaphoreType.DMA((9,)),
        ],
        compiler_params=params(),
        name="feed",
    )(spot, lens, middle, h, mixed, weights, ln, cot, late)


def norm_back_kernel(x_ref, dx_ref, dh_ref, ln_ref, dtok_ref):
    @pl.loop(0, 4)
    def _(block):
        rows = pl.ds(pl.multiple_of(block * 128, 128), 128)
        unit, inverse = norm_stats(x_ref[rows, :].astype(F32))
        moved = dx_ref[rows, :] + norm_pull(dh_ref[rows, :], unit, inverse, ln_ref[0:1, :])
        dtok_ref[rows, :] = moved.astype(BF)


def norm_back(x, dx, dh, ln):
    return pl.pallas_call(
        norm_back_kernel,
        out_shape=jax.ShapeDtypeStruct((ROWS, D), BF),
        in_specs=[VM] * 4,
        out_specs=VM,
        compiler_params=params(),
        name="norm_back",
    )(x, dx, dh, ln)


def finish_kernel(*refs):
    slabs, (qkv_ref, g1_ref, b1_ref, g2_ref, b2_ref), sum_s = refs[0:4], refs[4:9], refs[9]
    sum_s[...] = sum(slab[...].astype(F32) for slab in slabs)
    for pair in range(BLOCKS):
        for part in range(3):
            start = (pair * 3 + part) * OWN
            at = part * D + pair * 128
            qkv_ref[:, at : at + 128] = sum_s[start : start + OWN, :]
    for which, target in enumerate((g1_ref, b1_ref, g2_ref, b2_ref)):
        target[...] = sum_s[OUTER : OUTER + 1, which * OWN : which * OWN + OWN]


def finish(slabs):
    vector = jax.ShapeDtypeStruct((1, OWN), F32)
    return pl.pallas_call(
        finish_kernel,
        out_shape=(
            jax.ShapeDtypeStruct((OWN, 3 * D), F32),
            vector, vector, vector, vector,
        ),
        in_specs=[VM] * 4,
        out_specs=(VM,) * 5,
        scratch_shapes=[pltpu.VMEM((TAIL, 128), F32)],
        compiler_params=params(),
        name="finish",
    )(*slabs)


def unpack_kernel(late_ref, up_ref, down_ref, out_ref, sum_s):
    sum_s[...] = jnp.sum(late_ref[...].astype(F32), axis=0)
    for block in range(BLOCKS):
        lanes = slice(block * 128, block * 128 + 128)
        row = block * 48
        up_ref[0:16, lanes] = sum_s[row : row + 16, :]
        down_ref[0:16, lanes] = sum_s[row + 16 : row + 32, :]
        up_ref[16:24, lanes] = sum_s[row + 32 : row + 40, :]
        down_ref[16:24, lanes] = sum_s[row + 40 : row + 48, :]
        row = BLOCKS * 48 + block * 8
        out_ref[:, lanes] = sum_s[row : row + OWN, :]


def unpack(late):
    shard = jax.ShapeDtypeStruct((24, D), F32)
    return pl.pallas_call(
        unpack_kernel,
        out_shape=(shard, shard, jax.ShapeDtypeStruct((OWN, D), F32)),
        in_specs=[VM],
        out_specs=(VM, VM, VM),
        scratch_shapes=[pltpu.VMEM((WHOLE, 128), F32)],
        compiler_params=params(),
        name="unpack",
    )(late)


def fold_kernel(slabs_ref, *sums):
    for back, target in enumerate(sums):
        rows = slice(back * TAIL, back * TAIL + TAIL)
        target[...] = jnp.sum(slabs_ref[:, rows, :].astype(F32), axis=0).astype(BF)


def fold(slabs):
    piece = jax.ShapeDtypeStruct((TAIL, 128), BF)
    return pl.pallas_call(
        fold_kernel,
        out_shape=(piece,) * 4,
        in_specs=[VM],
        out_specs=(VM,) * 4,
        compiler_params=params(),
        name="fold",
    )(slabs)


def exchange(slabs, dims):
    return lax.all_to_all(slabs, AXES, 0, 0, axis_index_groups=peer_groups(dims), tiled=True)


def along_z(ahead):
    return [
        (device_number(x, y, z, c), device_number(x, y, (z + ahead) % 4, c))
        for x, y, z, c in itertools.product(range(4), range(4), range(4), range(2))
    ]


def copies_of_peers(own):
    ring = [own] + [lax.ppermute(own, AXES, along_z(ahead)) for ahead in (1, 2, 3)]
    ring = jnp.concatenate(ring, axis=0)
    return exchange(jnp.broadcast_to(ring, (16, *ring.shape)), "yx").reshape(PEERS, *own.shape)


def sum_over_peers(own, other):
    received = lax.ppermute(other, AXES, core_pairs())
    slab = (own.astype(F32) + received.astype(F32)).astype(BF)
    pieces = fold(exchange(slab.reshape(16, 4 * TAIL, 128), "yx"))
    return [pieces[0]] + [
        lax.ppermute(piece, AXES, along_z(-back)) for back, piece in enumerate(pieces) if back
    ]


def on_device(
    tokens,
    seq_lengths,
    ln1_gain,
    ln1_bias,
    qkv_weight,
    out_weight,
    ln2_gain,
    ln2_bias,
    up_weight,
    down_weight,
    cotangent,
):
    spot = jnp.stack([lax.axis_index("wide") & 1, lax.axis_index("narrow") & 3])
    spot = spot.astype(I32).reshape(1, 2)
    early, late = pack(
        ln1_gain, ln1_bias, qkv_weight, out_weight, ln2_gain, ln2_bias, up_weight.T, down_weight
    )
    late = lax.all_gather(late, AXES, axis_index_groups=peer_groups("zcyx"))
    early_own = copies_of_peers(early)
    early_oth = lax.ppermute(early_own, AXES, core_pairs())
    ht, qkv, weights, norms = project(spot, tokens, early_own, early_oth)
    mixed, middle, h_two, penalty, log_totals = attend(
        spot, seq_lengths, tokens, qkv, weights, norms
    )
    output, late_grad, dx, upstream, vectors = feed(
        spot, seq_lengths, middle, h_two, mixed, weights, norms, cotangent, late
    )
    late_grad = lax.psum_scatter(
        late_grad.reshape(128 * WHOLE, 128),
        AXES,
        scatter_dimension=0,
        axis_index_groups=peer_groups("zc"),
        tiled=True,
    )
    oth, own, dh_one = back(
        spot, seq_lengths, tokens, upstream, vectors, qkv, penalty, log_totals, weights, ht
    )
    tail = sum_over_peers(own, oth)
    dtokens = norm_back(tokens, dx, dh_one, norms)
    late_grad = exchange(late_grad.reshape(16, WHOLE, 128), "yx")
    qkv_grad, g1_grad, b1_grad, g2_grad, b2_grad = finish(tail)
    up_grad, down_grad, out_grad = unpack(late_grad)
    return (
        output,
        dtokens,
        g1_grad.reshape(OWN),
        b1_grad.reshape(OWN),
        qkv_grad,
        out_grad,
        g2_grad.reshape(OWN),
        b2_grad.reshape(OWN),
        up_grad.T,
        down_grad,
    )


def solution(mesh):
    rows = P(AXES, None)
    flat = P(AXES)
    columns = P(None, AXES)
    return jax.shard_map(
        on_device,
        mesh=mesh,
        in_specs=(rows, rows, flat, flat, rows, rows, flat, flat, columns, rows, rows),
        out_specs=(rows, rows, flat, flat, rows, rows, flat, flat, columns, rows),
        check_vma=False,
    )
```

time: 358 us -> 223 us (0.62)
  waiting for transfers between devices: 161 us -> 22.5 us
  blocking collectives: 42.1 us -> 70.1 us
  Pallas kernels: 119 us -> 94.1 us
  local copies, waits for them, and re-layouts: 8.18 us -> 2.05 us
  starting transfers between devices: 9.63 us -> 14.4 us
    all_gather x1, waiting for transfers between devices: 75.1 us -> 0.01 us  [on_device(): late = lax.all_gather(late, AXES, axis_index_groups=peer_groups('zcyx'))]
    reduce_scatter x3 -> x1, waiting for transfers between devices: 73 us -> 0.01 us  [on_device(): lax.psum_scatter(late_grad.reshape(128 * WHOLE, 128), AXES, scatter_dimen...]
    all_to_all x1 -> x2, blocking collectives: 42.1 us -> 70.1 us  [exchange(): lax.all_to_all(slabs, AXES, 0, 0, axis_index_groups=peer_groups(dims), ti...]
    pallas_call x8, Pallas kernels: 116 us -> 92.6 us  [the longest x1 27 us: feed(): pl.pallas_call(feed_kernel, grid=(1,), out_shape=(jax.ShapeDtypeStruct((R...]
    all_to_all x1, waiting for transfers between devices: 0.01 us -> 9.52 us  [exchange(): lax.all_to_all(slabs, AXES, 0, 0, axis_index_groups=peer_groups(dims), ti...]
    ppermute x6 -> x8, starting transfers between devices: 0.89 us -> 7.72 us  [the longest x3 5.45 us: copies_of_peers(): lax.ppermute(own, AXES, along_z(ahead))]
    unnamed x12 -> x10, local copies, waits for them, and re-layouts: 7.26 us -> 1.73 us
    ppermute x6 -> x8, waiting for transfers between devices: 13.3 us -> 13 us  [the longest x3 4.56 us: copies_of_peers(): lax.ppermute(own, AXES, along_z(ahead))]
  transfers between devices with their start and end apart: 11 -> 11, of which waited for: 6 -> 7; matrix products, arithmetic and copies ran while one was open for 1% -> 2% of each run, Pallas kernels for 21% -> 29%
where the time goes in v2:
time: 223 us; the launch traced here: 221 us
  Pallas kernels  94.1 us (42%)
  blocking collectives  70.1 us (31%)
  waiting for transfers between devices  22.5 us (10%)
  starting transfers between devices  14.4 us (6%)
  between operations  14.1 us (6%)
  other arithmetic  3.45 us (2%)
    all_to_all x2, blocking collectives, exchange(): lax.all_to_all(slabs, AXES, 0, 0, axis_index_groups=peer_groups(dims), ti...  70.1 us
    pallas_call x1, Pallas kernels, feed(): pl.pallas_call(feed_kernel, grid=(1,), out_shape=(jax.ShapeDtypeStruct((R...  27 us
    pallas_call x1, Pallas kernels, back(): pl.pallas_call(back_kernel, out_shape=(slab, slab, jax.ShapeDtypeStruct((...  26 us
    pallas_call x1, Pallas kernels, attend(): pl.pallas_call(attend_kernel, grid=(1,), out_shape=(jax.ShapeDtypeStruct(...  16.3 us
    pallas_call x1, Pallas kernels, project(): pl.pallas_call(project_kernel, out_shape=(jax.ShapeDtypeStruct((D, ROWS),...  12.9 us
    all_to_all x1, waiting for transfers between devices, exchange(): lax.all_to_all(slabs, AXES, 0, 0, axis_index_groups=peer_groups(dims), ti...  9.52 us
    all_to_all x1, starting transfers between devices, exchange(): lax.all_to_all(slabs, AXES, 0, 0, axis_index_groups=peer_groups(dims), ti...  6.6 us
    ppermute x3, starting transfers between devices, copies_of_peers(): lax.ppermute(own, AXES, along_z(ahead))  5.45 us
  transfers between devices with their start and end apart: 11, of which 7 were waited for; matrix products, arithmetic and copies ran while one was open for 2% of the time, Pallas kernels for 29%

profile of v2, /device:TPU:0, one launch (start us, length us, event | category | flops | bytes accessed | tf_op | source)
XLA Modules:
  0.0 220.8 jit_solution(18134647545381792811)
XLA Ops:
  7.2 0.0 all-gather.3.cloned.1.call-start
  7.2 1.6 pack.1
  8.8 0.0 all-gather.3.cloned.1.call-update
  8.8 0.0 reduce-scatter.2.cloned.1.call-start
  8.9 4.2 %collective-permute-start.2 = (bf16[152,128]{1,0:T(8,128)(2,1)}, bf16[152,128]{1,0:T(8,128)(2,1)S(1)}, u32[]{:S(2)}, u32[]{:S(2)}) collective-permute-start(bf16[152,128]{1,0:T(8,128)(2,1)} %get-tuple-element.41), channel_id=1, source_target_pairs={{0,3},{8,11},{1,0},{9,8},{2,1},{10,9},{3,2},{11,10},{16,19},{24,27... | collective-permute-start | bytes 116744 | tf_op jit(solution)/shard_map/ppermute | solution.py:827
  13.1 0.0 collective-permute-start.1
  13.1 1.3 collective-permute-start
  14.3 0.7 collective-permute-done.2
  15.0 3.8 %collective-permute-done.1 = bf16[152,128]{1,0:T(8,128)(2,1)S(1)} collective-permute-done((bf16[152,128]{1,0:T(8,128)(2,1)}, bf16[152,128]{1,0:T(8,128)(2,1)S(1)}, u32[]{:S(2)}, u32[]{:S(2)}) %collective-permute-start.1) | collective-permute-done | bytes 38944 | tf_op jit(solution)/shard_map/ppermute | solution.py:827
  18.8 0.1 collective-permute-done
  18.9 0.8 pad_maximum_fusion
  19.7 0.3 broadcast_in_dim.19
  20.0 40.5 %all_to_all.15 = bf16[16,608,128]{2,1,0:T(8,128)(2,1)S(1)} all-to-all(bf16[16,608,128]{2,1,0:T(8,128)(2,1)S(1)} %broadcast_in_dim.19), channel_id=1, replica_groups={{0,64,4,68,16,80,20,84,32,96,36,100,48,112,52,116},{8,72,12,76,24,88,28..., dimensions={0} | all-to-all | bytes 4980736 | tf_op jit(solution)/shard_map/all_to_all | solution.py:816
  60.5 0.0 copy-start
  60.5 0.0 collective-permute-start.3
  60.5 0.7 add_bitcast_fusion.spot_ref
  61.2 4.2 %collective-permute-done.3.oth_ref = bf16[64,152,128]{2,1,0:T(8,128)(2,1)} collective-permute-done((bf16[64,152,128]{2,1,0:T(8,128)(2,1)S(1)}, bf16[64,152,128]{2,1,0:T(8,128)(2,1)}, u32[]{:S(2)}, u32[]{:S(2)}) %collective-permute-start.3) | collective-permute-done | bytes 2490400 | tf_op jit(solution)/shard_map/ppermute | solution.py:861
  65.4 0.0 copy-done
  65.4 12.9 %project.1 = (bf16[768,512]{1,0:T(8,128)(2,1)}, bf16[512,2304]{1,0:T(8,128)(2,1)}, bf16[768,3072]{1,0:T(8,128)(2,1)}, f32[8,768]{1,0:T(8,128)}) custom-call(s32[1,2]{1,0:T(1,128)} %add_bitcast_fusion.spot_ref, bf16[512,768]{1,0:T(8,128)(2,1)} %x_ref.7, bf16[64,152,128]{2,1,0:T(8,128)(2,1)} %bitcast.21, bf16[64,152,128]{2,1,0:T(8,128)(2,1)} %collective-permute-done.3.oth_ref), custom_call_target="tpu_custom_call" | custom-call | tf_op jit(solution)/shard_map/project/pallas_call | solution.py:269
  78.2 16.3 %attend.1 = (bf16[512,1024]{1,0:T(8,128)(2,1)}, f32[512,768]{1,0:T(8,128)}, bf16[512,768]{1,0:T(8,128)(2,1)}, f32[512,512]{1,0:T(8,128)}, f32[6,8,512]{2,1,0:T(8,128)}) custom-call(s32[1,2]{1,0:T(1,128)} %add_bitcast_fusion.spot_ref, s32[1,4]{1,0:T(1,128)} %lens_ref.5, bf16[512,768]{1,0:T(8,128)(2,1)} %x_ref.7, ...), custom_call_target="tpu_custom_call" | custom-call | tf_op jit(solution)/shard_map/attend/pallas_call | solution.py:374
  94.5 0.0 all-gather.3.cloned.1.call-done
  94.5 27.0 %feed.1 = (bf16[512,768]{1,0:T(8,128)(2,1)}, bf16[128,336,128]{2,1,0:T(8,128)(2,1)}, f32[512,768]{1,0:T(8,128)}, bf16[512,768]{1,0:T(8,128)(2,1)}, f32[8,768]{1,0:T(8,128)}) custom-call(s32[1,2]{1,0:T(1,128)} %add_bitcast_fusion.spot_ref, s32[1,4]{1,0:T(1,128)} %lens_ref.5, f32[512,768]{1,0:T(8,128)} %get-tuple-element.45.middle_ref, ...), custom_call_target="tpu_custom_call" | custom-call | tf_op jit(solution)/shard_map/feed/pallas_call | solution.py:692
  121.5 0.0 reduce-scatter.2.cloned.1.call-update
  121.5 26.0 %back.1 = (bf16[64,112,128]{2,1,0:T(8,128)(2,1)}, bf16[64,112,128]{2,1,0:T(8,128)(2,1)}, f32[512,768]{1,0:T(8,128)}) custom-call(s32[1,2]{1,0:T(1,128)} %add_bitcast_fusion.spot_ref, s32[1,4]{1,0:T(1,128)} %lens_ref.5, bf16[512,768]{1,0:T(8,128)(2,1)} %x_ref.7, bf16[512,768]{1,0:T(8,128)(2,1)} %get-tuple-element.51.up, f32[8,768]{1,0:T(8,128)} %get-tuple-element.52.vec_ref, ...), custom_call_target="tpu_custom_call" | custom-call | tf_op jit(solution)/shard_map/back/pallas_call | solution.py:524
  147.6 0.2 collective-permute-start.4
  147.8 3.9 %collective-permute-done.4 = bf16[64,112,128]{2,1,0:T(8,128)(2,1)S(1)} collective-permute-done((bf16[64,112,128]{2,1,0:T(8,128)(2,1)}, bf16[64,112,128]{2,1,0:T(8,128)(2,1)S(1)}, u32[]{:S(2)}, u32[]{:S(2)}) %collective-permute-start.4) | collective-permute-done | bytes 1835040 | tf_op jit(solution)/shard_map/ppermute | solution.py:833
  151.7 2.0 add_convert_fusion
  153.7 29.6 %all_to_all.16.slabs_ref = bf16[16,448,128]{2,1,0:T(8,128)(2,1)} all-to-all(bf16[16,448,128]{2,1,0:T(8,128)(2,1)S(1)} %bitcast.23), channel_id=1, replica_groups={{0,64,4,68,16,80,20,84,32,96,36,100,48,112,52,116},{8,72,12,76,24,88,28..., dimensions={0} | all-to-all | bytes 3670016 | tf_op jit(solution)/shard_map/all_to_all | solution.py:816
  183.3 0.0 reduce-scatter.2.cloned.1.call-done
  183.3 6.6 %all-to-all-start.2 = ((bf16[16,336,128]{2,1,0:T(8,128)(2,1)}), bf16[16,336,128]{2,1,0:T(8,128)(2,1)S(1)}, u32[]{:S(2)}, u32[]{:S(2)}) async-start(bf16[16,336,128]{2,1,0:T(8,128)(2,1)} %bitcast.24), calls=%async_computation.3 | async-start | bytes 2752512 | tf_op jit(solution)/shard_map/all_to_all | solution.py:816
  189.9 2.3 %fold.1 = (bf16[112,128]{1,0:T(8,128)(2,1)}, bf16[112,128]{1,0:T(8,128)(2,1)}, bf16[112,128]{1,0:T(8,128)(2,1)}, bf16[112,128]{1,0:T(8,128)(2,1)}) custom-call(bf16[16,448,128]{2,1,0:T(8,128)(2,1)} %all_to_all.16.slabs_ref), custom_call_target="tpu_custom_call" | custom-call | tf_op jit(solution)/shard_map/fold/pallas_call | solution.py:805
  192.2 0.8 collective-permute-start.5
  193.0 0.4 collective-permute-start.6
  193.4 0.9 collective-permute-start.7
  194.3 4.3 %norm_back.1 = bf16[512,768]{1,0:T(8,128)(2,1)} custom-call(bf16[512,768]{1,0:T(8,128)(2,1)} %x_ref.7, f32[512,768]{1,0:T(8,128)} %get-tuple-element.50.dx_ref, f32[512,768]{1,0:T(8,128)} %get-tuple-element.56.dh_ref, f32[8,768]{1,0:T(8,128)} %get-tuple-element.44.ln_ref), custom_call_target="tpu_custom_call" | custom-call | tf_op jit(solution)/shard_map/norm_back/pallas_call | solution.py:733
  198.6 0.0 collective-permute-done.5.refs_1_
  198.6 0.0 copy-start.2
  198.6 0.0 collective-permute-done.6.refs_2_
  198.6 0.0 copy-start.3
  198.7 0.3 collective-permute-done.7.refs_3_
  199.0 0.0 copy-start.4
  199.0 0.2 copy-done.2
  199.2 0.0 copy-done.3
  199.3 0.4 copy-done.4
  199.6 1.5 finish.1
  201.1 9.5 %all-to-all-done.2.late_ref = bf16[16,336,128]{2,1,0:T(8,128)(2,1)S(1)} async-done(((bf16[16,336,128]{2,1,0:T(8,128)(2,1)}), bf16[16,336,128]{2,1,0:T(8,128)(2,1)S(1)}, u32[]{:S(2)}, u32[]{:S(2)}) %all-to-all-start.2) | async-done | bytes 1376288 | tf_op jit(solution)/shard_map/all_to_all | solution.py:816
  210.6 1.1 copy-done.1
  211.7 2.2 %unpack.1 = (f32[24,768]{1,0:T(8,128)}, f32[24,768]{1,0:T(8,128)}, f32[6,768]{1,0:T(8,128)}) custom-call(bf16[16,336,128]{2,1,0:T(8,128)(2,1)} %copy-done.1), custom_call_target="tpu_custom_call" | custom-call | tf_op jit(solution)/shard_map/unpack/pallas_call | solution.py:786
  (1 shorter events, 0.0 us)
Async XLA Ops:
  7.2 87.4 %all-gather.3.cloned.1.call-start = ((), (), s32[]{:S(2)}) async-start(), calls=%async_computation.5 | async-start | bytes 9510912 | tf_op jit(solution)/shard_map/all_gather | solution.py:859
  8.8 174.4 %reduce-scatter.2.cloned.1.call-start = ((), (), s32[]{:S(2)}) async-start(), calls=%async_computation.4 | async-start | bytes 12386304 | tf_op jit(solution)/shard_map/reduce_scatter | solution.py:869
  8.9 6.2 %collective-permute-start.2 = (bf16[152,128]{1,0:T(8,128)(2,1)}, bf16[152,128]{1,0:T(8,128)(2,1)S(1)}, u32[]{:S(2)}, u32[]{:S(2)}) collective-permute-start(bf16[152,128]{1,0:T(8,128)(2,1)} %get-tuple-element.41), channel_id=1, source_target_pairs={{0,3},{8,11},{1,0},{9,8},{2,1},{10,9},{3,2},{11,10},{16,19},{24,27... | collective-permute-start | bytes 116744 | tf_op jit(solution)/shard_map/ppermute | solution.py:827
  13.1 5.7 %collective-permute-start.1 = (bf16[152,128]{1,0:T(8,128)(2,1)}, bf16[152,128]{1,0:T(8,128)(2,1)S(1)}, u32[]{:S(2)}, u32[]{:S(2)}) collective-permute-start(bf16[152,128]{1,0:T(8,128)(2,1)} %get-tuple-element.41), channel_id=1, source_target_pairs={{0,2},{8,10},{1,3},{9,11},{2,0},{10,8},{3,1},{11,9},{16,18},{24,26... | collective-permute-start | bytes 116744 | tf_op jit(solution)/shard_map/ppermute | solution.py:827
  13.1 5.8 %collective-permute-start = (bf16[152,128]{1,0:T(8,128)(2,1)}, bf16[152,128]{1,0:T(8,128)(2,1)S(1)}, u32[]{:S(2)}, u32[]{:S(2)}) collective-permute-start(bf16[152,128]{1,0:T(8,128)(2,1)} %get-tuple-element.41), channel_id=1, source_target_pairs={{0,1},{8,9},{1,2},{9,10},{2,3},{10,11},{3,0},{11,8},{16,17},{24,25... | collective-permute-start | bytes 116744 | tf_op jit(solution)/shard_map/ppermute | solution.py:827
  60.5 4.9 %copy-start = (bf16[16,608,128]{2,1,0:T(8,128)(2,1)}, bf16[16,608,128]{2,1,0:T(8,128)(2,1)S(1)}, u32[]{:S(2)}) copy-start(bf16[16,608,128]{2,1,0:T(8,128)(2,1)S(1)} %all_to_all.15) | copy-start | bytes 7471108
  60.5 4.9 %collective-permute-start.3 = (bf16[64,152,128]{2,1,0:T(8,128)(2,1)S(1)}, bf16[64,152,128]{2,1,0:T(8,128)(2,1)}, u32[]{:S(2)}, u32[]{:S(2)}) collective-permute-start(bf16[64,152,128]{2,1,0:T(8,128)(2,1)S(1)} %bitcast.20), channel_id=1, source_target_pairs={{0,8},{8,0},{1,9},{9,1},{2,10},{10,2},{3,11},{11,3},{16,24},{24,16... | collective-permute-start | bytes 7471112 | tf_op jit(solution)/shard_map/ppermute | solution.py:861
  147.6 4.1 %collective-permute-start.4 = (bf16[64,112,128]{2,1,0:T(8,128)(2,1)}, bf16[64,112,128]{2,1,0:T(8,128)(2,1)S(1)}, u32[]{:S(2)}, u32[]{:S(2)}) collective-permute-start(bf16[64,112,128]{2,1,0:T(8,128)(2,1)} %get-tuple-element.58), channel_id=1, source_target_pairs={{0,8},{8,0},{1,9},{9,1},{2,10},{10,2},{3,11},{11,3},{16,24},{24,16... | collective-permute-start | bytes 5505032 | tf_op jit(solution)/shard_map/ppermute | solution.py:833
  183.3 27.3 %all-to-all-start.2 = ((bf16[16,336,128]{2,1,0:T(8,128)(2,1)}), bf16[16,336,128]{2,1,0:T(8,128)(2,1)S(1)}, u32[]{:S(2)}, u32[]{:S(2)}) async-start(bf16[16,336,128]{2,1,0:T(8,128)(2,1)} %bitcast.24), calls=%async_computation.3 | async-start | bytes 2752512 | tf_op jit(solution)/shard_map/all_to_all | solution.py:816
  192.2 6.4 %collective-permute-start.5 = (bf16[112,128]{1,0:T(8,128)(2,1)}, bf16[112,128]{1,0:T(8,128)(2,1)S(1)}, u32[]{:S(2)}, u32[]{:S(2)}) collective-permute-start(bf16[112,128]{1,0:T(8,128)(2,1)} %get-tuple-element.60), channel_id=1, source_target_pairs={{0,3},{8,11},{1,0},{9,8},{2,1},{10,9},{3,2},{11,10},{16,19},{24,27... | collective-permute-start | bytes 86024 | tf_op jit(solution)/shard_map/ppermute | solution.py:837
  193.0 5.6 %collective-permute-start.6 = (bf16[112,128]{1,0:T(8,128)(2,1)}, bf16[112,128]{1,0:T(8,128)(2,1)S(1)}, u32[]{:S(2)}, u32[]{:S(2)}) collective-permute-start(bf16[112,128]{1,0:T(8,128)(2,1)} %get-tuple-element.61), channel_id=1, source_target_pairs={{0,2},{8,10},{1,3},{9,11},{2,0},{10,8},{3,1},{11,9},{16,18},{24,26... | collective-permute-start | bytes 86024 | tf_op jit(solution)/shard_map/ppermute | solution.py:837
  193.4 5.6 %collective-permute-start.7 = (bf16[112,128]{1,0:T(8,128)(2,1)}, bf16[112,128]{1,0:T(8,128)(2,1)S(1)}, u32[]{:S(2)}, u32[]{:S(2)}) collective-permute-start(bf16[112,128]{1,0:T(8,128)(2,1)} %get-tuple-element.62), channel_id=1, source_target_pairs={{0,1},{8,9},{1,2},{9,10},{2,3},{10,11},{3,0},{11,8},{16,17},{24,25... | collective-permute-start | bytes 86024 | tf_op jit(solution)/shard_map/ppermute | solution.py:837
  198.6 0.6 copy-start.2
  198.6 0.6 copy-start.3
  199.0 0.6 copy-start.4
  210.6 1.1 copy-start.1
Sparse Core Ops, SparseCore 0:
  11.4 81.8 all-gather.2
  121.7 61.3 reduce-scatter.1

commit v3 on v2

--- a/solution.py
+++ b/solution.py
@@ -1,3 +1,4 @@
+import functools
 import itertools
 
 import jax
@@ -84,9 +85,9 @@
 
 
 def owner(group, core, spot):
-    y = group >> 4
-    x = (group >> 2) & 3
-    z = (spot[1] - (group & 3)) & 3
+    y = (spot[3] - (group >> 4)) & 3
+    x = (spot[2] - (group >> 2)) & 3
+    z = (spot[1] - group) & 3
     return ((x & 1) << 6) + (y << 4) + (core << 3) + ((x >> 1) << 2) + z
 
 
@@ -113,9 +114,9 @@
 
 
 def late_owner(group):
-    z = group >> 5
+    y = group >> 5
     c = (group >> 4) & 1
-    y = (group >> 2) & 3
+    z = (group >> 2) & 3
     x = group & 3
     return ((x & 1) << 6) + (y << 4) + (c << 3) + ((x >> 1) << 2) + z
 
@@ -182,7 +183,6 @@
 VM = pl.BlockSpec(memory_space=pltpu.VMEM)
 SM = pl.BlockSpec(memory_space=pltpu.SMEM)
 ANY = pl.BlockSpec(memory_space=pl.ANY)
-OUT_WEIGHT = pl.BlockSpec((D, D), lambda i: (0, 3), memory_space=pltpu.VMEM)
 
 
 def params(limit=60):
@@ -224,64 +224,6 @@
     )(g1[None], b1[None], qkv, out, g2[None], b2[None], up, down)
 
 
-def project_kernel(spot_ref, x_ref, own_ref, oth_ref, ht_ref, qkv_ref, w_ref, ln_ref, hs, rows_s):
-    spot = (spot_ref[0, 0], spot_ref[0, 1])
-    core = spot[0]
-    vectors = [jnp.zeros((1, D), F32) for _ in range(4)]
-    for half, source in enumerate((own_ref, oth_ref)):
-        side = core if half == 0 else 1 - core
-
-        @pl.loop(0, 8)
-        def _(block):
-            start = pl.multiple_of(block * (8 * EARLY), 8 * EARLY)
-            values = source[pl.ds(block * 8, 8)].astype(F32)
-            rows_s[pl.ds(start, 8 * EARLY), :] = values.reshape(8 * EARLY, 128)
-
-        for block in range(4 * BLOCKS):
-            for row in range(OWN):
-                to = half * HALF + row * PEERS
-                w_ref[to : to + PEERS, block * 128 : block * 128 + 128] = rows_s[
-                    pl.ds(block * OWN + row, PEERS, stride=EARLY), :
-                ].astype(BF)
-        packed = rows_s[pl.ds(GATHERED, PEERS, stride=EARLY), :]
-        mine = owned_features(side, spot)
-        vectors = [
-            vector + unpack_vector(packed, mine, which) for which, vector in enumerate(vectors)
-        ]
-    for which, vector in enumerate(vectors):
-        ln_ref[which : which + 1, :] = vector
-    ln_ref[4:8, :] = jnp.zeros((4, D), F32)
-
-    @pl.loop(0, 4)
-    def _(block):
-        rows = pl.ds(pl.multiple_of(block * 128, 128), 128)
-        unit, _ = norm_stats(x_ref[rows, :].astype(F32))
-        hs[rows, :] = (unit * ln_ref[0:1, :] + ln_ref[1:2, :]).astype(BF)
-
-    placed = dot_nn(hs[...], place_matrix(spot)).astype(BF)
-    for part in range(3):
-        columns = slice(part * D, part * D + D)
-        qkv_ref[:, columns] = dot_nn(placed, w_ref[:, columns]).astype(BF)
-    ht_ref[...] = dot_nt(place_transposed(spot), hs[...]).astype(BF)
-
-
-def project(spot, x, own, oth):
-    return pl.pallas_call(
-        project_kernel,
-        out_shape=(
-            jax.ShapeDtypeStruct((D, ROWS), BF),
-            jax.ShapeDtypeStruct((ROWS, 3 * D), BF),
-            jax.ShapeDtypeStruct((D, 4 * D), BF),
-            jax.ShapeDtypeStruct((8, D), F32),
-        ),
-        in_specs=[SM, VM, VM, VM],
-        out_specs=(VM, VM, VM, VM),
-        scratch_shapes=[pltpu.VMEM((ROWS, D), BF), pltpu.VMEM((PEERS * EARLY, 128), F32)],
-        compiler_params=params(),
-        name="project",
-    )(spot, x, own, oth)
-
-
 def softplus4(logits):
     sharp = 4.0 * logits
     return 0.25 * (jnp.maximum(sharp, 0.0) + jnp.log(1.0 + jnp.exp(-jnp.abs(sharp))))
@@ -318,48 +260,96 @@
     return pl.ds(pl.multiple_of(pair * 384 + part * 128, 128), 128)
 
 
-def attend_kernel(
-    spot_ref, lens_ref, x_ref, qkv_ref, wo_ref, ln_ref, mixed_ref, middle_ref, h_ref, pen_ref, lse_ref, attn_s, carry
+def front_kernel(
+    spot_ref, lens_ref, x_ref, own_ref, oth_ref,
+    ht_ref, qkv_ref, w_ref, ln_ref, mixed_ref, middle_ref, h_ref, pen_ref, lse_ref,
+    rows_s, w, h_s, qkv, pen, attn_s, carry, sems,
 ):
+    spot = tuple(spot_ref[0, at] for at in range(4))
+    core = spot[0]
+    vectors = [jnp.zeros((1, D), F32) for _ in range(4)]
+    for half, source in enumerate((own_ref, oth_ref)):
+        side = core if half == 0 else 1 - core
+
+        @pl.loop(0, 8)
+        def _(block):
+            for peer in range(8):
+                start = (block * 8 + peer) * (EARLY + 1)
+                rows_s[pl.ds(start, EARLY), :] = source[block * 8 + peer].astype(F32)
+
+        for block in range(4 * BLOCKS):
+            for row in range(OWN):
+                to = half * HALF + row * PEERS
+                w[to : to + PEERS, block * 128 : block * 128 + 128] = rows_s[
+                    pl.ds(block * OWN + row, PEERS, stride=EARLY + 1), :
+                ].astype(BF)
+        packed = rows_s[pl.ds(GATHERED, PEERS, stride=EARLY + 1), :]
+        mine = owned_features(side, spot)
+        vectors = [
+            vector + unpack_vector(packed, mine, which) for which, vector in enumerate(vectors)
+        ]
+    store_w = pltpu.make_async_copy(w, w_ref, sems.at[0])
+    store_w.start()
+    for which, vector in enumerate(vectors):
+        ln_ref[which : which + 1, :] = vector
+    ln_ref[4:8, :] = jnp.zeros((4, D), F32)
+
+    @pl.loop(0, 4)
+    def _(block):
+        rows = pl.ds(pl.multiple_of(block * 128, 128), 128)
+        unit, _ = norm_stats(x_ref[rows, :].astype(F32))
+        h_s[rows, :] = (unit * ln_ref[0:1, :] + ln_ref[1:2, :]).astype(BF)
+
+    place = place_matrix(spot)
+    placed = dot_nn(h_s[...], place).astype(BF)
+    for part in range(3):
+        columns = slice(part * D, part * D + D)
+        qkv[:, columns] = dot_nn(placed, w[:, columns]).astype(BF)
+    store_qkv = pltpu.make_async_copy(qkv, qkv_ref, sems.at[1])
+    store_qkv.start()
+
     ends = group_ends(lens_ref)
     scale = jnp.asarray(0.125, BF)
     row, column = iota((128, 256), 0), iota((128, 256), 1)
     before = one_hot((row < column) | (column >= 128))
     carry[...] = jnp.zeros_like(carry)
-    k0 = qkv_ref[:, 128:256]
+    k0 = qkv[:, 128:256]
     for block in range(4):
         count = (block + 1) * 128
         rows = slice(block * 128, count)
-        q0 = side_by_side(qkv_ref[rows, 0:128] * scale)[0:128]
+        q0 = side_by_side(qkv[rows, 0:128] * scale)[0:128]
         allowed, chosen = block_masks(block, ends)
         picked = jnp.where(chosen, softplus4(dot_nt(k0[:count], q0)), 0.0)
         high, low = split_low(picked)
         sums = dot_nn(high, before) + dot_nn(low, before)
-        pen_ref[:count, rows] = jnp.where(allowed, sums[:, 0:128] + carry[:count, :], FAR)
+        pen[:count, rows] = jnp.where(allowed, sums[:, 0:128] + carry[:count, :], FAR)
         carry[:count, :] = carry[:count, :] + sums[:, 128:256]
-
-    @pl.loop(0, 6)
-    def _(pair):
-        lanes = pl.ds(pl.multiple_of(pair * 128, 128), 128)
-        k = qkv_ref[:, lanes_of(pair, 1)]
-        v = qkv_ref[:, lanes_of(pair, 2)]
+    store_pen = pltpu.make_async_copy(pen, pen_ref, sems.at[2])
+    store_pen.start()
+
+    @pl.loop(0, 3)
+    def _(turn):
         for block in range(4):
             count = (block + 1) * 128
             rows = slice(block * 128, count)
-            q = side_by_side(qkv_ref[rows, lanes_of(pair, 0)] * scale)
-            shifted = dot_nt(k[:count], q) - twice(pen_ref[:count, rows])
-            top = jnp.max(shifted, axis=0, keepdims=True)
-            exponent = jnp.exp(shifted - top)
-            total = jnp.sum(exponent, axis=0, keepdims=True)
-            mixed = dot_tn(v[:count], exponent.astype(BF)) * (1.0 / total)
-            attn_s[lanes, rows] = own_halves(mixed).astype(BF)
-            log_total = top + jnp.log(total)
-            lse_ref[pair, 0:1, rows] = log_total[:, 0:128]
-            lse_ref[pair, 1:2, rows] = log_total[:, 128:256]
-
-    mixed_ref[...] = dot_tn(attn_s[...], place_late()).astype(BF)
-    mixed = dot_tn(attn_s[...], place_matrix((spot_ref[0, 0], spot_ref[0, 1]))).astype(BF)
-    middle_ref[...] = dot_nn(mixed, wo_ref[...])
+            penalty = twice(pen[:count, rows])
+            for pair in (2 * turn, 2 * turn + 1):
+                k = qkv[:count, lanes_of(pair, 1)]
+                v = qkv[:count, lanes_of(pair, 2)]
+                q = side_by_side(qkv[rows, lanes_of(pair, 0)] * scale)
+                shifted = dot_nt(k, q) - penalty
+                top = jnp.max(shifted, axis=0, keepdims=True)
+                exponent = jnp.exp(shifted - top)
+                total = jnp.sum(exponent, axis=0, keepdims=True)
+                mixed = dot_tn(v, exponent.astype(BF)) * (1.0 / total)
+                lanes = pl.ds(pl.multiple_of(pair * 128, 128), 128)
+                attn_s[lanes, rows] = own_halves(mixed).astype(BF)
+                log_total = top + jnp.log(total)
+                lse_ref[pair, 0:1, rows] = log_total[:, 0:128]
+                lse_ref[pair, 1:2, rows] = log_total[:, 128:256]
+
+    mixed = dot_tn(attn_s[...], place).astype(BF)
+    middle_ref[...] = dot_nn(mixed, w[:, 3 * D : 4 * D])
 
     @pl.loop(0, 4)
     def _(block):
@@ -369,77 +359,109 @@
         unit, _ = norm_stats(middle)
         h_ref[rows, :] = (unit * ln_ref[2:3, :] + ln_ref[3:4, :]).astype(BF)
 
-
-def attend(spot, lens, x, qkv, weights, ln):
+    mixed_ref[...] = dot_tn(attn_s[...], place_late()).astype(BF)
+    ht_ref[...] = dot_nt(place_transposed(spot), h_s[...]).astype(BF)
+    for store in (store_w, store_qkv, store_pen):
+        store.wait()
+
+
+def front(spot, lens, x, own, oth):
     return pl.pallas_call(
-        attend_kernel,
-        grid=(1,),
+        front_kernel,
         out_shape=(
+            jax.ShapeDtypeStruct((D, ROWS), BF),
+            jax.ShapeDtypeStruct((ROWS, 3 * D), BF),
+            jax.ShapeDtypeStruct((D, 4 * D), BF),
+            jax.ShapeDtypeStruct((8, D), F32),
             jax.ShapeDtypeStruct((ROWS, WIDE), BF),
             jax.ShapeDtypeStruct((ROWS, D), F32),
             jax.ShapeDtypeStruct((ROWS, D), BF),
             jax.ShapeDtypeStruct((ROWS, ROWS), F32),
             jax.ShapeDtypeStruct((6, 8, ROWS), F32),
         ),
-        in_specs=[SM, SM, VM, VM, OUT_WEIGHT, VM],
-        out_specs=(VM,) * 5,
-        scratch_shapes=[pltpu.VMEM((D, ROWS), BF), pltpu.VMEM((ROWS, 128), F32)],
+        in_specs=[SM, SM, VM, VM, VM],
+        out_specs=(VM, ANY, ANY, VM, VM, VM, VM, ANY, VM),
+        scratch_shapes=[
+            pltpu.VMEM((PEERS * (EARLY + 1), 128), F32),
+            pltpu.VMEM((D, 4 * D), BF),
+            pltpu.VMEM((ROWS, D), BF),
+            pltpu.VMEM((ROWS, 3 * D), BF),
+            pltpu.VMEM((ROWS, ROWS), F32),
+            pltpu.VMEM((D, ROWS), BF),
+            pltpu.VMEM((ROWS, 128), F32),
+            pltpu.SemaphoreType.DMA((3,)),
+        ],
         compiler_params=params(),
-        name="attend",
-    )(spot, lens, x, qkv, weights, ln)
-
-
-def back_pair(pair, qkv, up, pen, lse, total, grads, kept, dk_acc, dv_acc):
+        name="front",
+    )(spot, lens, x, own, oth)
+
+
+def add_blocks(sums, values):
+    for at in range(values.shape[0] // 128):
+        part = values[at * 128 : at * 128 + 128]
+        if at < len(sums):
+            sums[at] = sums[at] + part
+        else:
+            sums.append(part)
+
+
+def back_pairs(pairs, qkv, up, pen, lse, total, grads, kept):
     scale = jnp.asarray(0.125, BF)
-    k = qkv[:, lanes_of(pair, 1)]
-    v = qkv[:, lanes_of(pair, 2)]
-    dv_acc[...] = jnp.zeros_like(dv_acc)
-    dk_acc[...] = jnp.zeros_like(dk_acc)
+    dk = [[] for _ in pairs]
+    dv = [[] for _ in pairs]
     for block in range(4):
         count = (block + 1) * 128
         rows = slice(block * 128, count)
-        q = side_by_side(qkv[rows, lanes_of(pair, 0)] * scale)
-        u = side_by_side(up[rows, pl.ds(pl.multiple_of(pair * 128, 128), 128)])
-        log_total = jnp.concatenate([lse[pair, 0:1, rows], lse[pair, 1:2, rows]], axis=1)
-        soft = jnp.exp(dot_nt(k[:count], q) - twice(pen[:count, rows]) - log_total)
-        pulled = dot_nt(v[:count], u)
-        inner = jnp.sum(pulled * soft, axis=0, keepdims=True)
-        dz = soft * (pulled - inner)
-        total[:count, rows] = total[:count, rows] + (dz[:, 0:128] + dz[:, 128:256])
-        dv_acc[:count, :] = dv_acc[:count, :] + dot_nn(soft.astype(BF), u)
-        if kept is not None:
-            kept[block, :count, :] = dz
-        else:
-            low = dz.astype(BF)
-            dk_acc[:count, :] = dk_acc[:count, :] + dot_nn(low, q)
-            dq = (own_halves(dot_tn(k[:count], low)) * 0.125).T
-            grads[rows, lanes_of(pair, 0)] = dq.astype(BF)
-    grads[:, lanes_of(pair, 2)] = dv_acc[...].astype(BF)
-    if kept is None:
-        grads[:, lanes_of(pair, 1)] = dk_acc[...].astype(BF)
-
-
-def back_first(ends, qkv, total, grads, kept, dk_acc, carry):
+        penalty = twice(pen[:count, rows])
+        gathered = total[:count, rows]
+        for at, pair in enumerate(pairs):
+            k = qkv[:count, lanes_of(pair, 1)]
+            v = qkv[:count, lanes_of(pair, 2)]
+            q = side_by_side(qkv[rows, lanes_of(pair, 0)] * scale)
+            u = side_by_side(up[rows, pl.ds(pl.multiple_of(pair * 128, 128), 128)])
+            log_total = jnp.concatenate([lse[pair, 0:1, rows], lse[pair, 1:2, rows]], axis=1)
+            soft = jnp.exp(dot_nt(k, q) - penalty - log_total)
+            pulled = dot_nt(v, u)
+            inner = jnp.sum(pulled * soft, axis=0, keepdims=True)
+            dz = soft * (pulled - inner)
+            gathered = gathered + (dz[:, 0:128] + dz[:, 128:256])
+            add_blocks(dv[at], dot_nn(soft.astype(BF), u))
+            if kept is not None and at == 0:
+                kept[block, :count, :] = dz
+            else:
+                low = dz.astype(BF)
+                add_blocks(dk[at], dot_nn(low, q))
+                dq = (own_halves(dot_tn(k, low)) * 0.125).T
+                grads[rows, lanes_of(pair, 0)] = dq.astype(BF)
+        total[:count, rows] = gathered
+    for at, pair in enumerate(pairs):
+        grads[:, lanes_of(pair, 2)] = jnp.concatenate(dv[at], axis=0).astype(BF)
+        if dk[at]:
+            grads[:, lanes_of(pair, 1)] = jnp.concatenate(dk[at], axis=0).astype(BF)
+
+
+def back_first(ends, qkv, total, grads, kept):
     scale = jnp.asarray(0.125, BF)
-    k = qkv[:, 128:256]
     row, column = iota((128, 256), 0), iota((128, 256), 1)
     after = one_hot((row > column) | (column >= 128))
-    carry[...] = jnp.zeros_like(carry)
+    carry = jnp.zeros((ROWS, 128), F32)
+    dk = []
     for block in (3, 2, 1, 0):
         count = (block + 1) * 128
         rows = slice(block * 128, count)
+        k = qkv[:count, 128:256]
         q = side_by_side(qkv[rows, 0:128] * scale)
         _, chosen = block_masks(block, ends)
         high, low = split_low(total[:count, rows])
         sums = dot_nn(high, after) + dot_nn(low, after)
-        picked = sums[:, 0:128] + carry[:count, :]
-        carry[:count, :] = carry[:count, :] + sums[:, 128:256]
-        slope = 1.0 / (1.0 + jnp.exp(-4.0 * dot_nt(k[:count], q[0:128])))
+        picked = sums[:, 0:128] + carry[:count]
+        carry = carry[:count] + sums[:, 128:256]
+        slope = 1.0 / (1.0 + jnp.exp(-4.0 * dot_nt(k, q[0:128])))
         first = kept[block, :count, 0:128] - jnp.where(chosen, slope * picked, 0.0)
         low = jnp.concatenate([first, kept[block, :count, 128:256]], axis=1).astype(BF)
-        dk_acc[:count, :] = dk_acc[:count, :] + dot_nn(low, q)
-        grads[rows, 0:128] = (own_halves(dot_tn(k[:count], low)) * 0.125).T.astype(BF)
-    grads[:, 128:256] = dk_acc[...].astype(BF)
+        add_blocks(dk, dot_nn(low, q))
+        grads[rows, 0:128] = (own_halves(dot_tn(k, low)) * 0.125).T.astype(BF)
+    grads[:, 128:256] = jnp.concatenate(dk, axis=0).astype(BF)
 
 
 def put_rows(rows_s, piece, start):
@@ -450,39 +472,49 @@
 
 
 def back_kernel(
-    spot_ref, lens_ref, x_ref, up, vec_ref,
-    qkv_hbm, pen_hbm, lse_hbm, w_hbm, ht_hbm,
+    spot_ref, lens_ref, dx_ref, vec_ref,
+    qkv_hbm, pen_hbm, lse_hbm, w_hbm, ht_hbm, x_hbm,
     oth_ref, own_ref, dh_one_ref,
-    qkv, pen, lse, w, ht,
-    total, kept, grads, dk_acc, dv_acc, carry, dh_s, vec_s, rows_s, slab_s, sems, out_sems,
+    qkv, pen, lse, w, ht, x_ref, up,
+    total, kept, grads, dh_s, vec_s, rows_s, slab_s, sems, out_sems,
 ):
-    spot = (spot_ref[0, 0], spot_ref[0, 1])
+    spot = tuple(spot_ref[0, at] for at in range(4))
     core = spot[0]
     ends = group_ends(lens_ref)
     loads = [
         pltpu.make_async_copy(source, target, sems.at[number])
         for number, (source, target) in enumerate(
-            ((qkv_hbm, qkv), (pen_hbm, pen), (lse_hbm, lse), (w_hbm.at[:, 0 : 3 * D], w), (ht_hbm, ht))
+            (
+                (w_hbm, w),
+                (qkv_hbm, qkv),
+                (pen_hbm, pen),
+                (lse_hbm, lse),
+                (ht_hbm, ht),
+                (x_hbm, x_ref),
+            )
         )
     ]
     for load in loads:
         load.start()
     total[...] = jnp.zeros_like(total)
     vec_s[...] = vec_ref[...]
-    for load in loads[0:3]:
+    place = place_matrix(spot)
+    loads[0].wait()
+    placed = dot_nt(dx_ref[...].astype(BF), w[:, 3 * D : 4 * D]).astype(BF)
+    up[...] = dot_nt(placed, place).astype(BF)
+    for load in loads[1:4]:
         load.wait()
 
-    @pl.loop(1, 6)
-    def _(pair):
-        back_pair(pair, qkv, up, pen, lse, total, grads, None, dk_acc, dv_acc)
-
-    back_pair(0, qkv, up, pen, lse, total, grads, kept, dk_acc, dv_acc)
-    back_first(ends, qkv, total, grads, kept, dk_acc, carry)
-    for load in loads[3:]:
+    @pl.loop(0, 2)
+    def _(turn):
+        back_pairs((2 * turn + 2, 2 * turn + 3), qkv, up, pen, lse, total, grads, None)
+
+    back_pairs((0, 1), qkv, up, pen, lse, total, grads, kept)
+    back_first(ends, qkv, total, grads, kept)
+    for load in loads[4:]:
         load.wait()
-    high, low = split_low(dot_nt(grads[...], w[...]))
-    place = place_matrix(spot)
-    dh_s[...] = dot_nt(high, place) + dot_nt(low, place)
+    placed = dot_nt(grads[...], w[:, 0 : 3 * D]).astype(BF)
+    dh_s[...] = dot_nt(placed, place)
 
     @pl.loop(0, 4)
     def _(block):
@@ -509,8 +541,10 @@
         @pl.loop(0, 8)
         def _(block):
             for peer in range(8):
-                start = (block * 8 + peer) * STEP
-                slab_s[half, block * 8 + peer] = rows_s[pl.ds(start, TAIL), :].astype(BF)
+                group = block * 8 + peer
+                z, x = (spot[1] - group) & 3, (spot[2] - (group >> 2)) & 3
+                to = z * 16 + x * 4 + (group >> 4)
+                slab_s[half, to] = rows_s[pl.ds(group * STEP, TAIL), :].astype(BF)
 
         store = pltpu.make_async_copy(slab_s.at[half], target, out_sems.at[half])
         store.start()
@@ -519,41 +553,40 @@
         store.wait()
 
 
-def back(spot, lens, x, up, vec, qkv, pen, lse, weights, ht):
+def back(spot, lens, dx, vec, qkv, pen, lse, weights, ht, x):
     slab = jax.ShapeDtypeStruct((PEERS, TAIL, 128), BF)
     return pl.pallas_call(
         back_kernel,
         out_shape=(slab, slab, jax.ShapeDtypeStruct((ROWS, D), F32)),
-        in_specs=[SM, SM] + [VM] * 3 + [ANY] * 5,
+        in_specs=[SM, SM, VM, VM] + [ANY] * 6,
         out_specs=(ANY,) * 3,
         scratch_shapes=[
             pltpu.VMEM((ROWS, 3 * D), BF),
             pltpu.VMEM((ROWS, ROWS), F32),
             pltpu.VMEM((6, 8, ROWS), F32),
-            pltpu.VMEM((D, 3 * D), BF),
+            pltpu.VMEM((D, 4 * D), BF),
             pltpu.VMEM((D, ROWS), BF),
+            pltpu.VMEM((ROWS, D), BF),
+            pltpu.VMEM((ROWS, D), BF),
             pltpu.VMEM((ROWS, ROWS), F32),
             pltpu.VMEM((4, ROWS, 256), F32),
             pltpu.VMEM((ROWS, 3 * D), BF),
-            pltpu.VMEM((ROWS, 128), F32),
-            pltpu.VMEM((ROWS, 128), F32),
-            pltpu.VMEM((ROWS, 128), F32),
             pltpu.VMEM((ROWS, D), F32),
             pltpu.VMEM((8, D), F32),
             pltpu.VMEM((PEERS * STEP, 128), F32),
             pltpu.VMEM((2, PEERS, TAIL, 128), BF),
-            pltpu.SemaphoreType.DMA((5,)),
+            pltpu.SemaphoreType.DMA((6,)),
             pltpu.SemaphoreType.DMA((3,)),
         ],
         compiler_params=params(),
         name="back",
-    )(spot, lens, x, up, vec, qkv, pen, lse, weights, ht)
+    )(spot, lens, dx, vec, qkv, pen, lse, weights, ht, x)
 
 
 def feed_kernel(
-    spot_ref, lens_ref, middle_ref, h_ref, mixed_ref, wo_ref, ln_ref, cot_ref, late_ref,
-    y_ref, grad_ref, dx_ref, up_ref, vec_ref,
-    up_s, down_s, mid_s, gup_s, gdown_s, gout_s, dy_s, h_s, acc_s, dh_ref, sems, out_sems,
+    lens_ref, middle_ref, h_ref, ln_ref, cot_ref, mixed_hbm, late_ref,
+    y_ref, grad_ref, dx_ref, vec_ref,
+    up_s, down_s, mid_s, gup_s, gdown_s, gout_s, mixed_s, dy_s, h_s, y_s, dx_s, acc_s, dh_ref, sems, out_sems,
 ):
     def load_up(chunk):
         devices = pl.ds(chunk * 32, 32)
@@ -597,6 +630,8 @@
         load_down(chunk).start()
     for half in range(2):
         load_mid(half).start()
+    load_mixed = pltpu.make_async_copy(mixed_hbm, mixed_s, sems.at[10])
+    load_mixed.start()
     ends = group_ends(lens_ref)
     gain = ln_ref[2:3, :]
     vec_ref[...] = jnp.zeros_like(vec_ref)
@@ -652,7 +687,7 @@
     @pl.loop(0, 4)
     def _(block):
         rows = pl.ds(pl.multiple_of(block * 128, 128), 128)
-        y_ref[rows, :] = acc_s[rows, :].astype(BF)
+        y_s[rows, :] = acc_s[rows, :].astype(BF)
         unit, inverse = norm_stats(middle_ref[rows, :])
         gradient = dh_ref[rows, :]
         vec_ref[2:3, :] = vec_ref[2:3, :] + jnp.sum(gradient * unit, axis=0, keepdims=True)
@@ -660,10 +695,15 @@
         live = (iota((128, 1), 0) + block * 128) < ends[3]
         dy = jnp.where(live, cot_ref[rows, :].astype(F32), 0.0)
         moved = dy + norm_pull(gradient, unit, inverse, gain)
-        dx_ref[rows, :] = moved
+        dx_s[rows, :] = moved
         h_s[rows, :] = moved.astype(BF)
 
-    outer = dot_tn(mixed_ref[...], h_s[...])
+    store_y = pltpu.make_async_copy(y_s, y_ref, out_sems.at[9])
+    store_y.start()
+    store_dx = pltpu.make_async_copy(dx_s, dx_ref, out_sems.at[10])
+    store_dx.start()
+    load_mixed.wait()
+    outer = dot_tn(mixed_s[...], h_s[...])
     stores = []
     for block in range(0, BLOCKS, 2):
         pieces = [
@@ -676,31 +716,27 @@
         )
         store.start()
         stores.append(store)
-    placed = dot_nt(h_s[...], wo_ref[...]).astype(BF)
-    up_ref[...] = dot_nt(placed, place_matrix((spot_ref[0, 0], spot_ref[0, 1]))).astype(BF)
     for block in range(BLOCKS):
         for chunk in range(4):
             for copy in store_big(chunk, block):
                 copy.wait()
         for half in range(2):
             store_mid(half, block).wait()
-    for store in stores:
+    for store in (store_y, store_dx, *stores):
         store.wait()
 
 
-def feed(spot, lens, middle, h, mixed, weights, ln, cot, late):
+def feed(lens, middle, h, ln, cot, mixed, late):
     return pl.pallas_call(
         feed_kernel,
-        grid=(1,),
         out_shape=(
             jax.ShapeDtypeStruct((ROWS, D), BF),
             jax.ShapeDtypeStruct((128, WHOLE, 128), BF),
             jax.ShapeDtypeStruct((ROWS, D), F32),
-            jax.ShapeDtypeStruct((ROWS, D), BF),
             jax.ShapeDtypeStruct((8, D), F32),
         ),
-        in_specs=[SM, SM, VM, VM, VM, OUT_WEIGHT, VM, VM, ANY],
-        out_specs=(VM, ANY, VM, VM, VM),
+        in_specs=[SM, VM, VM, VM, VM, ANY, ANY],
+        out_specs=(ANY, ANY, ANY, VM),
         scratch_shapes=[
             pltpu.VMEM((4, 32, 16, D), BF),
             pltpu.VMEM((4, 32, 16, D), BF),
@@ -708,16 +744,19 @@
             pltpu.VMEM((4, 32, 16, D), BF),
             pltpu.VMEM((4, 32, 16, D), BF),
             pltpu.VMEM((3, 128, 16, 128), BF),
+            pltpu.VMEM((ROWS, WIDE), BF),
+            pltpu.VMEM((ROWS, D), BF),
             pltpu.VMEM((ROWS, D), BF),
             pltpu.VMEM((ROWS, D), BF),
             pltpu.VMEM((ROWS, D), F32),
             pltpu.VMEM((ROWS, D), F32),
-            pltpu.SemaphoreType.DMA((10,)),
-            pltpu.SemaphoreType.DMA((9,)),
+            pltpu.VMEM((ROWS, D), F32),
+            pltpu.SemaphoreType.DMA((11,)),
+            pltpu.SemaphoreType.DMA((11,)),
         ],
         compiler_params=params(),
         name="feed",
-    )(spot, lens, middle, h, mixed, weights, ln, cot, late)
+    )(lens, middle, h, ln, cot, mixed, late)
 
 
 def norm_back_kernel(x_ref, dx_ref, dh_ref, ln_ref, dtok_ref):
@@ -763,7 +802,7 @@
         in_specs=[VM] * 4,
         out_specs=(VM,) * 5,
         scratch_shapes=[pltpu.VMEM((TAIL, 128), F32)],
-        compiler_params=params(),
+        compiler_params=params(16),
         name="finish",
     )(*slabs)
 
@@ -789,7 +828,7 @@
         in_specs=[VM],
         out_specs=(VM, VM, VM),
         scratch_shapes=[pltpu.VMEM((WHOLE, 128), F32)],
-        compiler_params=params(),
+        compiler_params=params(16),
         name="unpack",
     )(late)
 
@@ -807,7 +846,7 @@
         out_shape=(piece,) * 4,
         in_specs=[VM],
         out_specs=(VM,) * 4,
-        compiler_params=params(),
+        compiler_params=params(16),
         name="fold",
     )(slabs)
 
@@ -816,25 +855,36 @@
     return lax.all_to_all(slabs, AXES, 0, 0, axis_index_groups=peer_groups(dims), tiled=True)
 
 
-def along_z(ahead):
-    return [
-        (device_number(x, y, z, c), device_number(x, y, (z + ahead) % 4, c))
-        for x, y, z, c in itertools.product(range(4), range(4), range(4), range(2))
-    ]
+def shift(values, dim, ahead):
+    pairs = []
+    for x, y, z, c in itertools.product(range(4), range(4), range(4), range(2)):
+        to = dict(x=x, y=y, z=z)
+        to[dim] = (to[dim] + ahead) % 4
+        pairs.append((device_number(x, y, z, c), device_number(to["x"], to["y"], to["z"], c)))
+    return lax.ppermute(values, AXES, pairs)
+
+
+def ring(own, dim):
+    return jnp.concatenate([own] + [shift(own, dim, ahead) for ahead in (1, 2, 3)], axis=0)
+
+
+def wide_ring(own, dim):
+    half = own.shape[0] // 2
+    near, last = shift(own, dim, 1), shift(own, dim, -1)
+    far = [shift(near[:half], dim, 1), shift(last[half:], dim, -1)]
+    return jnp.concatenate([own, near, *far, last], axis=0)
 
 
 def copies_of_peers(own):
-    ring = [own] + [lax.ppermute(own, AXES, along_z(ahead)) for ahead in (1, 2, 3)]
-    ring = jnp.concatenate(ring, axis=0)
-    return exchange(jnp.broadcast_to(ring, (16, *ring.shape)), "yx").reshape(PEERS, *own.shape)
+    return wide_ring(ring(ring(own, "z"), "x"), "y").reshape(PEERS, *own.shape)
 
 
 def sum_over_peers(own, other):
     received = lax.ppermute(other, AXES, core_pairs())
     slab = (own.astype(F32) + received.astype(F32)).astype(BF)
-    pieces = fold(exchange(slab.reshape(16, 4 * TAIL, 128), "yx"))
+    pieces = fold(exchange(slab.reshape(16, 4 * TAIL, 128), "zx"))
     return [pieces[0]] + [
-        lax.ppermute(piece, AXES, along_z(-back)) for back, piece in enumerate(pieces) if back
+        shift(piece, "y", -back) for back, piece in enumerate(pieces) if back
     ]
 
 
@@ -851,34 +901,34 @@
     down_weight,
     cotangent,
 ):
-    spot = jnp.stack([lax.axis_index("wide") & 1, lax.axis_index("narrow") & 3])
-    spot = spot.astype(I32).reshape(1, 2)
+    wide, narrow = lax.axis_index("wide"), lax.axis_index("narrow")
+    spot = jnp.stack([wide & 1, narrow & 3, (narrow >> 2) * 2 + (wide >> 3), (wide >> 1) & 3])
+    spot = spot.astype(I32).reshape(1, 4)
     early, late = pack(
         ln1_gain, ln1_bias, qkv_weight, out_weight, ln2_gain, ln2_bias, up_weight.T, down_weight
     )
-    late = lax.all_gather(late, AXES, axis_index_groups=peer_groups("zcyx"))
+    late = lax.all_gather(late, AXES, axis_index_groups=peer_groups("yczx"))
     early_own = copies_of_peers(early)
     early_oth = lax.ppermute(early_own, AXES, core_pairs())
-    ht, qkv, weights, norms = project(spot, tokens, early_own, early_oth)
-    mixed, middle, h_two, penalty, log_totals = attend(
-        spot, seq_lengths, tokens, qkv, weights, norms
+    ht, qkv, weights, norms, mixed, middle, h_two, penalty, log_totals = front(
+        spot, seq_lengths, tokens, early_own, early_oth
     )
-    output, late_grad, dx, upstream, vectors = feed(
-        spot, seq_lengths, middle, h_two, mixed, weights, norms, cotangent, late
+    output, late_grad, dx, vectors = feed(
+        seq_lengths, middle, h_two, norms, cotangent, mixed, late
     )
     late_grad = lax.psum_scatter(
         late_grad.reshape(128 * WHOLE, 128),
         AXES,
         scatter_dimension=0,
-        axis_index_groups=peer_groups("zc"),
+        axis_index_groups=peer_groups("yc"),
         tiled=True,
     )
     oth, own, dh_one = back(
-        spot, seq_lengths, tokens, upstream, vectors, qkv, penalty, log_totals, weights, ht
+        spot, seq_lengths, dx, vectors, qkv, penalty, log_totals, weights, ht, tokens
     )
     tail = sum_over_peers(own, oth)
     dtokens = norm_back(tokens, dx, dh_one, norms)
-    late_grad = exchange(late_grad.reshape(16, WHOLE, 128), "yx")
+    late_grad = exchange(late_grad.reshape(16, WHOLE, 128), "zx")
     qkv_grad, g1_grad, b1_grad, g2_grad, b2_grad = finish(tail)
     up_grad, down_grad, out_grad = unpack(late_grad)
     return (

time: 223 us -> 213 us (0.955)
  blocking collectives: 70.1 us -> 32 us
  waiting for transfers between devices: 22.5 us -> 49.7 us
  starting transfers between devices: 14.4 us -> 28 us
  Pallas kernels: 94.1 us -> 81.9 us
    all_to_all x2 -> x1, blocking collectives: 70.1 us -> 32 us  [exchange(): lax.all_to_all(slabs, AXES, 0, 0, axis_index_groups=peer_groups(dims), ti...]
    ppermute x6 -> x13, waiting for transfers between devices: 4.91 us -> 28.3 us  [shift(): return lax.ppermute(values, AXES, pairs)]
    ppermute x6 -> x13, starting transfers between devices: 7.53 us -> 20.5 us  [shift(): return lax.ppermute(values, AXES, pairs)]
    pallas_call x3 -> x2, Pallas kernels: 56.1 us -> 49.1 us  [the longest x1 25.1 us: feed(): pl.pallas_call(feed_kernel, out_shape=(jax.ShapeDtypeStruct((ROWS, D), BF...]
    all_to_all x1, waiting for transfers between devices: 9.52 us -> 13.3 us  [exchange(): lax.all_to_all(slabs, AXES, 0, 0, axis_index_groups=peer_groups(dims), ti...]
  transfers between devices with their start and end apart: 11 -> 18, of which waited for: 7 -> 9; matrix products, arithmetic and copies ran while one was open for 2% -> 2% of each run, Pallas kernels for 29% -> 26%
where the time goes in v3:
time: 213 us; the launch traced here: 210 us
  Pallas kernels  81.9 us (38%)
  waiting for transfers between devices  49.7 us (23%)
  blocking collectives  32 us (15%)
  starting transfers between devices  28 us (13%)
  between operations  14.2 us (7%)
  other arithmetic  2.9 us (1%)
    all_to_all x1, blocking collectives, exchange(): lax.all_to_all(slabs, AXES, 0, 0, axis_index_groups=peer_groups(dims), ti...  32 us
    ppermute x13, waiting for transfers between devices, shift(): return lax.ppermute(values, AXES, pairs)  28.3 us
    pallas_call x1, Pallas kernels, back(): pl.pallas_call(back_kernel, out_shape=(slab, slab, jax.ShapeDtypeStruct((...  25.1 us
    pallas_call x1, Pallas kernels, feed(): pl.pallas_call(feed_kernel, out_shape=(jax.ShapeDtypeStruct((ROWS, D), BF...  25.1 us
    pallas_call x1, Pallas kernels, front(): pl.pallas_call(front_kernel, out_shape=(jax.ShapeDtypeStruct((D, ROWS), B...  24 us
    ppermute x13, starting transfers between devices, shift(): return lax.ppermute(values, AXES, pairs)  20.5 us
    all_to_all x1, waiting for transfers between devices, exchange(): lax.all_to_all(slabs, AXES, 0, 0, axis_index_groups=peer_groups(dims), ti...  13.3 us
    all_to_all x1, starting transfers between devices, exchange(): lax.all_to_all(slabs, AXES, 0, 0, axis_index_groups=peer_groups(dims), ti...  6.93 us
  transfers between devices with their start and end apart: 18, of which 9 were waited for; matrix products, arithmetic and copies ran while one was open for 2% of the time, Pallas kernels for 26%

profile of v3, /device:TPU:0, one launch (start us, length us, event | category | flops | bytes accessed | tf_op | source)
XLA Modules:
  0.0 210.0 jit_solution(12808659256929728019)
XLA Ops:
  7.2 0.0 all-gather.3.cloned.1.call-start
  7.2 1.6 pack.1
  8.8 0.0 all-gather.3.cloned.1.call-update
  8.8 0.0 reduce-scatter.2.cloned.1.call-start
  8.9 4.2 %collective-permute-start.2 = (bf16[152,128]{1,0:T(8,128)(2,1)}, bf16[152,128]{1,0:T(8,128)(2,1)S(1)}, u32[]{:S(2)}, u32[]{:S(2)}) collective-permute-start(bf16[152,128]{1,0:T(8,128)(2,1)} %get-tuple-element.40), channel_id=1, source_target_pairs={{0,3},{8,11},{1,0},{9,8},{2,1},{10,9},{3,2},{11,10},{16,19},{24,27... | collective-permute-start | bytes 116744 | tf_op jit(solution)/shard_map/ppermute | solution.py:864
  13.1 1.3 collective-permute-start
  14.3 0.8 constant_dynamic-update-slice_fusion.10
  15.2 3.7 %collective-permute-done = bf16[152,128]{1,0:T(8,128)(2,1)S(1)} collective-permute-done((bf16[152,128]{1,0:T(8,128)(2,1)}, bf16[152,128]{1,0:T(8,128)(2,1)S(1)}, u32[]{:S(2)}, u32[]{:S(2)}) %collective-permute-start) | collective-permute-done | bytes 38944 | tf_op jit(solution)/shard_map/ppermute | solution.py:864
  18.9 0.0 collective-permute-done.1
  19.0 1.6 collective-permute-start.3
  20.6 2.7 %collective-permute-start.4 = (bf16[608,128]{1,0:T(8,128)(2,1)S(1)}, bf16[608,128]{1,0:T(8,128)(2,1)S(1)}, u32[]{:S(2)}, u32[]{:S(2)}) collective-permute-start(bf16[608,128]{1,0:T(8,128)(2,1)S(1)} %get-tuple-element.78), channel_id=1, source_target_pairs={{0,4},{8,12},{1,5},{9,13},{2,6},{10,14},{3,7},{11,15},{16,20},{24,... | collective-permute-start | bytes 466952 | tf_op jit(solution)/shard_map/ppermute | solution.py:864
  23.3 1.4 collective-permute-start.5
  24.7 2.5 %collective-permute-done.3 = bf16[608,128]{1,0:T(8,128)(2,1)S(1)} collective-permute-done((bf16[608,128]{1,0:T(8,128)(2,1)S(1)}, bf16[608,128]{1,0:T(8,128)(2,1)S(1)}, u32[]{:S(2)}, u32[]{:S(2)}) %collective-permute-start.3) | collective-permute-done | bytes 155680 | tf_op jit(solution)/shard_map/ppermute | solution.py:864
  27.2 1.9 collective-permute-done.4
  29.2 0.0 collective-permute-done.5
  29.3 3.2 %collective-permute-start.8 = (bf16[2432,128]{1,0:T(8,128)(2,1)S(1)}, bf16[2432,128]{1,0:T(8,128)(2,1)S(1)}, u32[]{:S(2)}, u32[]{:S(2)}) collective-permute-start(bf16[2432,128]{1,0:T(8,128)(2,1)S(1)} %get-tuple-element.70), channel_id=1, source_target_pairs={{0,48},{8,56},{1,49},{9,57},{2,50},{10,58},{3,51},{11,59},{16,0},{... | collective-permute-start | bytes 1867784 | tf_op jit(solution)/shard_map/ppermute | solution.py:864
  32.4 0.0 collective-permute-start.6
  32.4 11.0 %collective-permute-done.8 = bf16[2432,128]{1,0:T(8,128)(2,1)S(1)} collective-permute-done((bf16[2432,128]{1,0:T(8,128)(2,1)S(1)}, bf16[2432,128]{1,0:T(8,128)(2,1)S(1)}, u32[]{:S(2)}, u32[]{:S(2)}) %collective-permute-start.8) | collective-permute-done | bytes 622624 | tf_op jit(solution)/shard_map/ppermute | solution.py:864
  43.4 3.8 %collective-permute-start.9 = (bf16[1216,128]{1,0:T(8,128)(2,1)S(1)}, bf16[1216,128]{1,0:T(8,128)(2,1)S(1)}, u32[]{:S(2)}, u32[]{:S(2)}) collective-permute-start(bf16[1216,128]{1,0:T(8,128)(2,1)S(1)} %slice.9), channel_id=1, source_target_pairs={{0,48},{8,56},{1,49},{9,57},{2,50},{10,58},{3,51},{11,59},{16,0},{... | collective-permute-start | bytes 933896 | tf_op jit(solution)/shard_map/ppermute | solution.py:864
  47.2 0.0 collective-permute-done.6
  47.2 0.1 collective-permute-start.7
  47.3 0.1 constant_dynamic-update-slice_fusion.14
  47.4 9.2 %collective-permute-done.7 = bf16[1216,128]{1,0:T(8,128)(2,1)S(1)} collective-permute-done((bf16[1216,128]{1,0:T(8,128)(2,1)S(1)}, bf16[1216,128]{1,0:T(8,128)(2,1)S(1)}, u32[]{:S(2)}, u32[]{:S(2)}) %collective-permute-start.7) | collective-permute-done | bytes 311328 | tf_op jit(solution)/shard_map/ppermute | solution.py:864
  56.7 0.0 collective-permute-done.9
  56.7 0.1 constant_dynamic-update-slice_fusion.11
  56.8 0.3 collective-permute-start.10
  57.1 0.8 add_bitcast_fusion.spot_ref
  57.9 4.0 %collective-permute-done.10.oth_ref = bf16[64,152,128]{2,1,0:T(8,128)(2,1)} collective-permute-done((bf16[64,152,128]{2,1,0:T(8,128)(2,1)S(1)}, bf16[64,152,128]{2,1,0:T(8,128)(2,1)}, u32[]{:S(2)}, u32[]{:S(2)}) %collective-permute-start.10) | collective-permute-done | bytes 2490400 | tf_op jit(solution)/shard_map/ppermute | solution.py:912
  61.9 24.0 %front.1 = (bf16[768,512]{1,0:T(8,128)(2,1)}, bf16[512,2304]{1,0:T(8,128)(2,1)}, bf16[768,3072]{1,0:T(8,128)(2,1)}, f32[8,768]{1,0:T(8,128)}, bf16[512,1024]{1,0...) custom-call(s32[1,4]{1,0:T(1,128)} %add_bitcast_fusion.spot_ref, ...), custom_call_target="tpu_custom_call" | custom-call | tf_op jit(solution)/shard_map/front/pallas_call | solution.py:369
  85.9 0.0 all-gather.3.cloned.1.call-done
  86.0 25.1 %feed.1 = (bf16[512,768]{1,0:T(8,128)(2,1)}, bf16[128,336,128]{2,1,0:T(8,128)(2,1)}, f32[512,768]{1,0:T(8,128)}, f32[8,768]{1,0:T(8,128)}) custom-call(s32[1,4]{1,0:T(1,128)} %lens_ref.5, f32[512,768]{1,0:T(8,128)} %get-tuple-element.41.middle_ref, bf16[512,768]{1,0:T(8,128)(2,1)} %get-tuple-element.42.h_ref, f32[8,768]{1,0:T(8,128)} %get-tuple-element.43.ln_ref, ...), custom_call_target="tpu_custom_call" | custom-call | tf_op jit(solution)/shard_map/feed/pallas_call | solution.py:730
  111.1 0.0 reduce-scatter.2.cloned.1.call-update
  111.1 25.1 %back.1 = (bf16[64,112,128]{2,1,0:T(8,128)(2,1)}, bf16[64,112,128]{2,1,0:T(8,128)(2,1)}, f32[512,768]{1,0:T(8,128)}) custom-call(s32[1,4]{1,0:T(1,128)} %add_bitcast_fusion.spot_ref, s32[1,4]{1,0:T(1,128)} %lens_ref.5, f32[512,768]{1,0:T(8,128)} %get-tuple-element.47.dx_ref, f32[8,768]{1,0:T(8,128)} %get-tuple-element.48.vec_ref, ...), custom_call_target="tpu_custom_call" | custom-call | tf_op jit(solution)/shard_map/back/pallas_call | solution.py:558
  136.2 0.2 collective-permute-start.11
  136.4 3.9 %collective-permute-done.11 = bf16[64,112,128]{2,1,0:T(8,128)(2,1)S(1)} collective-permute-done((bf16[64,112,128]{2,1,0:T(8,128)(2,1)}, bf16[64,112,128]{2,1,0:T(8,128)(2,1)S(1)}, u32[]{:S(2)}, u32[]{:S(2)}) %collective-permute-start.11) | collective-permute-done | bytes 1835040 | tf_op jit(solution)/shard_map/ppermute | solution.py:883
  140.3 2.1 add_convert_fusion
  142.3 32.0 %all_to_all.10.slabs_ref = bf16[16,448,128]{2,1,0:T(8,128)(2,1)S(1)} all-to-all(bf16[16,448,128]{2,1,0:T(8,128)(2,1)S(1)} %bitcast.23), channel_id=1, replica_groups={{0,64,4,68,1,65,5,69,2,66,6,70,3,67,7,71},{8,72,12,76,9,73,13,77,10,74,..., dimensions={0} | all-to-all | bytes 3670016 | tf_op jit(solution)/shard_map/all_to_all | solution.py:855
  174.3 0.1 reduce-scatter.2.cloned.1.call-done
  174.4 6.9 %all-to-all-start.1 = ((bf16[16,336,128]{2,1,0:T(8,128)(2,1)}), bf16[16,336,128]{2,1,0:T(8,128)(2,1)S(1)}, u32[]{:S(2)}, u32[]{:S(2)}) async-start(bf16[16,336,128]{2,1,0:T(8,128)(2,1)} %bitcast.26), calls=%async_computation.2 | async-start | bytes 2752512 | tf_op jit(solution)/shard_map/all_to_all | solution.py:855
  181.4 0.2 fold.1
  181.6 0.9 collective-permute-start.12
  182.5 0.5 collective-permute-start.13
  183.0 0.9 collective-permute-start.14
  183.9 4.3 %norm_back.1 = bf16[512,768]{1,0:T(8,128)(2,1)} custom-call(bf16[512,768]{1,0:T(8,128)(2,1)} %x_ref.3, f32[512,768]{1,0:T(8,128)} %get-tuple-element.47.dx_ref, f32[512,768]{1,0:T(8,128)} %get-tuple-element.54.dh_ref, f32[8,768]{1,0:T(8,128)} %get-tuple-element.43.ln_ref), custom_call_target="tpu_custom_call" | custom-call | tf_op jit(solution)/shard_map/norm_back/pallas_call | solution.py:772
  188.2 0.0 collective-permute-done.12.refs_1_
  188.2 0.7 finish.1
  188.9 13.3 %all-to-all-done.1.late_ref = bf16[16,336,128]{2,1,0:T(8,128)(2,1)S(1)} async-done(((bf16[16,336,128]{2,1,0:T(8,128)(2,1)}), bf16[16,336,128]{2,1,0:T(8,128)(2,1)S(1)}, u32[]{:S(2)}, u32[]{:S(2)}) %all-to-all-start.1) | async-done | bytes 1376288 | tf_op jit(solution)/shard_map/all_to_all | solution.py:855
  202.2 0.9 unpack.1
  (16 shorter events, 0.4 us)
Async XLA Ops:
  7.2 78.8 %all-gather.3.cloned.1.call-start = ((), (), s32[]{:S(2)}) async-start(), calls=%async_computation.4 | async-start | bytes 9510912 | tf_op jit(solution)/shard_map/all_gather | solution.py:910
  8.8 165.6 %reduce-scatter.2.cloned.1.call-start = ((), (), s32[]{:S(2)}) async-start(), calls=%async_computation.3 | async-start | bytes 12386304 | tf_op jit(solution)/shard_map/reduce_scatter | solution.py:919
  8.9 10.1 %collective-permute-start.2 = (bf16[152,128]{1,0:T(8,128)(2,1)}, bf16[152,128]{1,0:T(8,128)(2,1)S(1)}, u32[]{:S(2)}, u32[]{:S(2)}) collective-permute-start(bf16[152,128]{1,0:T(8,128)(2,1)} %get-tuple-element.40), channel_id=1, source_target_pairs={{0,3},{8,11},{1,0},{9,8},{2,1},{10,9},{3,2},{11,10},{16,19},{24,27... | collective-permute-start | bytes 116744 | tf_op jit(solution)/shard_map/ppermute | solution.py:864
  13.1 5.8 %collective-permute-start.1 = (bf16[152,128]{1,0:T(8,128)(2,1)}, bf16[152,128]{1,0:T(8,128)(2,1)S(1)}, u32[]{:S(2)}, u32[]{:S(2)}) collective-permute-start(bf16[152,128]{1,0:T(8,128)(2,1)} %get-tuple-element.40), channel_id=1, source_target_pairs={{0,2},{8,10},{1,3},{9,11},{2,0},{10,8},{3,1},{11,9},{16,18},{24,26... | collective-permute-start | bytes 116744 | tf_op jit(solution)/shard_map/ppermute | solution.py:864
  13.1 5.8 %collective-permute-start = (bf16[152,128]{1,0:T(8,128)(2,1)}, bf16[152,128]{1,0:T(8,128)(2,1)S(1)}, u32[]{:S(2)}, u32[]{:S(2)}) collective-permute-start(bf16[152,128]{1,0:T(8,128)(2,1)} %get-tuple-element.40), channel_id=1, source_target_pairs={{0,1},{8,9},{1,2},{9,10},{2,3},{10,11},{3,0},{11,8},{16,17},{24,25... | collective-permute-start | bytes 116744 | tf_op jit(solution)/shard_map/ppermute | solution.py:864
  19.0 8.2 %collective-permute-start.3 = (bf16[608,128]{1,0:T(8,128)(2,1)S(1)}, bf16[608,128]{1,0:T(8,128)(2,1)S(1)}, u32[]{:S(2)}, u32[]{:S(2)}) collective-permute-start(bf16[608,128]{1,0:T(8,128)(2,1)S(1)} %get-tuple-element.78), channel_id=1, source_target_pairs={{0,64},{8,72},{1,65},{9,73},{2,66},{10,74},{3,67},{11,75},{16,80},... | collective-permute-start | bytes 466952 | tf_op jit(solution)/shard_map/ppermute | solution.py:864
  20.6 8.6 %collective-permute-start.4 = (bf16[608,128]{1,0:T(8,128)(2,1)S(1)}, bf16[608,128]{1,0:T(8,128)(2,1)S(1)}, u32[]{:S(2)}, u32[]{:S(2)}) collective-permute-start(bf16[608,128]{1,0:T(8,128)(2,1)S(1)} %get-tuple-element.78), channel_id=1, source_target_pairs={{0,4},{8,12},{1,5},{9,13},{2,6},{10,14},{3,7},{11,15},{16,20},{24,... | collective-permute-start | bytes 466952 | tf_op jit(solution)/shard_map/ppermute | solution.py:864
  23.3 5.9 %collective-permute-start.5 = (bf16[608,128]{1,0:T(8,128)(2,1)S(1)}, bf16[608,128]{1,0:T(8,128)(2,1)S(1)}, u32[]{:S(2)}, u32[]{:S(2)}) collective-permute-start(bf16[608,128]{1,0:T(8,128)(2,1)S(1)} %get-tuple-element.78), channel_id=1, source_target_pairs={{0,68},{8,76},{1,69},{9,77},{2,70},{10,78},{3,71},{11,79},{16,84},... | collective-permute-start | bytes 466952 | tf_op jit(solution)/shard_map/ppermute | solution.py:864
  29.3 14.1 %collective-permute-start.8 = (bf16[2432,128]{1,0:T(8,128)(2,1)S(1)}, bf16[2432,128]{1,0:T(8,128)(2,1)S(1)}, u32[]{:S(2)}, u32[]{:S(2)}) collective-permute-start(bf16[2432,128]{1,0:T(8,128)(2,1)S(1)} %get-tuple-element.70), channel_id=1, source_target_pairs={{0,48},{8,56},{1,49},{9,57},{2,50},{10,58},{3,51},{11,59},{16,0},{... | collective-permute-start | bytes 1867784 | tf_op jit(solution)/shard_map/ppermute | solution.py:864
  32.4 14.8 %collective-permute-start.6 = (bf16[2432,128]{1,0:T(8,128)(2,1)S(1)}, bf16[2432,128]{1,0:T(8,128)(2,1)S(1)}, u32[]{:S(2)}, u32[]{:S(2)}) collective-permute-start(bf16[2432,128]{1,0:T(8,128)(2,1)S(1)} %get-tuple-element.70), channel_id=1, source_target_pairs={{0,16},{8,24},{1,17},{9,25},{2,18},{10,26},{3,19},{11,27},{16,32},... | collective-permute-start | bytes 1867784 | tf_op jit(solution)/shard_map/ppermute | solution.py:864
  43.4 13.2 %collective-permute-start.9 = (bf16[1216,128]{1,0:T(8,128)(2,1)S(1)}, bf16[1216,128]{1,0:T(8,128)(2,1)S(1)}, u32[]{:S(2)}, u32[]{:S(2)}) collective-permute-start(bf16[1216,128]{1,0:T(8,128)(2,1)S(1)} %slice.9), channel_id=1, source_target_pairs={{0,48},{8,56},{1,49},{9,57},{2,50},{10,58},{3,51},{11,59},{16,0},{... | collective-permute-start | bytes 933896 | tf_op jit(solution)/shard_map/ppermute | solution.py:864
  47.2 9.4 %collective-permute-start.7 = (bf16[1216,128]{1,0:T(8,128)(2,1)S(1)}, bf16[1216,128]{1,0:T(8,128)(2,1)S(1)}, u32[]{:S(2)}, u32[]{:S(2)}) collective-permute-start(bf16[1216,128]{1,0:T(8,128)(2,1)S(1)} %slice.8), channel_id=1, source_target_pairs={{0,16},{8,24},{1,17},{9,25},{2,18},{10,26},{3,19},{11,27},{16,32},... | collective-permute-start | bytes 933896 | tf_op jit(solution)/shard_map/ppermute | solution.py:864
  56.8 5.1 %copy-start = (bf16[9728,128]{1,0:T(8,128)(2,1)}, bf16[9728,128]{1,0:T(8,128)(2,1)S(1)}, u32[]{:S(2)}) copy-start(bf16[9728,128]{1,0:T(8,128)(2,1)S(1)} %constant_dynamic-update-slice_fusion.11) | copy-start | bytes 7471108
  56.8 5.1 %collective-permute-start.10 = (bf16[64,152,128]{2,1,0:T(8,128)(2,1)S(1)}, bf16[64,152,128]{2,1,0:T(8,128)(2,1)}, u32[]{:S(2)}, u32[]{:S(2)}) collective-permute-start(bf16[64,152,128]{2,1,0:T(8,128)(2,1)S(1)} %bitcast.24), channel_id=1, source_target_pairs={{0,8},{8,0},{1,9},{9,1},{2,10},{10,2},{3,11},{11,3},{16,24},{24,16... | collective-permute-start | bytes 7471112 | tf_op jit(solution)/shard_map/ppermute | solution.py:912
  136.2 4.1 %collective-permute-start.11 = (bf16[64,112,128]{2,1,0:T(8,128)(2,1)}, bf16[64,112,128]{2,1,0:T(8,128)(2,1)S(1)}, u32[]{:S(2)}, u32[]{:S(2)}) collective-permute-start(bf16[64,112,128]{2,1,0:T(8,128)(2,1)} %get-tuple-element.56), channel_id=1, source_target_pairs={{0,8},{8,0},{1,9},{9,1},{2,10},{10,2},{3,11},{11,3},{16,24},{24,16... | collective-permute-start | bytes 5505032 | tf_op jit(solution)/shard_map/ppermute | solution.py:883
  174.4 27.8 %all-to-all-start.1 = ((bf16[16,336,128]{2,1,0:T(8,128)(2,1)}), bf16[16,336,128]{2,1,0:T(8,128)(2,1)S(1)}, u32[]{:S(2)}, u32[]{:S(2)}) async-start(bf16[16,336,128]{2,1,0:T(8,128)(2,1)} %bitcast.26), calls=%async_computation.2 | async-start | bytes 2752512 | tf_op jit(solution)/shard_map/all_to_all | solution.py:855
  181.6 6.6 %collective-permute-start.12 = (bf16[112,128]{1,0:T(8,128)(2,1)S(1)}, bf16[112,128]{1,0:T(8,128)(2,1)S(1)}, u32[]{:S(2)}, u32[]{:S(2)}) collective-permute-start(bf16[112,128]{1,0:T(8,128)(2,1)S(1)} %get-tuple-element.58), channel_id=1, source_target_pairs={{0,48},{8,56},{1,49},{9,57},{2,50},{10,58},{3,51},{11,59},{16,0},{... | collective-permute-start | bytes 86024 | tf_op jit(solution)/shard_map/ppermute | solution.py:864
  182.5 5.7 %collective-permute-start.13 = (bf16[112,128]{1,0:T(8,128)(2,1)S(1)}, bf16[112,128]{1,0:T(8,128)(2,1)S(1)}, u32[]{:S(2)}, u32[]{:S(2)}) collective-permute-start(bf16[112,128]{1,0:T(8,128)(2,1)S(1)} %get-tuple-element.59), channel_id=1, source_target_pairs={{0,32},{8,40},{1,33},{9,41},{2,34},{10,42},{3,35},{11,43},{16,48},... | collective-permute-start | bytes 86024 | tf_op jit(solution)/shard_map/ppermute | solution.py:864
  183.0 5.2 %collective-permute-start.14 = (bf16[112,128]{1,0:T(8,128)(2,1)S(1)}, bf16[112,128]{1,0:T(8,128)(2,1)S(1)}, u32[]{:S(2)}, u32[]{:S(2)}) collective-permute-start(bf16[112,128]{1,0:T(8,128)(2,1)S(1)} %get-tuple-element.60), channel_id=1, source_target_pairs={{0,16},{8,24},{1,17},{9,25},{2,18},{10,26},{3,19},{11,27},{16,32},... | collective-permute-start | bytes 86024 | tf_op jit(solution)/shard_map/ppermute | solution.py:864
Sparse Core Ops, SparseCore 0:
  11.4 73.8 all-gather.2
  111.2 63.1 reduce-scatter.1

commit v4 on v3

--- a/solution.py
+++ b/solution.py
@@ -23,10 +23,9 @@
 GATHERED = OUTER + OWN * BLOCKS
 EARLY = 152
 LATE = 48
-WHOLE = 336
-TAIL = 112
+WHOLE = 288
+TAIL = 152
 STEP = TAIL + 1
-WIDE = 128 * 8
 EPS = 1e-05
 FAR = 1e30
 TANH_SCALE = 0.7978845608028654
@@ -52,6 +51,16 @@
     return groups
 
 
+def mixed_groups(first, second):
+    halves = [peer_groups(dims) for dims in (first, second)]
+    return [
+        group
+        for core, groups in enumerate(halves)
+        for group in groups
+        if (group[0] >> 3) & 1 == core
+    ]
+
+
 def core_pairs():
     return [
         (device_number(x, y, z, c), device_number(x, y, z, 1 - c))
@@ -85,9 +94,10 @@
 
 
 def owner(group, core, spot):
-    y = (spot[3] - (group >> 4)) & 3
+    far, near = group >> 4, group & 3
+    y = (spot[3] - (far + core * (near - far))) & 3
     x = (spot[2] - (group >> 2)) & 3
-    z = (spot[1] - group) & 3
+    z = (spot[1] - (near + core * (far - near))) & 3
     return ((x & 1) << 6) + (y << 4) + (core << 3) + ((x >> 1) << 2) + z
 
 
@@ -111,21 +121,6 @@
     side = spot[0] + other - 2 * spot[0] * other
     feature = owner(inner & (PEERS - 1), side, spot) * OWN + (inner >> 6)
     return one_hot(iota((D, D), 1) == feature)
-
-
-def late_owner(group):
-    y = group >> 5
-    c = (group >> 4) & 1
-    z = (group >> 2) & 3
-    x = group & 3
-    return ((x & 1) << 6) + (y << 4) + (c << 3) + ((x >> 1) << 2) + z
-
-
-def place_late():
-    slot = iota((1, WIDE), 1)
-    inner = slot & 7
-    feature = jnp.where(inner < OWN, late_owner(slot >> 3) * OWN + inner, -1)
-    return one_hot(iota((D, WIDE), 0) == feature)
 
 
 def vector_lanes(which):
@@ -262,8 +257,8 @@
 
 def front_kernel(
     spot_ref, lens_ref, x_ref, own_ref, oth_ref,
-    ht_ref, qkv_ref, w_ref, ln_ref, mixed_ref, middle_ref, h_ref, pen_ref, lse_ref,
-    rows_s, w, h_s, qkv, pen, attn_s, carry, sems,
+    ht_ref, qkv_ref, w_ref, ln_ref, mixed_ref, middle_ref, h_ref, soft_ref,
+    rows_s, w, h_s, qkv, pen, soft_s, attn_s, carry, sems,
 ):
     spot = tuple(spot_ref[0, at] for at in range(4))
     core = spot[0]
@@ -324,8 +319,9 @@
         sums = dot_nn(high, before) + dot_nn(low, before)
         pen[:count, rows] = jnp.where(allowed, sums[:, 0:128] + carry[:count, :], FAR)
         carry[:count, :] = carry[:count, :] + sums[:, 128:256]
-    store_pen = pltpu.make_async_copy(pen, pen_ref, sems.at[2])
-    store_pen.start()
+
+    def store_soft(pair):
+        return pltpu.make_async_copy(soft_s.at[pair], soft_ref.at[pair], sems.at[2])
 
     @pl.loop(0, 3)
     def _(turn):
@@ -341,15 +337,15 @@
                 top = jnp.max(shifted, axis=0, keepdims=True)
                 exponent = jnp.exp(shifted - top)
                 total = jnp.sum(exponent, axis=0, keepdims=True)
-                mixed = dot_tn(v, exponent.astype(BF)) * (1.0 / total)
+                soft = (exponent * (1.0 / total)).astype(BF)
+                soft_s[pair, :count, block * 256 : block * 256 + 256] = soft
                 lanes = pl.ds(pl.multiple_of(pair * 128, 128), 128)
-                attn_s[lanes, rows] = own_halves(mixed).astype(BF)
-                log_total = top + jnp.log(total)
-                lse_ref[pair, 0:1, rows] = log_total[:, 0:128]
-                lse_ref[pair, 1:2, rows] = log_total[:, 128:256]
-
-    mixed = dot_tn(attn_s[...], place).astype(BF)
-    middle_ref[...] = dot_nn(mixed, w[:, 3 * D : 4 * D])
+                attn_s[lanes, rows] = own_halves(dot_tn(v, soft)).astype(BF)
+        store_soft(2 * turn).start()
+        store_soft(2 * turn + 1).start()
+
+    mixed_ref[...] = dot_tn(attn_s[...], place).astype(BF)
+    middle_ref[...] = dot_nn(mixed_ref[...], w[:, 3 * D : 4 * D])
 
     @pl.loop(0, 4)
     def _(block):
@@ -359,9 +355,8 @@
         unit, _ = norm_stats(middle)
         h_ref[rows, :] = (unit * ln_ref[2:3, :] + ln_ref[3:4, :]).astype(BF)
 
-    mixed_ref[...] = dot_tn(attn_s[...], place_late()).astype(BF)
     ht_ref[...] = dot_nt(place_transposed(spot), h_s[...]).astype(BF)
-    for store in (store_w, store_qkv, store_pen):
+    for store in (store_w, store_qkv, *(store_soft(pair) for pair in range(6))):
         store.wait()
 
 
@@ -373,20 +368,20 @@
             jax.ShapeDtypeStruct((ROWS, 3 * D), BF),
             jax.ShapeDtypeStruct((D, 4 * D), BF),
             jax.ShapeDtypeStruct((8, D), F32),
-            jax.ShapeDtypeStruct((ROWS, WIDE), BF),
+            jax.ShapeDtypeStruct((ROWS, D), BF),
             jax.ShapeDtypeStruct((ROWS, D), F32),
             jax.ShapeDtypeStruct((ROWS, D), BF),
-            jax.ShapeDtypeStruct((ROWS, ROWS), F32),
-            jax.ShapeDtypeStruct((6, 8, ROWS), F32),
+            jax.ShapeDtypeStruct((6, ROWS, 1024), BF),
         ),
         in_specs=[SM, SM, VM, VM, VM],
-        out_specs=(VM, ANY, ANY, VM, VM, VM, VM, ANY, VM),
+        out_specs=(VM, ANY, ANY, VM, VM, VM, VM, ANY),
         scratch_shapes=[
             pltpu.VMEM((PEERS * (EARLY + 1), 128), F32),
             pltpu.VMEM((D, 4 * D), BF),
             pltpu.VMEM((ROWS, D), BF),
             pltpu.VMEM((ROWS, 3 * D), BF),
             pltpu.VMEM((ROWS, ROWS), F32),
+            pltpu.VMEM((6, ROWS, 1024), BF),
             pltpu.VMEM((D, ROWS), BF),
             pltpu.VMEM((ROWS, 128), F32),
             pltpu.SemaphoreType.DMA((3,)),
@@ -405,27 +400,26 @@
             sums.append(part)
 
 
-def back_pairs(pairs, qkv, up, pen, lse, total, grads, kept):
+def back_pairs(pairs, qkv, up, weights, total, grads, kept):
     scale = jnp.asarray(0.125, BF)
     dk = [[] for _ in pairs]
     dv = [[] for _ in pairs]
     for block in range(4):
         count = (block + 1) * 128
         rows = slice(block * 128, count)
-        penalty = twice(pen[:count, rows])
         gathered = total[:count, rows]
         for at, pair in enumerate(pairs):
             k = qkv[:count, lanes_of(pair, 1)]
             v = qkv[:count, lanes_of(pair, 2)]
             q = side_by_side(qkv[rows, lanes_of(pair, 0)] * scale)
             u = side_by_side(up[rows, pl.ds(pl.multiple_of(pair * 128, 128), 128)])
-            log_total = jnp.concatenate([lse[pair, 0:1, rows], lse[pair, 1:2, rows]], axis=1)
-            soft = jnp.exp(dot_nt(k, q) - penalty - log_total)
+            low_soft = weights[pair, :count, block * 256 : block * 256 + 256]
+            soft = low_soft.astype(F32)
             pulled = dot_nt(v, u)
             inner = jnp.sum(pulled * soft, axis=0, keepdims=True)
             dz = soft * (pulled - inner)
             gathered = gathered + (dz[:, 0:128] + dz[:, 128:256])
-            add_blocks(dv[at], dot_nn(soft.astype(BF), u))
+            add_blocks(dv[at], dot_nn(low_soft, u))
             if kept is not None and at == 0:
                 kept[block, :count, :] = dz
             else:
@@ -471,11 +465,58 @@
         ]
 
 
+def middle_kernel(
+    spot_ref, lens_ref, cot_ref, middle_ref, dh_ref, ln_ref, w_hbm,
+    dx_ref, low_ref, up_ref, vec_ref, w, sem,
+):
+    spot = tuple(spot_ref[0, at] for at in range(4))
+    load = pltpu.make_async_copy(w_hbm.at[:, 3 * D : 4 * D], w, sem)
+    load.start()
+    ends = group_ends(lens_ref)
+    vec_ref[...] = jnp.zeros_like(vec_ref)
+    gain = ln_ref[2:3, :]
+
+    @pl.loop(0, 4)
+    def _(block):
+        rows = pl.ds(pl.multiple_of(block * 128, 128), 128)
+        unit, inverse = norm_stats(middle_ref[rows, :])
+        gradient = dh_ref[rows, :]
+        vec_ref[2:3, :] = vec_ref[2:3, :] + jnp.sum(gradient * unit, axis=0, keepdims=True)
+        vec_ref[3:4, :] = vec_ref[3:4, :] + jnp.sum(gradient, axis=0, keepdims=True)
+        live = (iota((128, 1), 0) + block * 128) < ends[3]
+        dy = jnp.where(live, cot_ref[rows, :].astype(F32), 0.0)
+        moved = dy + norm_pull(gradient, unit, inverse, gain)
+        dx_ref[rows, :] = moved
+        low_ref[rows, :] = moved.astype(BF)
+
+    load.wait()
+    placed = dot_nt(low_ref[...], w[...]).astype(BF)
+    up_ref[...] = dot_nt(placed, place_matrix(spot)).astype(BF)
+
+
+def middle_back(spot, lens, cot, middle, dh, norms, weights):
+    low = jax.ShapeDtypeStruct((ROWS, D), BF)
+    return pl.pallas_call(
+        middle_kernel,
+        out_shape=(
+            jax.ShapeDtypeStruct((ROWS, D), F32),
+            low,
+            low,
+            jax.ShapeDtypeStruct((8, D), F32),
+        ),
+        in_specs=[SM, SM] + [VM] * 4 + [ANY],
+        out_specs=(VM,) * 4,
+        scratch_shapes=[pltpu.VMEM((D, D), BF), pltpu.SemaphoreType.DMA],
+        compiler_params=params(),
+        name="middle_back",
+    )(spot, lens, cot, middle, dh, norms, weights)
+
+
 def back_kernel(
-    spot_ref, lens_ref, dx_ref, vec_ref,
-    qkv_hbm, pen_hbm, lse_hbm, w_hbm, ht_hbm, x_hbm,
+    spot_ref, lens_ref, vec_ref, up,
+    qkv_hbm, soft_hbm, w_hbm, ht_hbm, x_hbm, low_hbm, mixed_hbm,
     oth_ref, own_ref, dh_one_ref,
-    qkv, pen, lse, w, ht, x_ref, up,
+    qkv, soft, w, ht, x_ref, low, mixed,
     total, kept, grads, dh_s, vec_s, rows_s, slab_s, sems, out_sems,
 ):
     spot = tuple(spot_ref[0, at] for at in range(4))
@@ -485,36 +526,42 @@
         pltpu.make_async_copy(source, target, sems.at[number])
         for number, (source, target) in enumerate(
             (
-                (w_hbm, w),
                 (qkv_hbm, qkv),
-                (pen_hbm, pen),
-                (lse_hbm, lse),
+                (w_hbm.at[:, 0 : 3 * D], w),
                 (ht_hbm, ht),
                 (x_hbm, x_ref),
+                (low_hbm, low),
+                (mixed_hbm, mixed),
             )
         )
     ]
-    for load in loads:
+
+    def load_soft(pair):
+        return pltpu.make_async_copy(soft_hbm.at[pair], soft.at[pair], sems.at[6 + pair])
+
+    loads[0].start()
+    for pair in (2, 3, 4, 5, 0, 1):
+        load_soft(pair).start()
+    for load in loads[1:]:
         load.start()
     total[...] = jnp.zeros_like(total)
     vec_s[...] = vec_ref[...]
-    place = place_matrix(spot)
     loads[0].wait()
-    placed = dot_nt(dx_ref[...].astype(BF), w[:, 3 * D : 4 * D]).astype(BF)
-    up[...] = dot_nt(placed, place).astype(BF)
-    for load in loads[1:4]:
-        load.wait()
 
     @pl.loop(0, 2)
     def _(turn):
-        back_pairs((2 * turn + 2, 2 * turn + 3), qkv, up, pen, lse, total, grads, None)
-
-    back_pairs((0, 1), qkv, up, pen, lse, total, grads, kept)
+        load_soft(2 * turn + 2).wait()
+        load_soft(2 * turn + 3).wait()
+        back_pairs((2 * turn + 2, 2 * turn + 3), qkv, up, soft, total, grads, None)
+
+    load_soft(0).wait()
+    load_soft(1).wait()
+    back_pairs((0, 1), qkv, up, soft, total, grads, kept)
     back_first(ends, qkv, total, grads, kept)
-    for load in loads[4:]:
+    for load in loads[1:]:
         load.wait()
-    placed = dot_nt(grads[...], w[:, 0 : 3 * D]).astype(BF)
-    dh_s[...] = dot_nt(placed, place)
+    placed = dot_nt(grads[...], w[...]).astype(BF)
+    dh_s[...] = dot_nt(placed, place_matrix(spot))
 
     @pl.loop(0, 4)
     def _(block):
@@ -524,26 +571,32 @@
         vec_s[0:1, :] = vec_s[0:1, :] + jnp.sum(gradient * unit, axis=0, keepdims=True)
         vec_s[1:2, :] = vec_s[1:2, :] + jnp.sum(gradient, axis=0, keepdims=True)
 
-    store_dh = pltpu.make_async_copy(dh_s, dh_one_ref, out_sems.at[2])
-    store_dh.start()
+    stores = [pltpu.make_async_copy(dh_s, dh_one_ref, out_sems.at[2])]
+    stores[0].start()
     vectors = [vec_s[which : which + 1, :] for which in range(4)]
-    stores = [store_dh]
+    outer = dot_tn(mixed[...], low[...])
     for half, target in ((1, oth_ref), (0, own_ref)):
         side = core if half == 0 else 1 - core
         slots = slice(half * HALF, half * HALF + HALF)
-        for part in range(3):
-            piece = dot_nn(ht[slots, :], grads[:, part * D : part * D + D])
+        for part in range(4):
+            if part < 3:
+                piece = dot_nn(ht[slots, :], grads[:, part * D : part * D + D])
+            else:
+                piece = outer[slots]
             for block in range(BLOCKS):
                 start = (part * BLOCKS + block) * OWN
                 put_rows(rows_s, piece[:, block * 128 : block * 128 + 128], start)
-        rows_s[pl.ds(OUTER, PEERS, stride=STEP), :] = pack_vectors(vectors, side, spot)
+        rows_s[pl.ds(GATHERED, PEERS, stride=STEP), :] = pack_vectors(vectors, side, spot)
+        for spare in range(GATHERED + 1, TAIL):
+            rows_s[pl.ds(spare, PEERS, stride=STEP), :] = jnp.zeros((PEERS, 128), F32)
 
         @pl.loop(0, 8)
         def _(block):
             for peer in range(8):
                 group = block * 8 + peer
-                z, x = (spot[1] - group) & 3, (spot[2] - (group >> 2)) & 3
-                to = z * 16 + x * 4 + (group >> 4)
+                first = (spot[3] + side * (spot[1] - spot[3]) - (group >> 4)) & 3
+                second = (spot[1] + side * (spot[3] - spot[1]) - group) & 3
+                to = first * 16 + second * 4 + ((spot[2] - (group >> 2)) & 3)
                 slab_s[half, to] = rows_s[pl.ds(group * STEP, TAIL), :].astype(BF)
 
         store = pltpu.make_async_copy(slab_s.at[half], target, out_sems.at[half])
@@ -553,19 +606,19 @@
         store.wait()
 
 
-def back(spot, lens, dx, vec, qkv, pen, lse, weights, ht, x):
+def back(spot, lens, vec, up, qkv, soft, weights, ht, x, low, mixed):
     slab = jax.ShapeDtypeStruct((PEERS, TAIL, 128), BF)
     return pl.pallas_call(
         back_kernel,
         out_shape=(slab, slab, jax.ShapeDtypeStruct((ROWS, D), F32)),
-        in_specs=[SM, SM, VM, VM] + [ANY] * 6,
+        in_specs=[SM, SM, VM, VM] + [ANY] * 7,
         out_specs=(ANY,) * 3,
         scratch_shapes=[
             pltpu.VMEM((ROWS, 3 * D), BF),
-            pltpu.VMEM((ROWS, ROWS), F32),
-            pltpu.VMEM((6, 8, ROWS), F32),
-            pltpu.VMEM((D, 4 * D), BF),
+            pltpu.VMEM((6, ROWS, 1024), BF),
+            pltpu.VMEM((D, 3 * D), BF),
             pltpu.VMEM((D, ROWS), BF),
+            pltpu.VMEM((ROWS, D), BF),
             pltpu.VMEM((ROWS, D), BF),
             pltpu.VMEM((ROWS, D), BF),
             pltpu.VMEM((ROWS, ROWS), F32),
@@ -575,18 +628,17 @@
             pltpu.VMEM((8, D), F32),
             pltpu.VMEM((PEERS * STEP, 128), F32),
             pltpu.VMEM((2, PEERS, TAIL, 128), BF),
-            pltpu.SemaphoreType.DMA((6,)),
+            pltpu.SemaphoreType.DMA((12,)),
             pltpu.SemaphoreType.DMA((3,)),
         ],
         compiler_params=params(),
         name="back",
-    )(spot, lens, dx, vec, qkv, pen, lse, weights, ht, x)
+    )(spot, lens, vec, up, qkv, soft, weights, ht, x, low, mixed)
 
 
 def feed_kernel(
-    lens_ref, middle_ref, h_ref, ln_ref, cot_ref, mixed_hbm, late_ref,
-    y_ref, grad_ref, dx_ref, vec_ref,
-    up_s, down_s, mid_s, gup_s, gdown_s, gout_s, mixed_s, dy_s, h_s, y_s, dx_s, acc_s, dh_ref, sems, out_sems,
+    spot_ref, lens_ref, middle_ref, h_ref, cot_ref, late_ref, y_ref, own_ref, oth_ref, dh_ref,
+    up_s, down_s, mid_in, mid_s, gup_s, gdown_s, dy_s, acc_s, sems, out_sems,
 ):
     def load_up(chunk):
         devices = pl.ds(chunk * 32, 32)
@@ -601,40 +653,54 @@
     def load_mid(half):
         devices = pl.ds(half * 64, 64)
         return pltpu.make_async_copy(
-            late_ref.at[devices, 32:48, :], mid_s.at[half], sems.at[8 + half]
+            late_ref.at[devices, 32:48, :], mid_in.at[half], sems.at[8 + half]
         )
 
-    def store_big(chunk, block):
-        devices = pl.ds(chunk * 32, 32)
-        lanes = slice(block * 128, block * 128 + 128)
+    def both_cores(source, y, rows, sem, first, second):
         return [
-            pltpu.make_async_copy(
-                grads.at[chunk, :, :, lanes],
-                grad_ref.at[devices, block * 48 + offset : block * 48 + offset + 16, :],
-                out_sems.at[chunk],
-            )
-            for grads, offset in ((gup_s, 0), (gdown_s, 16))
+            pltpu.make_async_copy(source.at[0], first.at[y, :, :, rows, :], sem),
+            pltpu.make_async_copy(source.at[1], second.at[:, y, :, rows, :], sem),
         ]
 
-    def store_mid(half, block):
-        devices = pl.ds(half * 64, 64)
-        lanes = slice(block * 128, block * 128 + 128)
-        return pltpu.make_async_copy(
-            mid_s.at[half, :, :, lanes],
-            grad_ref.at[devices, block * 48 + 32 : block * 48 + 48, :],
-            out_sems.at[4 + half],
-        )
+    def big_stores(chunk, first, second):
+        copies = []
+        for block in range(BLOCKS):
+            lanes = slice(block * 128, block * 128 + 128)
+            for grads, offset in ((gup_s, 0), (gdown_s, 16)):
+                rows = slice(block * 48 + offset, block * 48 + offset + 16)
+                source = grads.at[chunk, :, :, :, :, lanes]
+                copies += both_cores(source, chunk, rows, out_sems.at[chunk], first, second)
+        return copies
+
+    def mid_stores(half, first, second):
+        copies = []
+        for block in range(BLOCKS):
+            lanes = slice(block * 128, block * 128 + 128)
+            rows = slice(block * 48 + 32, block * 48 + 48)
+            for y in range(2):
+                source = mid_s.at[half, y, :, :, :, :, lanes]
+                copies += both_cores(
+                    source, half * 2 + y, rows, out_sems.at[4 + half], first, second
+                )
+        return copies
+
+    def send(stores, number):
+        @pl.when(spot_ref[0, 0] == 0)
+        def _():
+            for copy in stores(number, own_ref, oth_ref):
+                copy.start()
+
+        @pl.when(spot_ref[0, 0] == 1)
+        def _():
+            for copy in stores(number, oth_ref, own_ref):
+                copy.start()
 
     for chunk in range(4):
         load_up(chunk).start()
         load_down(chunk).start()
     for half in range(2):
         load_mid(half).start()
-    load_mixed = pltpu.make_async_copy(mixed_hbm, mixed_s, sems.at[10])
-    load_mixed.start()
     ends = group_ends(lens_ref)
-    gain = ln_ref[2:3, :]
-    vec_ref[...] = jnp.zeros_like(vec_ref)
 
     @pl.loop(0, 4)
     def _(block):
@@ -664,99 +730,59 @@
         up_grad, down_grad = both_ways(
             up_s[chunk].reshape(ROWS, D), down_s[chunk].reshape(ROWS, D)
         )
-        gup_s[chunk] = up_grad.astype(BF).reshape(32, 16, D)
-        gdown_s[chunk] = down_grad.astype(BF).reshape(32, 16, D)
-        for block in range(BLOCKS):
-            for copy in store_big(chunk, block):
-                copy.start()
+        gup_s[chunk] = up_grad.astype(BF).reshape(2, 4, 4, 16, D)
+        gdown_s[chunk] = down_grad.astype(BF).reshape(2, 4, 4, 16, D)
+        send(big_stores, chunk)
 
     @pl.loop(0, 2)
     def _(half):
         load_mid(half).wait()
-        mid = mid_s[half].astype(F32)
+        mid = mid_in[half].astype(F32)
         up_grad, down_grad = both_ways(
             mid[:, 0:8, :].reshape(ROWS, D).astype(BF), mid[:, 8:16, :].reshape(ROWS, D).astype(BF)
         )
         joined = jnp.concatenate(
             [up_grad.reshape(PEERS, 8, D), down_grad.reshape(PEERS, 8, D)], axis=1
         )
-        mid_s[half] = joined.astype(BF)
-        for block in range(BLOCKS):
-            store_mid(half, block).start()
-
-    @pl.loop(0, 4)
-    def _(block):
-        rows = pl.ds(pl.multiple_of(block * 128, 128), 128)
-        y_s[rows, :] = acc_s[rows, :].astype(BF)
-        unit, inverse = norm_stats(middle_ref[rows, :])
-        gradient = dh_ref[rows, :]
-        vec_ref[2:3, :] = vec_ref[2:3, :] + jnp.sum(gradient * unit, axis=0, keepdims=True)
-        vec_ref[3:4, :] = vec_ref[3:4, :] + jnp.sum(gradient, axis=0, keepdims=True)
-        live = (iota((128, 1), 0) + block * 128) < ends[3]
-        dy = jnp.where(live, cot_ref[rows, :].astype(F32), 0.0)
-        moved = dy + norm_pull(gradient, unit, inverse, gain)
-        dx_s[rows, :] = moved
-        h_s[rows, :] = moved.astype(BF)
-
-    store_y = pltpu.make_async_copy(y_s, y_ref, out_sems.at[9])
-    store_y.start()
-    store_dx = pltpu.make_async_copy(dx_s, dx_ref, out_sems.at[10])
-    store_dx.start()
-    load_mixed.wait()
-    outer = dot_tn(mixed_s[...], h_s[...])
-    stores = []
-    for block in range(0, BLOCKS, 2):
-        pieces = [
-            outer[:, at * 128 : at * 128 + 128].reshape(128, 8, 128) for at in (block, block + 1)
-        ]
-        gout_s[block // 2] = jnp.concatenate(pieces, axis=1).astype(BF)
-        start = 288 + block * 8
-        store = pltpu.make_async_copy(
-            gout_s.at[block // 2], grad_ref.at[:, start : start + 16, :], out_sems.at[6 + block // 2]
-        )
-        store.start()
-        stores.append(store)
-    for block in range(BLOCKS):
-        for chunk in range(4):
-            for copy in store_big(chunk, block):
-                copy.wait()
-        for half in range(2):
-            store_mid(half, block).wait()
-    for store in (store_y, store_dx, *stores):
-        store.wait()
-
-
-def feed(lens, middle, h, ln, cot, mixed, late):
+        mid_s[half] = joined.astype(BF).reshape(2, 2, 4, 4, 16, D)
+        send(mid_stores, half)
+
+    y_ref[...] = acc_s[...].astype(BF)
+    for chunk in range(4):
+        for copy in big_stores(chunk, own_ref, oth_ref):
+            copy.wait()
+    for half in range(2):
+        for copy in mid_stores(half, own_ref, oth_ref):
+            copy.wait()
+
+
+def feed(spot, lens, middle, h, cot, late):
+    slab = jax.ShapeDtypeStruct((4, 4, 4, WHOLE, 128), BF)
     return pl.pallas_call(
         feed_kernel,
         out_shape=(
             jax.ShapeDtypeStruct((ROWS, D), BF),
-            jax.ShapeDtypeStruct((128, WHOLE, 128), BF),
+            slab,
+            slab,
             jax.ShapeDtypeStruct((ROWS, D), F32),
-            jax.ShapeDtypeStruct((8, D), F32),
         ),
-        in_specs=[SM, VM, VM, VM, VM, ANY, ANY],
-        out_specs=(ANY, ANY, ANY, VM),
+        in_specs=[SM, SM, VM, VM, VM, ANY],
+        out_specs=(VM, ANY, ANY, VM),
         scratch_shapes=[
             pltpu.VMEM((4, 32, 16, D), BF),
             pltpu.VMEM((4, 32, 16, D), BF),
             pltpu.VMEM((2, PEERS, 16, D), BF),
-            pltpu.VMEM((4, 32, 16, D), BF),
-            pltpu.VMEM((4, 32, 16, D), BF),
-            pltpu.VMEM((3, 128, 16, 128), BF),
-            pltpu.VMEM((ROWS, WIDE), BF),
-            pltpu.VMEM((ROWS, D), BF),
-            pltpu.VMEM((ROWS, D), BF),
+            pltpu.VMEM((2, 2, 2, 4, 4, 16, D), BF),
+            pltpu.VMEM((4, 2, 4, 4, 16, D), BF),
+            pltpu.VMEM((4, 2, 4, 4, 16, D), BF),
             pltpu.VMEM((ROWS, D), BF),
             pltpu.VMEM((ROWS, D), F32),
-            pltpu.VMEM((ROWS, D), F32),
-            pltpu.VMEM((ROWS, D), F32),
-            pltpu.SemaphoreType.DMA((11,)),
-            pltpu.SemaphoreType.DMA((11,)),
+            pltpu.SemaphoreType.DMA((10,)),
+            pltpu.SemaphoreType.DMA((6,)),
         ],
         compiler_params=params(),
         name="feed",
-    )(lens, middle, h, ln, cot, mixed, late)
+    )(spot, lens, middle, h, cot, late)
 
 
 def norm_back_kernel(x_ref, dx_ref, dh_ref, ln_ref, dtok_ref):
@@ -779,16 +805,17 @@
     )(x, dx, dh, ln)
 
 
-def finish_kernel(*refs):
-    slabs, (qkv_ref, g1_ref, b1_ref, g2_ref, b2_ref), sum_s = refs[0:4], refs[4:9], refs[9]
-    sum_s[...] = sum(slab[...].astype(F32) for slab in slabs)
+def finish_kernel(slabs_ref, qkv_ref, out_ref, g1_ref, b1_ref, g2_ref, b2_ref, sum_s):
+    sum_s[...] = jnp.sum(slabs_ref[...].astype(F32), axis=0)
     for pair in range(BLOCKS):
         for part in range(3):
             start = (pair * 3 + part) * OWN
             at = part * D + pair * 128
             qkv_ref[:, at : at + 128] = sum_s[start : start + OWN, :]
+        start = OUTER + pair * OWN
+        out_ref[:, pair * 128 : pair * 128 + 128] = sum_s[start : start + OWN, :]
     for which, target in enumerate((g1_ref, b1_ref, g2_ref, b2_ref)):
-        target[...] = sum_s[OUTER : OUTER + 1, which * OWN : which * OWN + OWN]
+        target[...] = sum_s[GATHERED : GATHERED + 1, which * OWN : which * OWN + OWN]
 
 
 def finish(slabs):
@@ -797,17 +824,18 @@
         finish_kernel,
         out_shape=(
             jax.ShapeDtypeStruct((OWN, 3 * D), F32),
+            jax.ShapeDtypeStruct((OWN, D), F32),
             vector, vector, vector, vector,
         ),
-        in_specs=[VM] * 4,
-        out_specs=(VM,) * 5,
+        in_specs=[VM],
+        out_specs=(VM,) * 6,
         scratch_shapes=[pltpu.VMEM((TAIL, 128), F32)],
         compiler_params=params(16),
         name="finish",
-    )(*slabs)
-
-
-def unpack_kernel(late_ref, up_ref, down_ref, out_ref, sum_s):
+    )(slabs)
+
+
+def unpack_kernel(late_ref, up_ref, down_ref, sum_s):
     sum_s[...] = jnp.sum(late_ref[...].astype(F32), axis=0)
     for block in range(BLOCKS):
         lanes = slice(block * 128, block * 128 + 128)
@@ -816,76 +844,105 @@
         down_ref[0:16, lanes] = sum_s[row + 16 : row + 32, :]
         up_ref[16:24, lanes] = sum_s[row + 32 : row + 40, :]
         down_ref[16:24, lanes] = sum_s[row + 40 : row + 48, :]
-        row = BLOCKS * 48 + block * 8
-        out_ref[:, lanes] = sum_s[row : row + OWN, :]
 
 
 def unpack(late):
     shard = jax.ShapeDtypeStruct((24, D), F32)
     return pl.pallas_call(
         unpack_kernel,
-        out_shape=(shard, shard, jax.ShapeDtypeStruct((OWN, D), F32)),
+        out_shape=(shard, shard),
         in_specs=[VM],
-        out_specs=(VM, VM, VM),
+        out_specs=(VM, VM),
         scratch_shapes=[pltpu.VMEM((WHOLE, 128), F32)],
         compiler_params=params(16),
         name="unpack",
     )(late)
 
 
-def fold_kernel(slabs_ref, *sums):
-    for back, target in enumerate(sums):
-        rows = slice(back * TAIL, back * TAIL + TAIL)
-        target[...] = jnp.sum(slabs_ref[:, rows, :].astype(F32), axis=0).astype(BF)
-
-
-def fold(slabs):
-    piece = jax.ShapeDtypeStruct((TAIL, 128), BF)
+def add_pair(own, other):
+    received = lax.ppermute(other, AXES, core_pairs())
+    return (own.astype(F32) + received.astype(F32)).astype(BF)
+
+
+def add_kernel(left_ref, right_ref, sum_ref, left, right, total, sems):
+    def copies(source, target, column):
+        return [
+            pltpu.make_async_copy(
+                source.at[pl.ds(part * 8, 8)], target.at[pl.ds(part * 8, 8)], sems.at[part, column]
+            )
+            for part in range(8)
+        ]
+
+    lefts, rights = copies(left_ref, left, 0), copies(right_ref, right, 1)
+    stores = copies(total, sum_ref, 2)
+    for load in itertools.chain(*zip(lefts, rights)):
+        load.start()
+    for part in range(8):
+        lefts[part].wait()
+        rights[part].wait()
+        at = slice(part * 8, part * 8 + 8)
+        total[at] = (left[at].astype(F32) + right[at].astype(F32)).astype(BF)
+        stores[part].start()
+    for store in stores:
+        store.wait()
+
+
+def add_large_pair(own, other):
+    received = lax.ppermute(other, AXES, core_pairs())
     return pl.pallas_call(
-        fold_kernel,
-        out_shape=(piece,) * 4,
-        in_specs=[VM],
-        out_specs=(VM,) * 4,
-        compiler_params=params(16),
-        name="fold",
-    )(slabs)
-
-
-def exchange(slabs, dims):
-    return lax.all_to_all(slabs, AXES, 0, 0, axis_index_groups=peer_groups(dims), tiled=True)
-
-
-def shift(values, dim, ahead):
+        add_kernel,
+        out_shape=jax.ShapeDtypeStruct(own.shape, BF),
+        in_specs=[ANY, ANY],
+        out_specs=ANY,
+        scratch_shapes=[pltpu.VMEM(own.shape, BF)] * 3 + [pltpu.SemaphoreType.DMA((8, 3))],
+        compiler_params=params(),
+        name="add_large_pair",
+    )(own, received)
+
+
+def scatter(slabs, rows):
+    return lax.psum_scatter(
+        slabs.reshape(PEERS * rows, 128),
+        AXES,
+        scatter_dimension=0,
+        axis_index_groups=mixed_groups("y", "z"),
+        tiled=True,
+    )
+
+
+def exchange(slabs, rows):
+    return lax.all_to_all(
+        slabs.reshape(16, rows, 128),
+        AXES,
+        0,
+        0,
+        axis_index_groups=mixed_groups("zx", "yx"),
+        tiled=True,
+    )
+
+
+def shift(values, dims, ahead):
     pairs = []
     for x, y, z, c in itertools.product(range(4), range(4), range(4), range(2)):
         to = dict(x=x, y=y, z=z)
-        to[dim] = (to[dim] + ahead) % 4
+        to[dims[c]] = (to[dims[c]] + ahead) % 4
         pairs.append((device_number(x, y, z, c), device_number(to["x"], to["y"], to["z"], c)))
     return lax.ppermute(values, AXES, pairs)
 
 
-def ring(own, dim):
-    return jnp.concatenate([own] + [shift(own, dim, ahead) for ahead in (1, 2, 3)], axis=0)
-
-
-def wide_ring(own, dim):
+def ring(own, dims):
+    return jnp.concatenate([own] + [shift(own, dims, ahead) for ahead in (1, 2, 3)], axis=0)
+
+
+def wide_ring(own, dims):
     half = own.shape[0] // 2
-    near, last = shift(own, dim, 1), shift(own, dim, -1)
-    far = [shift(near[:half], dim, 1), shift(last[half:], dim, -1)]
+    near, last = shift(own, dims, 1), shift(own, dims, -1)
+    far = [shift(near[:half], dims, 1), shift(last[half:], dims, -1)]
     return jnp.concatenate([own, near, *far, last], axis=0)
 
 
 def copies_of_peers(own):
-    return wide_ring(ring(ring(own, "z"), "x"), "y").reshape(PEERS, *own.shape)
-
-
-def sum_over_peers(own, other):
-    received = lax.ppermute(other, AXES, core_pairs())
-    slab = (own.astype(F32) + received.astype(F32)).astype(BF)
-    pieces = fold(exchange(slab.reshape(16, 4 * TAIL, 128), "zx"))
-    return [pieces[0]] + [
-        shift(piece, "y", -back) for back, piece in enumerate(pieces) if back
-    ]
+    return wide_ring(ring(ring(own, "zy"), "xx"), "yz").reshape(PEERS, *own.shape)
 
 
 def on_device(
@@ -910,27 +967,26 @@
     late = lax.all_gather(late, AXES, axis_index_groups=peer_groups("yczx"))
     early_own = copies_of_peers(early)
     early_oth = lax.ppermute(early_own, AXES, core_pairs())
-    ht, qkv, weights, norms, mixed, middle, h_two, penalty, log_totals = front(
+    ht, qkv, weights, norms, mixed, middle, h_two, soft = front(
         spot, seq_lengths, tokens, early_own, early_oth
     )
-    output, late_grad, dx, vectors = feed(
-        seq_lengths, middle, h_two, norms, cotangent, mixed, late
+    output, own, oth, dh_two = feed(spot, seq_lengths, middle, h_two, cotangent, late)
+    late_grad = add_large_pair(own.reshape(PEERS, WHOLE, 128), oth.reshape(PEERS, WHOLE, 128))
+    dx, low, upstream, vectors = middle_back(
+        spot, seq_lengths, cotangent, middle, dh_two, norms, weights
     )
-    late_grad = lax.psum_scatter(
-        late_grad.reshape(128 * WHOLE, 128),
-        AXES,
-        scatter_dimension=0,
-        axis_index_groups=peer_groups("yc"),
-        tiled=True,
+    late_grad, upstream = lax.optimization_barrier((late_grad, upstream))
+    late_grad = scatter(late_grad, WHOLE)
+    oth, own, dh_one = back(
+        spot, seq_lengths, vectors, upstream, qkv, soft, weights, ht, tokens, low, mixed
     )
-    oth, own, dh_one = back(
-        spot, seq_lengths, dx, vectors, qkv, penalty, log_totals, weights, ht, tokens
-    )
-    tail = sum_over_peers(own, oth)
+    tail = scatter(add_pair(own, oth), TAIL)
+    late_grad = exchange(late_grad, WHOLE)
     dtokens = norm_back(tokens, dx, dh_one, norms)
-    late_grad = exchange(late_grad.reshape(16, WHOLE, 128), "zx")
-    qkv_grad, g1_grad, b1_grad, g2_grad, b2_grad = finish(tail)
-    up_grad, down_grad, out_grad = unpack(late_grad)
+    tail, late_grad = lax.optimization_barrier((tail, late_grad))
+    tail = exchange(tail, TAIL)
+    up_grad, down_grad = unpack(late_grad)
+    qkv_grad, out_grad, g1_grad, b1_grad, g2_grad, b2_grad = finish(tail)
     return (
         output,
         dtokens,

time: 213 us -> 210 us (0.986)
  blocking collectives: 32 us -> 0 us
  waiting for transfers between devices: 49.7 us -> 67.3 us
  Pallas kernels: 81.9 us -> 91 us
  starting transfers between devices: 28 us -> 30.8 us
    all_to_all x1 -> x0, blocking collectives: 32 us -> none  [exchange(): lax.all_to_all(slabs, AXES, 0, 0, axis_index_groups=peer_groups(dims), ti...]
    reduce_scatter x1 -> x2, waiting for transfers between devices: 0.09 us -> 23.7 us  [scatter(): lax.psum_scatter(slabs.reshape(PEERS * rows, 128), AXES, scatter_dimensio...]
    pallas_call x2 -> x3, Pallas kernels: 1.14 us -> 12.8 us  [the longest x1 6.09 us: middle_back(): pl.pallas_call(middle_kernel, out_shape=(jax.ShapeDtypeStruct((ROWS, D),...]
    all_to_all x1 -> x2, waiting for transfers between devices: 13.3 us -> 5.55 us  [exchange(): lax.all_to_all(slabs.reshape(16, rows, 128), AXES, 0, 0, axis_index_group...]
    all_to_all x1 -> x2, starting transfers between devices: 6.93 us -> 11.7 us  [exchange(): lax.all_to_all(slabs.reshape(16, rows, 128), AXES, 0, 0, axis_index_group...]
    ppermute x13 -> x10, waiting for transfers between devices: 28.3 us -> 24.6 us  [shift(): return lax.ppermute(values, AXES, pairs)]
    ppermute x1 -> x2, waiting for transfers between devices: 3.87 us -> 6.64 us  [the longest x1 4.71 us: add_pair(): received = lax.ppermute(other, AXES, core_pairs())]
    all_gather x1, waiting for transfers between devices: 0.02 us -> 2.78 us  [on_device(): late = lax.all_gather(late, AXES, axis_index_groups=peer_groups('yczx'))]
  transfers between devices with their start and end apart: 18 -> 18, of which waited for: 9 -> 12; matrix products, arithmetic and copies ran while one was open for 2% -> 3% of each run, Pallas kernels for 26% -> 28%
where the time goes in v4:
time: 210 us; the launch traced here: 209 us
  Pallas kernels  91 us (43%)
  waiting for transfers between devices  67.3 us (32%)
  starting transfers between devices  30.8 us (15%)
  between operations  14 us (7%)
  other arithmetic  4.68 us (2%)
    ppermute x10, waiting for transfers between devices, shift(): return lax.ppermute(values, AXES, pairs)  24.6 us
    pallas_call x1, Pallas kernels, front(): pl.pallas_call(front_kernel, out_shape=(jax.ShapeDtypeStruct((D, ROWS), B...  24.5 us
    pallas_call x1, Pallas kernels, feed(): pl.pallas_call(feed_kernel, out_shape=(jax.ShapeDtypeStruct((ROWS, D), BF...  23.8 us
    reduce_scatter x2, waiting for transfers between devices, scatter(): lax.psum_scatter(slabs.reshape(PEERS * rows, 128), AXES, scatter_dimensio...  23.7 us
    pallas_call x1, Pallas kernels, back(): pl.pallas_call(back_kernel, out_shape=(slab, slab, jax.ShapeDtypeStruct((...  23.3 us
    ppermute x10, starting transfers between devices, shift(): return lax.ppermute(values, AXES, pairs)  18.1 us
    all_to_all x2, starting transfers between devices, exchange(): lax.all_to_all(slabs.reshape(16, rows, 128), AXES, 0, 0, axis_index_group...  11.7 us
    pallas_call x1, Pallas kernels, middle_back(): pl.pallas_call(middle_kernel, out_shape=(jax.ShapeDtypeStruct((ROWS, D),...  6.09 us
  transfers between devices with their start and end apart: 18, of which 12 were waited for; matrix products, arithmetic and copies ran while one was open for 3% of the time, Pallas kernels for 28%

profile of v4, /device:TPU:0, one launch (start us, length us, event | category | flops | bytes accessed | tf_op | source)
XLA Modules:
  0.0 209.0 jit_solution(1638293703746275124)
XLA Ops:
  7.2 0.0 all-gather.3.cloned.1.call-start
  7.2 1.6 pack.1
  8.8 0.0 all-gather.3.cloned.1.call-update
  8.8 0.0 reduce-scatter.5.cloned.1.call-start
  8.9 4.2 %collective-permute-start.2 = (bf16[152,128]{1,0:T(8,128)(2,1)}, bf16[152,128]{1,0:T(8,128)(2,1)S(1)}, u32[]{:S(2)}, u32[]{:S(2)}) collective-permute-start(bf16[152,128]{1,0:T(8,128)(2,1)} %get-tuple-element.43), channel_id=1, source_target_pairs={{0,3},{8,56},{1,0},{9,57},{2,1},{10,58},{3,2},{11,59},{16,19},{24,... | collective-permute-start | bytes 116744 | tf_op jit(solution)/shard_map/ppermute | solution.py:930
  13.1 0.0 collective-permute-start.1
  13.1 1.3 collective-permute-start
  14.3 0.8 constant_dynamic-update-slice_fusion.10
  15.2 3.7 %collective-permute-done = bf16[152,128]{1,0:T(8,128)(2,1)S(1)} collective-permute-done((bf16[152,128]{1,0:T(8,128)(2,1)}, bf16[152,128]{1,0:T(8,128)(2,1)S(1)}, u32[]{:S(2)}, u32[]{:S(2)}) %collective-permute-start) | collective-permute-done | bytes 38944 | tf_op jit(solution)/shard_map/ppermute | solution.py:930
  19.0 0.0 collective-permute-done.2
  19.0 1.6 collective-permute-start.3
  20.6 2.7 %collective-permute-start.4 = (bf16[608,128]{1,0:T(8,128)(2,1)S(1)}, bf16[608,128]{1,0:T(8,128)(2,1)S(1)}, u32[]{:S(2)}, u32[]{:S(2)}) collective-permute-start(bf16[608,128]{1,0:T(8,128)(2,1)S(1)} %get-tuple-element.84), channel_id=1, source_target_pairs={{0,4},{8,12},{1,5},{9,13},{2,6},{10,14},{3,7},{11,15},{16,20},{24,... | collective-permute-start | bytes 466952 | tf_op jit(solution)/shard_map/ppermute | solution.py:930
  23.3 1.4 collective-permute-start.5
  24.7 1.8 collective-permute-done.3
  26.6 1.6 collective-permute-done.4
  28.3 0.5 collective-permute-done.5
  28.8 3.0 %collective-permute-start.8 = (bf16[2432,128]{1,0:T(8,128)(2,1)S(1)}, bf16[2432,128]{1,0:T(8,128)(2,1)S(1)}, u32[]{:S(2)}, u32[]{:S(2)}) collective-permute-start(bf16[2432,128]{1,0:T(8,128)(2,1)S(1)} %get-tuple-element.76), channel_id=1, source_target_pairs={{0,48},{8,11},{1,49},{9,8},{2,50},{10,9},{3,51},{11,10},{16,0},{24... | collective-permute-start | bytes 1867784 | tf_op jit(solution)/shard_map/ppermute | solution.py:930
  31.9 8.0 %collective-permute-done.8 = bf16[2432,128]{1,0:T(8,128)(2,1)S(1)} collective-permute-done((bf16[2432,128]{1,0:T(8,128)(2,1)S(1)}, bf16[2432,128]{1,0:T(8,128)(2,1)S(1)}, u32[]{:S(2)}, u32[]{:S(2)}) %collective-permute-start.8) | collective-permute-done | bytes 622624 | tf_op jit(solution)/shard_map/ppermute | solution.py:930
  39.9 3.8 %collective-permute-start.9 = (bf16[1216,128]{1,0:T(8,128)(2,1)S(1)}, bf16[1216,128]{1,0:T(8,128)(2,1)S(1)}, u32[]{:S(2)}, u32[]{:S(2)}) collective-permute-start(bf16[1216,128]{1,0:T(8,128)(2,1)S(1)} %slice.9), channel_id=1, source_target_pairs={{0,48},{8,11},{1,49},{9,8},{2,50},{10,9},{3,51},{11,10},{16,0},{24... | collective-permute-start | bytes 933896 | tf_op jit(solution)/shard_map/ppermute | solution.py:930
  43.7 0.1 collective-permute-start.7
  43.8 0.1 constant_dynamic-update-slice_fusion.14
  43.9 8.9 %collective-permute-done.7 = bf16[1216,128]{1,0:T(8,128)(2,1)S(1)} collective-permute-done((bf16[1216,128]{1,0:T(8,128)(2,1)S(1)}, bf16[1216,128]{1,0:T(8,128)(2,1)S(1)}, u32[]{:S(2)}, u32[]{:S(2)}) %collective-permute-start.7) | collective-permute-done | bytes 311328 | tf_op jit(solution)/shard_map/ppermute | solution.py:930
  52.9 0.1 constant_dynamic-update-slice_fusion.11
  53.0 0.3 collective-permute-start.10
  53.2 0.8 add_bitcast_fusion.spot_ref
  54.1 4.0 %collective-permute-done.10.oth_ref = bf16[64,152,128]{2,1,0:T(8,128)(2,1)} collective-permute-done((bf16[64,152,128]{2,1,0:T(8,128)(2,1)S(1)}, bf16[64,152,128]{2,1,0:T(8,128)(2,1)}, u32[]{:S(2)}, u32[]{:S(2)}) %collective-permute-start.10) | collective-permute-done | bytes 2490400 | tf_op jit(solution)/shard_map/ppermute | solution.py:969
  58.1 24.5 %front.1 = (bf16[768,512]{1,0:T(8,128)(2,1)}, bf16[512,2304]{1,0:T(8,128)(2,1)}, bf16[768,3072]{1,0:T(8,128)(2,1)}, f32[8,768]{1,0:T(8,128)}, bf16[512,768]{1,0:...) custom-call(s32[1,4]{1,0:T(1,128)} %add_bitcast_fusion.spot_ref, ...), custom_call_target="tpu_custom_call" | custom-call | tf_op jit(solution)/shard_map/front/pallas_call | solution.py:364
  82.6 2.8 %all-gather.3.cloned.1.call-done = bf16[6144,768]{1,0:T(8,128)(2,1)} async-done(((bf16[48,768]{1,0:T(8,128)(2,1)}), bf16[6144,768]{1,0:T(8,128)(2,1)}) %all-gather.3.cloned.1.call-update) | async-done | bytes 9437200 | tf_op jit(solution)/shard_map/all_gather | solution.py:967
  85.3 23.8 %feed.1 = (bf16[512,768]{1,0:T(8,128)(2,1)}, bf16[4,4,4,288,128]{4,3,2,1,0:T(8,128)(2,1)}, bf16[4,4,4,288,128]{4,3,2,1,0:T(8,128)(2,1)}, f32[512,768]{1,0:T(8,128)}) custom-call(s32[1,4]{1,0:T(1,128)} %add_bitcast_fusion.spot_ref, s32[1,4]{1,0:T(1,128)} %lens_ref.7, f32[512,768]{1,0:T(8,128)} %get-tuple-element.44.middle_ref, ...), custom_call_target="tpu_custom_call" | custom-call | tf_op jit(solution)/shard_map/feed/pallas_call | solution.py:761
  109.2 0.3 collective-permute-start.11
  109.5 6.1 %middle_back.1 = (f32[512,768]{1,0:T(8,128)}, bf16[512,768]{1,0:T(8,128)(2,1)}, bf16[512,768]{1,0:T(8,128)(2,1)}, f32[8,768]{1,0:T(8,128)}) custom-call(s32[1,4]{1,0:T(1,128)} %add_bitcast_fusion.spot_ref, s32[1,4]{1,0:T(1,128)} %lens_ref.7, bf16[512,768]{1,0:T(8,128)(2,1)} %cot_ref.3, f32[512,768]{1,0:T(8,128)} %get-tuple-element.44.middle_ref, ...), custom_call_target="tpu_custom_call" | custom-call | tf_op jit(solution)/shard_map/middle_back/pallas_call | solution.py:499
  115.6 1.9 collective-permute-done.11.right_ref
  117.5 5.9 %add_large_pair.1 = bf16[64,288,128]{2,1,0:T(8,128)(2,1)} custom-call(bf16[64,288,128]{2,1,0:T(8,128)(2,1)} %bitcast.27, bf16[64,288,128]{2,1,0:T(8,128)(2,1)} %collective-permute-done.11.right_ref), custom_call_target="tpu_custom_call" | custom-call | tf_op jit(solution)/shard_map/add_large_pair/pallas_call | solution.py:892
  123.4 0.0 reduce-scatter.5.cloned.1.call-update
  123.4 0.0 reduce-scatter.3.cloned.1.call-start
  123.5 23.3 %back.1 = (bf16[64,152,128]{2,1,0:T(8,128)(2,1)}, bf16[64,152,128]{2,1,0:T(8,128)(2,1)}, f32[512,768]{1,0:T(8,128)}) custom-call(s32[1,4]{1,0:T(1,128)} %add_bitcast_fusion.spot_ref, s32[1,4]{1,0:T(1,128)} %lens_ref.7, f32[8,768]{1,0:T(8,128)} %get-tuple-element.52.vec_ref, bf16[512,768]{1,0:T(8,128)(2,1)} %get-tuple-element.56.up, ...), custom_call_target="tpu_custom_call" | custom-call | tf_op jit(solution)/shard_map/back/pallas_call | solution.py:611
  146.7 0.3 collective-permute-start.12
  147.0 4.7 %collective-permute-done.12 = bf16[64,152,128]{2,1,0:T(8,128)(2,1)S(1)} collective-permute-done((bf16[64,152,128]{2,1,0:T(8,128)(2,1)}, bf16[64,152,128]{2,1,0:T(8,128)(2,1)S(1)}, u32[]{:S(2)}, u32[]{:S(2)}) %collective-permute-start.12) | collective-permute-done | bytes 2490400 | tf_op jit(solution)/shard_map/ppermute | solution.py:863
  151.7 3.8 %add_convert_fusion = bf16[64,152,128]{2,1,0:T(8,128)(2,1)} fusion(bf16[64,152,128]{2,1,0:T(8,128)(2,1)S(1)} %collective-permute-done.12, bf16[64,152,128]{2,1,0:T(8,128)(2,1)} %get-tuple-element.63), kind=kLoop, calls=%fused_computation | loop fusion | flops 4980736 | bytes 7471104 | tf_op jit(solution)/shard_map/convert_element_type | solution.py:864
  155.6 0.0 reduce-scatter.3.cloned.1.call-update
  155.6 0.0 reduce-scatter.5.cloned.1.call-done
  155.6 4.9 %all-to-all-start = ((bf16[16,288,128]{2,1,0:T(8,128)(2,1)}), bf16[16,288,128]{2,1,0:T(8,128)(2,1)S(1)}, u32[]{:S(2)}, u32[]{:S(2)}) async-start(bf16[16,288,128]{2,1,0:T(8,128)(2,1)} %bitcast.30), calls=%async_computation.2 | async-start | bytes 2359296 | tf_op jit(solution)/shard_map/all_to_all | solution.py:914
  160.6 23.7 %reduce-scatter.3.cloned.1.call-done = bf16[2432,128]{1,0:T(8,128)(2,1)} async-done(((bf16[9728,128]{1,0:T(8,128)(2,1)}), bf16[2432,128]{1,0:T(8,128)(2,1)}) %reduce-scatter.3.cloned.1.call-update) | async-done | bytes 622608 | tf_op jit(solution)/shard_map/reduce_scatter | solution.py:904
  184.2 6.8 %all-to-all-start.1 = ((bf16[16,152,128]{2,1,0:T(8,128)(2,1)}), bf16[16,152,128]{2,1,0:T(8,128)(2,1)S(1)}, u32[]{:S(2)}, u32[]{:S(2)}) async-start(bf16[16,152,128]{2,1,0:T(8,128)(2,1)} %bitcast.31), calls=%async_computation.3 | async-start | bytes 1245184 | tf_op jit(solution)/shard_map/all_to_all | solution.py:914
  191.0 4.3 %norm_back.1 = bf16[512,768]{1,0:T(8,128)(2,1)} custom-call(bf16[512,768]{1,0:T(8,128)(2,1)} %x_ref.3, f32[512,768]{1,0:T(8,128)} %get-tuple-element.51.dx_ref, f32[512,768]{1,0:T(8,128)} %get-tuple-element.62.dh_ref, f32[8,768]{1,0:T(8,128)} %get-tuple-element.49.ln_ref), custom_call_target="tpu_custom_call" | custom-call | tf_op jit(solution)/shard_map/norm_back/pallas_call | solution.py:798
  195.3 0.8 unpack.1
  196.1 5.5 %all-to-all-done.1.slabs_ref = bf16[16,152,128]{2,1,0:T(8,128)(2,1)S(1)} async-done(((bf16[16,152,128]{2,1,0:T(8,128)(2,1)}), bf16[16,152,128]{2,1,0:T(8,128)(2,1)S(1)}, u32[]{:S(2)}, u32[]{:S(2)}) %all-to-all-start.1) | async-done | bytes 622624 | tf_op jit(solution)/shard_map/all_to_all | solution.py:914
  201.7 0.7 finish.1
  (17 shorter events, 0.4 us)
Async XLA Ops:
  7.2 78.2 %all-gather.3.cloned.1.call-start = ((), (), s32[]{:S(2)}) async-start(), calls=%async_computation.6 | async-start | bytes 9510912 | tf_op jit(solution)/shard_map/all_gather | solution.py:967
  8.8 146.8 %reduce-scatter.5.cloned.1.call-start = ((), (), s32[]{:S(2)}) async-start(), calls=%async_computation.5 | async-start | bytes 5898240 | tf_op jit(solution)/shard_map/reduce_scatter | solution.py:904
  8.9 10.1 %collective-permute-start.2 = (bf16[152,128]{1,0:T(8,128)(2,1)}, bf16[152,128]{1,0:T(8,128)(2,1)S(1)}, u32[]{:S(2)}, u32[]{:S(2)}) collective-permute-start(bf16[152,128]{1,0:T(8,128)(2,1)} %get-tuple-element.43), channel_id=1, source_target_pairs={{0,3},{8,56},{1,0},{9,57},{2,1},{10,58},{3,2},{11,59},{16,19},{24,... | collective-permute-start | bytes 116744 | tf_op jit(solution)/shard_map/ppermute | solution.py:930
  13.1 5.8 %collective-permute-start.1 = (bf16[152,128]{1,0:T(8,128)(2,1)}, bf16[152,128]{1,0:T(8,128)(2,1)S(1)}, u32[]{:S(2)}, u32[]{:S(2)}) collective-permute-start(bf16[152,128]{1,0:T(8,128)(2,1)} %get-tuple-element.43), channel_id=1, source_target_pairs={{0,2},{8,40},{1,3},{9,41},{2,0},{10,42},{3,1},{11,43},{16,18},{24,... | collective-permute-start | bytes 116744 | tf_op jit(solution)/shard_map/ppermute | solution.py:930
  13.1 5.8 %collective-permute-start = (bf16[152,128]{1,0:T(8,128)(2,1)}, bf16[152,128]{1,0:T(8,128)(2,1)S(1)}, u32[]{:S(2)}, u32[]{:S(2)}) collective-permute-start(bf16[152,128]{1,0:T(8,128)(2,1)} %get-tuple-element.43), channel_id=1, source_target_pairs={{0,1},{8,24},{1,2},{9,25},{2,3},{10,26},{3,0},{11,27},{16,17},{24,... | collective-permute-start | bytes 116744 | tf_op jit(solution)/shard_map/ppermute | solution.py:930
  19.0 7.5 %collective-permute-start.3 = (bf16[608,128]{1,0:T(8,128)(2,1)S(1)}, bf16[608,128]{1,0:T(8,128)(2,1)S(1)}, u32[]{:S(2)}, u32[]{:S(2)}) collective-permute-start(bf16[608,128]{1,0:T(8,128)(2,1)S(1)} %get-tuple-element.84), channel_id=1, source_target_pairs={{0,64},{8,72},{1,65},{9,73},{2,66},{10,74},{3,67},{11,75},{16,80},... | collective-permute-start | bytes 466952 | tf_op jit(solution)/shard_map/ppermute | solution.py:930
  20.6 7.6 %collective-permute-start.4 = (bf16[608,128]{1,0:T(8,128)(2,1)S(1)}, bf16[608,128]{1,0:T(8,128)(2,1)S(1)}, u32[]{:S(2)}, u32[]{:S(2)}) collective-permute-start(bf16[608,128]{1,0:T(8,128)(2,1)S(1)} %get-tuple-element.84), channel_id=1, source_target_pairs={{0,4},{8,12},{1,5},{9,13},{2,6},{10,14},{3,7},{11,15},{16,20},{24,... | collective-permute-start | bytes 466952 | tf_op jit(solution)/shard_map/ppermute | solution.py:930
  23.3 5.5 %collective-permute-start.5 = (bf16[608,128]{1,0:T(8,128)(2,1)S(1)}, bf16[608,128]{1,0:T(8,128)(2,1)S(1)}, u32[]{:S(2)}, u32[]{:S(2)}) collective-permute-start(bf16[608,128]{1,0:T(8,128)(2,1)S(1)} %get-tuple-element.84), channel_id=1, source_target_pairs={{0,68},{8,76},{1,69},{9,77},{2,70},{10,78},{3,71},{11,79},{16,84},... | collective-permute-start | bytes 466952 | tf_op jit(solution)/shard_map/ppermute | solution.py:930
  28.8 11.0 %collective-permute-start.8 = (bf16[2432,128]{1,0:T(8,128)(2,1)S(1)}, bf16[2432,128]{1,0:T(8,128)(2,1)S(1)}, u32[]{:S(2)}, u32[]{:S(2)}) collective-permute-start(bf16[2432,128]{1,0:T(8,128)(2,1)S(1)} %get-tuple-element.76), channel_id=1, source_target_pairs={{0,48},{8,11},{1,49},{9,8},{2,50},{10,9},{3,51},{11,10},{16,0},{24... | collective-permute-start | bytes 1867784 | tf_op jit(solution)/shard_map/ppermute | solution.py:930
  31.9 11.8 %collective-permute-start.6 = (bf16[2432,128]{1,0:T(8,128)(2,1)S(1)}, bf16[2432,128]{1,0:T(8,128)(2,1)S(1)}, u32[]{:S(2)}, u32[]{:S(2)}) collective-permute-start(bf16[2432,128]{1,0:T(8,128)(2,1)S(1)} %get-tuple-element.76), channel_id=1, source_target_pairs={{0,16},{8,9},{1,17},{9,10},{2,18},{10,11},{3,19},{11,8},{16,32},{2... | collective-permute-start | bytes 1867784 | tf_op jit(solution)/shard_map/ppermute | solution.py:930
  39.9 12.9 %collective-permute-start.9 = (bf16[1216,128]{1,0:T(8,128)(2,1)S(1)}, bf16[1216,128]{1,0:T(8,128)(2,1)S(1)}, u32[]{:S(2)}, u32[]{:S(2)}) collective-permute-start(bf16[1216,128]{1,0:T(8,128)(2,1)S(1)} %slice.9), channel_id=1, source_target_pairs={{0,48},{8,11},{1,49},{9,8},{2,50},{10,9},{3,51},{11,10},{16,0},{24... | collective-permute-start | bytes 933896 | tf_op jit(solution)/shard_map/ppermute | solution.py:930
  43.7 9.1 %collective-permute-start.7 = (bf16[1216,128]{1,0:T(8,128)(2,1)S(1)}, bf16[1216,128]{1,0:T(8,128)(2,1)S(1)}, u32[]{:S(2)}, u32[]{:S(2)}) collective-permute-start(bf16[1216,128]{1,0:T(8,128)(2,1)S(1)} %slice.8), channel_id=1, source_target_pairs={{0,16},{8,9},{1,17},{9,10},{2,18},{10,11},{3,19},{11,8},{16,32},{2... | collective-permute-start | bytes 933896 | tf_op jit(solution)/shard_map/ppermute | solution.py:930
  53.0 5.1 %copy-start = (bf16[9728,128]{1,0:T(8,128)(2,1)}, bf16[9728,128]{1,0:T(8,128)(2,1)S(1)}, u32[]{:S(2)}) copy-start(bf16[9728,128]{1,0:T(8,128)(2,1)S(1)} %constant_dynamic-update-slice_fusion.11) | copy-start | bytes 7471108
  53.0 5.1 %collective-permute-start.10 = (bf16[64,152,128]{2,1,0:T(8,128)(2,1)S(1)}, bf16[64,152,128]{2,1,0:T(8,128)(2,1)}, u32[]{:S(2)}, u32[]{:S(2)}) collective-permute-start(bf16[64,152,128]{2,1,0:T(8,128)(2,1)S(1)} %bitcast.28), channel_id=1, source_target_pairs={{0,8},{8,0},{1,9},{9,1},{2,10},{10,2},{3,11},{11,3},{16,24},{24,16... | collective-permute-start | bytes 7471112 | tf_op jit(solution)/shard_map/ppermute | solution.py:969
  109.2 8.3 %collective-permute-start.11 = (bf16[64,288,128]{2,1,0:T(8,128)(2,1)}, bf16[64,288,128]{2,1,0:T(8,128)(2,1)}, u32[]{:S(2)}, u32[]{:S(2)}) collective-permute-start(bf16[64,288,128]{2,1,0:T(8,128)(2,1)} %bitcast.37), channel_id=1, source_target_pairs={{0,8},{8,0},{1,9},{9,1},{2,10},{10,2},{3,11},{11,3},{16,24},{24,16... | collective-permute-start | bytes 14155784 | tf_op jit(solution)/shard_map/ppermute | solution.py:891
  123.4 60.8 %reduce-scatter.3.cloned.1.call-start = ((), (), s32[]{:S(2)}) async-start(), calls=%async_computation.4 | async-start | bytes 3112960 | tf_op jit(solution)/shard_map/reduce_scatter | solution.py:904
  146.7 5.0 %collective-permute-start.12 = (bf16[64,152,128]{2,1,0:T(8,128)(2,1)}, bf16[64,152,128]{2,1,0:T(8,128)(2,1)S(1)}, u32[]{:S(2)}, u32[]{:S(2)}) collective-permute-start(bf16[64,152,128]{2,1,0:T(8,128)(2,1)} %get-tuple-element.64), channel_id=1, source_target_pairs={{0,8},{8,0},{1,9},{9,1},{2,10},{10,2},{3,11},{11,3},{16,24},{24,16... | collective-permute-start | bytes 7471112 | tf_op jit(solution)/shard_map/ppermute | solution.py:863
  155.6 28.6 %all-to-all-start = ((bf16[16,288,128]{2,1,0:T(8,128)(2,1)}), bf16[16,288,128]{2,1,0:T(8,128)(2,1)S(1)}, u32[]{:S(2)}, u32[]{:S(2)}) async-start(bf16[16,288,128]{2,1,0:T(8,128)(2,1)} %bitcast.30), calls=%async_computation.2 | async-start | bytes 2359296 | tf_op jit(solution)/shard_map/all_to_all | solution.py:914
  184.2 17.4 %all-to-all-start.1 = ((bf16[16,152,128]{2,1,0:T(8,128)(2,1)}), bf16[16,152,128]{2,1,0:T(8,128)(2,1)S(1)}, u32[]{:S(2)}, u32[]{:S(2)}) async-start(bf16[16,152,128]{2,1,0:T(8,128)(2,1)} %bitcast.31), calls=%async_computation.3 | async-start | bytes 1245184 | tf_op jit(solution)/shard_map/all_to_all | solution.py:914
Sparse Core Ops, SparseCore 0:
  11.4 73.8 all-gather.2
  123.5 30.0 reduce-scatter.4
  156.0 28.1 reduce-scatter.2

commit v5 on v4

--- a/solution.py
+++ b/solution.py
@@ -637,8 +637,8 @@
 
 
 def feed_kernel(
-    spot_ref, lens_ref, middle_ref, h_ref, cot_ref, late_ref, y_ref, own_ref, oth_ref, dh_ref,
-    up_s, down_s, mid_in, mid_s, gup_s, gdown_s, dy_s, acc_s, sems, out_sems,
+    spot_ref, lens_ref, h_ref, cot_ref, late_ref, act_ref, own_ref, oth_ref, dh_ref,
+    up_s, down_s, mid_in, mid_s, gup_s, gdown_s, dy_s, act_s, sems, out_sems,
 ):
     def load_up(chunk):
         devices = pl.ds(chunk * 32, 32)
@@ -705,12 +705,14 @@
     @pl.loop(0, 4)
     def _(block):
         rows = pl.ds(pl.multiple_of(block * 128, 128), 128)
-        acc_s[rows, :] = middle_ref[rows, :]
         live = (iota((128, 1), 0) + block * 128) < ends[3]
         dy_s[rows, :] = jnp.where(live, cot_ref[rows, :].astype(F32), 0.0).astype(BF)
         dh_ref[rows, :] = jnp.zeros((128, D), F32)
 
-    def both_ways(up, down):
+    def store_act(chunk):
+        return pltpu.make_async_copy(act_s.at[chunk], act_ref.at[chunk], out_sems.at[6 + chunk])
+
+    def both_ways(chunk, up, down):
         value = dot_nt(h_ref[...], up)
         square = value * value
         bend = jnp.tanh(TANH_SCALE * (value + TANH_CUBE * (value * square)))
@@ -719,7 +721,7 @@
             1.0 + 3.0 * TANH_CUBE * square
         )
         pulled = (dot_nt(dy_s[...], down) * slope).astype(BF)
-        acc_s[...] = acc_s[...] + dot_nn(act, down)
+        act_s[chunk] = act
         dh_ref[...] = dh_ref[...] + dot_nn(pulled, up)
         return dot_tn(pulled, h_ref[...]), dot_tn(act, dy_s[...])
 
@@ -728,26 +730,31 @@
         load_up(chunk).wait()
         load_down(chunk).wait()
         up_grad, down_grad = both_ways(
-            up_s[chunk].reshape(ROWS, D), down_s[chunk].reshape(ROWS, D)
+            chunk, up_s[chunk].reshape(ROWS, D), down_s[chunk].reshape(ROWS, D)
         )
         gup_s[chunk] = up_grad.astype(BF).reshape(2, 4, 4, 16, D)
         gdown_s[chunk] = down_grad.astype(BF).reshape(2, 4, 4, 16, D)
         send(big_stores, chunk)
+        store_act(chunk).start()
 
     @pl.loop(0, 2)
     def _(half):
         load_mid(half).wait()
         mid = mid_in[half].astype(F32)
         up_grad, down_grad = both_ways(
-            mid[:, 0:8, :].reshape(ROWS, D).astype(BF), mid[:, 8:16, :].reshape(ROWS, D).astype(BF)
+            4 + half,
+            mid[:, 0:8, :].reshape(ROWS, D).astype(BF),
+            mid[:, 8:16, :].reshape(ROWS, D).astype(BF),
         )
         joined = jnp.concatenate(
             [up_grad.reshape(PEERS, 8, D), down_grad.reshape(PEERS, 8, D)], axis=1
         )
         mid_s[half] = joined.astype(BF).reshape(2, 2, 4, 4, 16, D)
         send(mid_stores, half)
-
-    y_ref[...] = acc_s[...].astype(BF)
+        store_act(4 + half).start()
+
+    for chunk in range(6):
+        store_act(chunk).wait()
     for chunk in range(4):
         for copy in big_stores(chunk, own_ref, oth_ref):
             copy.wait()
@@ -756,18 +763,18 @@
             copy.wait()
 
 
-def feed(spot, lens, middle, h, cot, late):
+def feed(spot, lens, h, cot, late):
     slab = jax.ShapeDtypeStruct((4, 4, 4, WHOLE, 128), BF)
     return pl.pallas_call(
         feed_kernel,
         out_shape=(
-            jax.ShapeDtypeStruct((ROWS, D), BF),
+            jax.ShapeDtypeStruct((6, ROWS, ROWS), BF),
             slab,
             slab,
             jax.ShapeDtypeStruct((ROWS, D), F32),
         ),
-        in_specs=[SM, SM, VM, VM, VM, ANY],
-        out_specs=(VM, ANY, ANY, VM),
+        in_specs=[SM, SM, VM, VM, ANY],
+        out_specs=(ANY, ANY, ANY, VM),
         scratch_shapes=[
             pltpu.VMEM((4, 32, 16, D), BF),
             pltpu.VMEM((4, 32, 16, D), BF),
@@ -776,13 +783,60 @@
             pltpu.VMEM((4, 2, 4, 4, 16, D), BF),
             pltpu.VMEM((4, 2, 4, 4, 16, D), BF),
             pltpu.VMEM((ROWS, D), BF),
+            pltpu.VMEM((6, ROWS, ROWS), BF),
+            pltpu.SemaphoreType.DMA((10,)),
+            pltpu.SemaphoreType.DMA((12,)),
+        ],
+        compiler_params=params(),
+        name="feed",
+    )(spot, lens, h, cot, late)
+
+
+def output_kernel(middle_ref, act_ref, late_ref, y_ref, down_s, mid_s, acc_s, sems):
+    loads = [
+        pltpu.make_async_copy(
+            late_ref.at[pl.ds(chunk * 32, 32), 16:32, :], down_s.at[chunk], sems.at[chunk]
+        )
+        for chunk in range(4)
+    ] + [
+        pltpu.make_async_copy(
+            late_ref.at[pl.ds(half * 64, 64), 32:48, :], mid_s.at[half], sems.at[4 + half]
+        )
+        for half in range(2)
+    ]
+    for load in loads:
+        load.start()
+    acc_s[...] = middle_ref[...]
+    for load in loads:
+        load.wait()
+
+    @pl.loop(0, 4)
+    def _(chunk):
+        acc_s[...] = acc_s[...] + dot_nn(act_ref[chunk], down_s[chunk].reshape(ROWS, D))
+
+    @pl.loop(0, 2)
+    def _(half):
+        down = mid_s[half].astype(F32)[:, 8:16, :].reshape(ROWS, D).astype(BF)
+        acc_s[...] = acc_s[...] + dot_nn(act_ref[4 + half], down)
+
+    y_ref[...] = acc_s[...].astype(BF)
+
+
+def layer_output(middle, act, late):
+    return pl.pallas_call(
+        output_kernel,
+        out_shape=jax.ShapeDtypeStruct((ROWS, D), BF),
+        in_specs=[VM, VM, ANY],
+        out_specs=VM,
+        scratch_shapes=[
+            pltpu.VMEM((4, 32, 16, D), BF),
+            pltpu.VMEM((2, PEERS, 16, D), BF),
             pltpu.VMEM((ROWS, D), F32),
-            pltpu.SemaphoreType.DMA((10,)),
             pltpu.SemaphoreType.DMA((6,)),
         ],
         compiler_params=params(),
-        name="feed",
-    )(spot, lens, middle, h, cot, late)
+        name="layer_output",
+    )(middle, act, late)
 
 
 def norm_back_kernel(x_ref, dx_ref, dh_ref, ln_ref, dtok_ref):
@@ -970,7 +1024,7 @@
     ht, qkv, weights, norms, mixed, middle, h_two, soft = front(
         spot, seq_lengths, tokens, early_own, early_oth
     )
-    output, own, oth, dh_two = feed(spot, seq_lengths, middle, h_two, cotangent, late)
+    act, own, oth, dh_two = feed(spot, seq_lengths, h_two, cotangent, late)
     late_grad = add_large_pair(own.reshape(PEERS, WHOLE, 128), oth.reshape(PEERS, WHOLE, 128))
     dx, low, upstream, vectors = middle_back(
         spot, seq_lengths, cotangent, middle, dh_two, norms, weights
@@ -980,10 +1034,12 @@
     oth, own, dh_one = back(
         spot, seq_lengths, vectors, upstream, qkv, soft, weights, ht, tokens, low, mixed
     )
-    tail = scatter(add_pair(own, oth), TAIL)
+    tail, act = lax.optimization_barrier((add_pair(own, oth), act))
+    tail = scatter(tail, TAIL)
     late_grad = exchange(late_grad, WHOLE)
     dtokens = norm_back(tokens, dx, dh_one, norms)
-    tail, late_grad = lax.optimization_barrier((tail, late_grad))
+    output = layer_output(middle, act, late)
+    tail, late_grad, output = lax.optimization_barrier((tail, late_grad, output))
     tail = exchange(tail, TAIL)
     up_grad, down_grad = unpack(late_grad)
     qkv_grad, out_grad, g1_grad, b1_grad, g2_grad, b2_grad = finish(tail)

time: 210 us -> 218 us (1.038); the launches traced: 209 us -> 220 us
  Pallas kernels: 91 us -> 112 us
  waiting for transfers between devices: 67.3 us -> 56.1 us
    pallas_call x1 -> x2, Pallas kernels: 23.8 us -> 44.5 us  [the longest x1 34.3 us: feed(): pl.pallas_call(feed_kernel, out_shape=(jax.ShapeDtypeStruct((6, ROWS, ROW...]
    reduce_scatter x2, waiting for transfers between devices: 23.7 us -> 13.7 us  [scatter(): lax.psum_scatter(slabs.reshape(PEERS * rows, 128), AXES, scatter_dimensio...]
    ppermute x10, waiting for transfers between devices: 24.6 us -> 20.6 us  [shift(): return lax.ppermute(values, AXES, pairs)]
    all_gather x1, waiting for transfers between devices: 2.78 us -> 5.81 us  [on_device(): late = lax.all_gather(late, AXES, axis_index_groups=peer_groups('yczx'))]
  transfers between devices with their start and end apart: 18 -> 18, of which waited for: 12 -> 13; matrix products, arithmetic and copies ran while one was open for 3% -> 3% of each run, Pallas kernels for 28% -> 31%
where the time goes in v5:
time: 218 us; the launch traced here: 220 us
  Pallas kernels  112 us (51%)
  waiting for transfers between devices  56.1 us (26%)
  starting transfers between devices  31.7 us (15%)
  between operations  14.1 us (6%)
  other arithmetic  4.83 us (2%)
    pallas_call x1, Pallas kernels, feed(): pl.pallas_call(feed_kernel, out_shape=(jax.ShapeDtypeStruct((6, ROWS, ROW...  34.3 us
    pallas_call x1, Pallas kernels, front(): pl.pallas_call(front_kernel, out_shape=(jax.ShapeDtypeStruct((D, ROWS), B...  24.5 us
    pallas_call x1, Pallas kernels, back(): pl.pallas_call(back_kernel, out_shape=(slab, slab, jax.ShapeDtypeStruct((...  23.3 us
    ppermute x10, waiting for transfers between devices, shift(): return lax.ppermute(values, AXES, pairs)  20.6 us
    ppermute x10, starting transfers between devices, shift(): return lax.ppermute(values, AXES, pairs)  19.1 us
    reduce_scatter x2, waiting for transfers between devices, scatter(): lax.psum_scatter(slabs.reshape(PEERS * rows, 128), AXES, scatter_dimensio...  13.7 us
    all_to_all x2, starting transfers between devices, exchange(): lax.all_to_all(slabs.reshape(16, rows, 128), AXES, 0, 0, axis_index_group...  11.4 us
    pallas_call x1, Pallas kernels, layer_output(): pl.pallas_call(output_kernel, out_shape=jax.ShapeDtypeStruct((ROWS, D), B...  10.2 us
  transfers between devices with their start and end apart: 18, of which 13 were waited for; matrix products, arithmetic and copies ran while one was open for 3% of the time, Pallas kernels for 31%

profile of v5, /device:TPU:0, one launch (start us, length us, event | category | flops | bytes accessed | tf_op | source)
XLA Modules:
  0.0 219.7 jit_solution(342423219618883545)
XLA Ops:
  7.2 0.0 all-gather.3.cloned.1.call-start
  7.2 1.6 pack.1
  8.8 0.0 all-gather.3.cloned.1.call-update
  8.8 0.0 reduce-scatter.5.cloned.1.call-start
  8.9 2.1 collective-permute-start
  11.0 3.6 %collective-permute-start.1 = (bf16[152,128]{1,0:T(8,128)(2,1)}, bf16[152,128]{1,0:T(8,128)(2,1)S(1)}, u32[]{:S(2)}, u32[]{:S(2)}) collective-permute-start(bf16[152,128]{1,0:T(8,128)(2,1)} %get-tuple-element.46), channel_id=1, source_target_pairs={{0,2},{8,40},{1,3},{9,41},{2,0},{10,42},{3,1},{11,43},{16,18},{24,... | collective-permute-start | bytes 116744 | tf_op jit(solution)/shard_map/ppermute | solution.py:984
  14.5 1.0 collective-permute-start.2
  15.5 0.8 constant_dynamic-update-slice_fusion.10
  16.4 0.7 collective-permute-done.1
  17.1 1.6 collective-permute-done.2
  18.8 1.6 collective-permute-start.3
  20.3 2.7 %collective-permute-start.4 = (bf16[608,128]{1,0:T(8,128)(2,1)S(1)}, bf16[608,128]{1,0:T(8,128)(2,1)S(1)}, u32[]{:S(2)}, u32[]{:S(2)}) collective-permute-start(bf16[608,128]{1,0:T(8,128)(2,1)S(1)} %get-tuple-element.90), channel_id=1, source_target_pairs={{0,4},{8,12},{1,5},{9,13},{2,6},{10,14},{3,7},{11,15},{16,20},{24,... | collective-permute-start | bytes 466952 | tf_op jit(solution)/shard_map/ppermute | solution.py:984
  23.0 1.4 collective-permute-start.5
  24.5 1.2 collective-permute-done.3
  25.8 2.1 collective-permute-done.4
  28.0 0.6 collective-permute-done.5
  28.6 1.6 collective-permute-start.6
  30.2 1.7 collective-permute-start.8
  31.9 8.6 %collective-permute-done.6 = bf16[2432,128]{1,0:T(8,128)(2,1)S(1)} collective-permute-done((bf16[2432,128]{1,0:T(8,128)(2,1)S(1)}, bf16[2432,128]{1,0:T(8,128)(2,1)S(1)}, u32[]{:S(2)}, u32[]{:S(2)}) %collective-permute-start.6) | collective-permute-done | bytes 622624 | tf_op jit(solution)/shard_map/ppermute | solution.py:984
  40.5 0.3 collective-permute-start.7
  40.9 3.0 %collective-permute-start.9 = (bf16[1216,128]{1,0:T(8,128)(2,1)S(1)}, bf16[1216,128]{1,0:T(8,128)(2,1)S(1)}, u32[]{:S(2)}, u32[]{:S(2)}) collective-permute-start(bf16[1216,128]{1,0:T(8,128)(2,1)S(1)} %slice.9), channel_id=1, source_target_pairs={{0,48},{8,11},{1,49},{9,8},{2,50},{10,9},{3,51},{11,10},{16,0},{24... | collective-permute-start | bytes 933896 | tf_op jit(solution)/shard_map/ppermute | solution.py:984
  43.9 0.1 constant_dynamic-update-slice_fusion.14
  44.0 5.7 %collective-permute-done.7 = bf16[1216,128]{1,0:T(8,128)(2,1)S(1)} collective-permute-done((bf16[1216,128]{1,0:T(8,128)(2,1)S(1)}, bf16[1216,128]{1,0:T(8,128)(2,1)S(1)}, u32[]{:S(2)}, u32[]{:S(2)}) %collective-permute-start.7) | collective-permute-done | bytes 311328 | tf_op jit(solution)/shard_map/ppermute | solution.py:984
  49.8 0.1 constant_dynamic-update-slice_fusion.11
  49.9 0.3 collective-permute-start.10
  50.3 0.9 add_bitcast_fusion.spot_ref
  51.2 3.9 %collective-permute-done.10.oth_ref = bf16[64,152,128]{2,1,0:T(8,128)(2,1)} collective-permute-done((bf16[64,152,128]{2,1,0:T(8,128)(2,1)S(1)}, bf16[64,152,128]{2,1,0:T(8,128)(2,1)}, u32[]{:S(2)}, u32[]{:S(2)}) %collective-permute-start.10) | collective-permute-done | bytes 2490400 | tf_op jit(solution)/shard_map/ppermute | solution.py:1023
  55.1 24.5 %front.1 = (bf16[768,512]{1,0:T(8,128)(2,1)}, bf16[512,2304]{1,0:T(8,128)(2,1)}, bf16[768,3072]{1,0:T(8,128)(2,1)}, f32[8,768]{1,0:T(8,128)}, bf16[512,768]{1,0:...) custom-call(s32[1,4]{1,0:T(1,128)} %add_bitcast_fusion.spot_ref, ...), custom_call_target="tpu_custom_call" | custom-call | tf_op jit(solution)/shard_map/front/pallas_call | solution.py:364
  79.6 5.8 %all-gather.3.cloned.1.call-done = bf16[6144,768]{1,0:T(8,128)(2,1)} async-done(((bf16[48,768]{1,0:T(8,128)(2,1)}), bf16[6144,768]{1,0:T(8,128)(2,1)}) %all-gather.3.cloned.1.call-update) | async-done | bytes 9437200 | tf_op jit(solution)/shard_map/all_gather | solution.py:1021
  85.4 34.3 %feed.1 = (bf16[6,512,512]{2,1,0:T(8,128)(2,1)}, bf16[4,4,4,288,128]{4,3,2,1,0:T(8,128)(2,1)}, bf16[4,4,4,288,128]{4,3,2,1,0:T(8,128)(2,1)}, f32[512,768]{1,0:T(8,128)}) custom-call(s32[1,4]{1,0:T(1,128)} %add_bitcast_fusion.spot_ref, s32[1,4]{1,0:T(1,128)} %lens_ref.7, bf16[512,768]{1,0:T(8,128)(2,1)} %get-tuple-element.48.h_ref, bf16[512,768]{1,0:T(8,128)(2,1)} %cot_ref.3, ...), custom_call_target="tpu_custom_call" | custom-call | tf_op jit(solution)/shard_map/feed/pallas_call | solution.py:768
  119.7 0.4 collective-permute-start.11
  120.1 6.1 %middle_back.1 = (f32[512,768]{1,0:T(8,128)}, bf16[512,768]{1,0:T(8,128)(2,1)}, bf16[512,768]{1,0:T(8,128)(2,1)}, f32[8,768]{1,0:T(8,128)}) custom-call(s32[1,4]{1,0:T(1,128)} %add_bitcast_fusion.spot_ref, s32[1,4]{1,0:T(1,128)} %lens_ref.7, bf16[512,768]{1,0:T(8,128)(2,1)} %cot_ref.3, f32[512,768]{1,0:T(8,128)} %get-tuple-element.47.middle_ref, ...), custom_call_target="tpu_custom_call" | custom-call | tf_op jit(solution)/shard_map/middle_back/pallas_call | solution.py:499
  126.2 1.9 collective-permute-done.11.right_ref
  128.1 5.9 %add_large_pair.1 = bf16[64,288,128]{2,1,0:T(8,128)(2,1)} custom-call(bf16[64,288,128]{2,1,0:T(8,128)(2,1)} %bitcast.28, bf16[64,288,128]{2,1,0:T(8,128)(2,1)} %collective-permute-done.11.right_ref), custom_call_target="tpu_custom_call" | custom-call | tf_op jit(solution)/shard_map/add_large_pair/pallas_call | solution.py:946
  134.0 0.0 reduce-scatter.3.cloned.1.call-start
  134.1 23.3 %back.1 = (bf16[64,152,128]{2,1,0:T(8,128)(2,1)}, bf16[64,152,128]{2,1,0:T(8,128)(2,1)}, f32[512,768]{1,0:T(8,128)}) custom-call(s32[1,4]{1,0:T(1,128)} %add_bitcast_fusion.spot_ref, s32[1,4]{1,0:T(1,128)} %lens_ref.7, f32[8,768]{1,0:T(8,128)} %get-tuple-element.53.vec_ref, bf16[512,768]{1,0:T(8,128)(2,1)} %get-tuple-element.57.up, ...), custom_call_target="tpu_custom_call" | custom-call | tf_op jit(solution)/shard_map/back/pallas_call | solution.py:611
  157.4 0.4 collective-permute-start.12
  157.7 4.6 %collective-permute-done.12 = bf16[64,152,128]{2,1,0:T(8,128)(2,1)S(1)} collective-permute-done((bf16[64,152,128]{2,1,0:T(8,128)(2,1)}, bf16[64,152,128]{2,1,0:T(8,128)(2,1)S(1)}, u32[]{:S(2)}, u32[]{:S(2)}) %collective-permute-start.12) | collective-permute-done | bytes 2490400 | tf_op jit(solution)/shard_map/ppermute | solution.py:917
  162.4 3.9 %add_convert_fusion = bf16[64,152,128]{2,1,0:T(8,128)(2,1)} fusion(bf16[64,152,128]{2,1,0:T(8,128)(2,1)S(1)} %collective-permute-done.12, bf16[64,152,128]{2,1,0:T(8,128)(2,1)} %get-tuple-element.63), kind=kLoop, calls=%fused_computation | loop fusion | flops 4980736 | bytes 7471104 | tf_op jit(solution)/shard_map/convert_element_type | solution.py:918
  166.3 0.0 reduce-scatter.5.cloned.1.call-done
  166.4 4.9 %all-to-all-start = ((bf16[16,288,128]{2,1,0:T(8,128)(2,1)}), bf16[16,288,128]{2,1,0:T(8,128)(2,1)S(1)}, u32[]{:S(2)}, u32[]{:S(2)}) async-start(bf16[16,288,128]{2,1,0:T(8,128)(2,1)} %bitcast.31), calls=%async_computation.2 | async-start | bytes 2359296 | tf_op jit(solution)/shard_map/all_to_all | solution.py:968
  171.2 10.2 %layer_output.1 = bf16[512,768]{1,0:T(8,128)(2,1)} custom-call(f32[512,768]{1,0:T(8,128)} %get-tuple-element.47.middle_ref, bf16[6,512,512]{2,1,0:T(8,128)(2,1)} %get-tuple-element.68.act_ref, bf16[128,48,768]{2,1,0:T(8,128)(2,1)} %bitcast.25), custom_call_target="tpu_custom_call" | custom-call | tf_op jit(solution)/shard_map/layer_output/pallas_call | solution.py:826
  181.4 13.7 %reduce-scatter.3.cloned.1.call-done = bf16[2432,128]{1,0:T(8,128)(2,1)} async-done(((bf16[9728,128]{1,0:T(8,128)(2,1)}), bf16[2432,128]{1,0:T(8,128)(2,1)}) %reduce-scatter.3.cloned.1.call-update) | async-done | bytes 622608 | tf_op jit(solution)/shard_map/reduce_scatter | solution.py:958
  195.0 6.5 %all-to-all-start.1 = ((bf16[16,152,128]{2,1,0:T(8,128)(2,1)}), bf16[16,152,128]{2,1,0:T(8,128)(2,1)S(1)}, u32[]{:S(2)}, u32[]{:S(2)}) async-start(bf16[16,152,128]{2,1,0:T(8,128)(2,1)} %bitcast.32), calls=%async_computation.3 | async-start | bytes 1245184 | tf_op jit(solution)/shard_map/all_to_all | solution.py:968
  201.6 4.3 %norm_back.1 = bf16[512,768]{1,0:T(8,128)(2,1)} custom-call(bf16[512,768]{1,0:T(8,128)(2,1)} %x_ref.3, f32[512,768]{1,0:T(8,128)} %get-tuple-element.70.dx_ref, f32[512,768]{1,0:T(8,128)} %get-tuple-element.71.dh_ref, f32[8,768]{1,0:T(8,128)} %get-tuple-element.51.ln_ref), custom_call_target="tpu_custom_call" | custom-call | tf_op jit(solution)/shard_map/norm_back/pallas_call | solution.py:852
  205.9 0.8 unpack.1
  206.7 5.5 %all-to-all-done.1.slabs_ref = bf16[16,152,128]{2,1,0:T(8,128)(2,1)S(1)} async-done(((bf16[16,152,128]{2,1,0:T(8,128)(2,1)}), bf16[16,152,128]{2,1,0:T(8,128)(2,1)S(1)}, u32[]{:S(2)}, u32[]{:S(2)}) %all-to-all-start.1) | async-done | bytes 622624 | tf_op jit(solution)/shard_map/all_to_all | solution.py:968
  212.3 0.7 finish.1
  (18 shorter events, 0.4 us)
Async XLA Ops:
  7.2 78.2 %all-gather.3.cloned.1.call-start = ((), (), s32[]{:S(2)}) async-start(), calls=%async_computation.6 | async-start | bytes 9510912 | tf_op jit(solution)/shard_map/all_gather | solution.py:1021
  8.8 157.5 %reduce-scatter.5.cloned.1.call-start = ((), (), s32[]{:S(2)}) async-start(), calls=%async_computation.5 | async-start | bytes 5898240 | tf_op jit(solution)/shard_map/reduce_scatter | solution.py:958
  8.9 7.5 %collective-permute-start = (bf16[152,128]{1,0:T(8,128)(2,1)}, bf16[152,128]{1,0:T(8,128)(2,1)S(1)}, u32[]{:S(2)}, u32[]{:S(2)}) collective-permute-start(bf16[152,128]{1,0:T(8,128)(2,1)} %get-tuple-element.46), channel_id=1, source_target_pairs={{0,1},{8,24},{1,2},{9,25},{2,3},{10,26},{3,0},{11,27},{16,17},{24,... | collective-permute-start | bytes 116744 | tf_op jit(solution)/shard_map/ppermute | solution.py:984
  11.0 6.2 %collective-permute-start.1 = (bf16[152,128]{1,0:T(8,128)(2,1)}, bf16[152,128]{1,0:T(8,128)(2,1)S(1)}, u32[]{:S(2)}, u32[]{:S(2)}) collective-permute-start(bf16[152,128]{1,0:T(8,128)(2,1)} %get-tuple-element.46), channel_id=1, source_target_pairs={{0,2},{8,40},{1,3},{9,41},{2,0},{10,42},{3,1},{11,43},{16,18},{24,... | collective-permute-start | bytes 116744 | tf_op jit(solution)/shard_map/ppermute | solution.py:984
  14.5 4.2 %collective-permute-start.2 = (bf16[152,128]{1,0:T(8,128)(2,1)}, bf16[152,128]{1,0:T(8,128)(2,1)S(1)}, u32[]{:S(2)}, u32[]{:S(2)}) collective-permute-start(bf16[152,128]{1,0:T(8,128)(2,1)} %get-tuple-element.46), channel_id=1, source_target_pairs={{0,3},{8,56},{1,0},{9,57},{2,1},{10,58},{3,2},{11,59},{16,19},{24,... | collective-permute-start | bytes 116744 | tf_op jit(solution)/shard_map/ppermute | solution.py:984
  18.8 7.0 %collective-permute-start.3 = (bf16[608,128]{1,0:T(8,128)(2,1)S(1)}, bf16[608,128]{1,0:T(8,128)(2,1)S(1)}, u32[]{:S(2)}, u32[]{:S(2)}) collective-permute-start(bf16[608,128]{1,0:T(8,128)(2,1)S(1)} %get-tuple-element.90), channel_id=1, source_target_pairs={{0,64},{8,72},{1,65},{9,73},{2,66},{10,74},{3,67},{11,75},{16,80},... | collective-permute-start | bytes 466952 | tf_op jit(solution)/shard_map/ppermute | solution.py:984
  20.3 7.6 %collective-permute-start.4 = (bf16[608,128]{1,0:T(8,128)(2,1)S(1)}, bf16[608,128]{1,0:T(8,128)(2,1)S(1)}, u32[]{:S(2)}, u32[]{:S(2)}) collective-permute-start(bf16[608,128]{1,0:T(8,128)(2,1)S(1)} %get-tuple-element.90), channel_id=1, source_target_pairs={{0,4},{8,12},{1,5},{9,13},{2,6},{10,14},{3,7},{11,15},{16,20},{24,... | collective-permute-start | bytes 466952 | tf_op jit(solution)/shard_map/ppermute | solution.py:984
  23.0 5.5 %collective-permute-start.5 = (bf16[608,128]{1,0:T(8,128)(2,1)S(1)}, bf16[608,128]{1,0:T(8,128)(2,1)S(1)}, u32[]{:S(2)}, u32[]{:S(2)}) collective-permute-start(bf16[608,128]{1,0:T(8,128)(2,1)S(1)} %get-tuple-element.90), channel_id=1, source_target_pairs={{0,68},{8,76},{1,69},{9,77},{2,70},{10,78},{3,71},{11,79},{16,84},... | collective-permute-start | bytes 466952 | tf_op jit(solution)/shard_map/ppermute | solution.py:984
  28.6 11.9 %collective-permute-start.6 = (bf16[2432,128]{1,0:T(8,128)(2,1)S(1)}, bf16[2432,128]{1,0:T(8,128)(2,1)S(1)}, u32[]{:S(2)}, u32[]{:S(2)}) collective-permute-start(bf16[2432,128]{1,0:T(8,128)(2,1)S(1)} %get-tuple-element.82), channel_id=1, source_target_pairs={{0,16},{8,9},{1,17},{9,10},{2,18},{10,11},{3,19},{11,8},{16,32},{2... | collective-permute-start | bytes 1867784 | tf_op jit(solution)/shard_map/ppermute | solution.py:984
  30.2 10.6 %collective-permute-start.8 = (bf16[2432,128]{1,0:T(8,128)(2,1)S(1)}, bf16[2432,128]{1,0:T(8,128)(2,1)S(1)}, u32[]{:S(2)}, u32[]{:S(2)}) collective-permute-start(bf16[2432,128]{1,0:T(8,128)(2,1)S(1)} %get-tuple-element.82), channel_id=1, source_target_pairs={{0,48},{8,11},{1,49},{9,8},{2,50},{10,9},{3,51},{11,10},{16,0},{24... | collective-permute-start | bytes 1867784 | tf_op jit(solution)/shard_map/ppermute | solution.py:984
  40.5 9.2 %collective-permute-start.7 = (bf16[1216,128]{1,0:T(8,128)(2,1)S(1)}, bf16[1216,128]{1,0:T(8,128)(2,1)S(1)}, u32[]{:S(2)}, u32[]{:S(2)}) collective-permute-start(bf16[1216,128]{1,0:T(8,128)(2,1)S(1)} %slice.8), channel_id=1, source_target_pairs={{0,16},{8,9},{1,17},{9,10},{2,18},{10,11},{3,19},{11,8},{16,32},{2... | collective-permute-start | bytes 933896 | tf_op jit(solution)/shard_map/ppermute | solution.py:984
  40.9 8.9 %collective-permute-start.9 = (bf16[1216,128]{1,0:T(8,128)(2,1)S(1)}, bf16[1216,128]{1,0:T(8,128)(2,1)S(1)}, u32[]{:S(2)}, u32[]{:S(2)}) collective-permute-start(bf16[1216,128]{1,0:T(8,128)(2,1)S(1)} %slice.9), channel_id=1, source_target_pairs={{0,48},{8,11},{1,49},{9,8},{2,50},{10,9},{3,51},{11,10},{16,0},{24... | collective-permute-start | bytes 933896 | tf_op jit(solution)/shard_map/ppermute | solution.py:984
  49.9 5.2 %copy-start = (bf16[9728,128]{1,0:T(8,128)(2,1)}, bf16[9728,128]{1,0:T(8,128)(2,1)S(1)}, u32[]{:S(2)}) copy-start(bf16[9728,128]{1,0:T(8,128)(2,1)S(1)} %constant_dynamic-update-slice_fusion.11) | copy-start | bytes 7471108
  49.9 5.2 %collective-permute-start.10 = (bf16[64,152,128]{2,1,0:T(8,128)(2,1)S(1)}, bf16[64,152,128]{2,1,0:T(8,128)(2,1)}, u32[]{:S(2)}, u32[]{:S(2)}) collective-permute-start(bf16[64,152,128]{2,1,0:T(8,128)(2,1)S(1)} %bitcast.29), channel_id=1, source_target_pairs={{0,8},{8,0},{1,9},{9,1},{2,10},{10,2},{3,11},{11,3},{16,24},{24,16... | collective-permute-start | bytes 7471112 | tf_op jit(solution)/shard_map/ppermute | solution.py:1023
  119.7 8.3 %collective-permute-start.11 = (bf16[64,288,128]{2,1,0:T(8,128)(2,1)}, bf16[64,288,128]{2,1,0:T(8,128)(2,1)}, u32[]{:S(2)}, u32[]{:S(2)}) collective-permute-start(bf16[64,288,128]{2,1,0:T(8,128)(2,1)} %bitcast.38), channel_id=1, source_target_pairs={{0,8},{8,0},{1,9},{9,1},{2,10},{10,2},{3,11},{11,3},{16,24},{24,16... | collective-permute-start | bytes 14155784 | tf_op jit(solution)/shard_map/ppermute | solution.py:945
  134.0 61.0 %reduce-scatter.3.cloned.1.call-start = ((), (), s32[]{:S(2)}) async-start(), calls=%async_computation.4 | async-start | bytes 3112960 | tf_op jit(solution)/shard_map/reduce_scatter | solution.py:958
  157.4 5.0 %collective-permute-start.12 = (bf16[64,152,128]{2,1,0:T(8,128)(2,1)}, bf16[64,152,128]{2,1,0:T(8,128)(2,1)S(1)}, u32[]{:S(2)}, u32[]{:S(2)}) collective-permute-start(bf16[64,152,128]{2,1,0:T(8,128)(2,1)} %get-tuple-element.64), channel_id=1, source_target_pairs={{0,8},{8,0},{1,9},{9,1},{2,10},{10,2},{3,11},{11,3},{16,24},{24,16... | collective-permute-start | bytes 7471112 | tf_op jit(solution)/shard_map/ppermute | solution.py:917
  166.4 28.7 %all-to-all-start = ((bf16[16,288,128]{2,1,0:T(8,128)(2,1)}), bf16[16,288,128]{2,1,0:T(8,128)(2,1)S(1)}, u32[]{:S(2)}, u32[]{:S(2)}) async-start(bf16[16,288,128]{2,1,0:T(8,128)(2,1)} %bitcast.31), calls=%async_computation.2 | async-start | bytes 2359296 | tf_op jit(solution)/shard_map/all_to_all | solution.py:968
  195.0 17.2 %all-to-all-start.1 = ((bf16[16,152,128]{2,1,0:T(8,128)(2,1)}), bf16[16,152,128]{2,1,0:T(8,128)(2,1)S(1)}, u32[]{:S(2)}, u32[]{:S(2)}) async-start(bf16[16,152,128]{2,1,0:T(8,128)(2,1)} %bitcast.32), calls=%async_computation.3 | async-start | bytes 1245184 | tf_op jit(solution)/shard_map/all_to_all | solution.py:968
Sparse Core Ops, SparseCore 0:
  11.4 73.9 all-gather.2
  134.2 30.0 reduce-scatter.4
  166.7 28.3 reduce-scatter.2
